TPU v7x, 32 devices: a whole 2x2x4 slice. The times are simulated.
32 devices in a mesh: tok: 8 (over z, y), out: 4 (over x, core).
Axes of the slice: x: 2, y: 2, z: 4, core: 2. Of those that a mesh axis runs over, the one named last changes fastest.
Arguments:
- acts: bfloat16 [3, 512, 8192], P(None, 'tok'), may hold values from -6 to 6
- grads: bfloat16 [3, 512, 4096], P(None, 'tok', 'out'), may hold values from -6 to 6
- act_basis: float32 [1024, 8, 8], P('tok'), may hold values from -2 to 2
- grad_basis: float32 [512, 8, 8], P('out'), may hold values from -2 to 2
Outputs:
- eigen_corr: float32 [4096, 8192], P('out', 'tok')
All inputs are finite; a program needn't handle non-finite values.
Results may differ from a plain program's by a relative error of at most 0.014.
Values may be sent and summed in bfloat16 or wider, within the bound.
No kernel may reach another device: no remote copies, remote signals or barrier semaphores. Data moves between devices by JAX's collectives and lax.ppermute only.
A program may use at most 128 MiB of HBM per device.

v0:
```python
import jax
import jax.numpy as jnp
from jax import lax
from jax.sharding import PartitionSpec as P


def rotate_local(values, basis):
    seqs, rows, width = values.shape
    span = min(128, width)
    count = span // 8
    groups = width // span
    blocks = basis.reshape(groups, count, 8, 8)
    identity = jnp.eye(count, dtype=jnp.float32)
    diagonal = (blocks[:, :, :, None, :] * identity[None, :, None, :, None]).reshape(
        groups, span, span
    )
    high_part = diagonal.astype(jnp.bfloat16)
    low_part = (diagonal - high_part.astype(jnp.float32)).astype(jnp.bfloat16)
    spread = values.reshape(seqs * rows, groups, span)
    turned = jnp.einsum("rgp,gpq->rgq", spread, high_part, preferred_element_type=jnp.float32)
    turned = turned + jnp.einsum(
        "rgp,gpq->rgq", spread, low_part, preferred_element_type=jnp.float32
    )
    return turned.reshape(seqs, rows, width).astype(jnp.bfloat16)


def shards(acts, grads, act_basis, grad_basis):
    turned_acts = rotate_local(
        lax.all_to_all(acts, "tok", split_axis=2, concat_axis=1, tiled=True), act_basis
    )
    turned_grads = rotate_local(grads, grad_basis)
    seqs, length, columns = turned_acts.shape
    scale = length ** (-0.5)
    products = jnp.einsum(
        "sto,sti->soi",
        lax.all_gather(turned_grads, "tok", axis=1, tiled=True),
        turned_acts,
        preferred_element_type=jnp.float32,
    )
    scaled = products * scale
    return jnp.sum(scaled * scaled, axis=0)


def solution(mesh):
    placed = (
        P(None, "tok", None),
        P(None, "tok", "out"),
        P("tok", None, None),
        P("out", None, None),
    )
    return jax.shard_map(
        shards, mesh=mesh, in_specs=placed, out_specs=P("out", "tok"), check_vma=False
    )
```

profile of v0, /device:TPU:0, one launch (start us, length us, event | category | flops | bytes accessed | tf_op | source)
XLA Modules:
  0.0 176.4 jit_solution(1605978482055774496)
XLA Ops:
  6.5 11.3 %copy.28 = bf16[3,64,8192]{1,0,2:T(4,128)(2,1)} copy(bf16[3,64,8192]{2,1,0:T(8,128)(2,1)} %param.4) | data formatting | bytes 6291456 | tf_op args[0]
  17.8 9.7 %reshape.29 = bf16[8,2,98304]{2,1,0:T(2,128)(2,1)} reshape(bf16[8192,3,64]{2,1,0:T(4,128)(2,1)} %bitcast.26) | data formatting | bytes 6291456
  27.6 0.0 copy-start.1
  27.6 7.4 %all-to-all-start = ((bf16[8,2,98304]{2,1,0:T(2,128)(2,1)}), bf16[8,2,98304]{2,1,0:T(2,128)(2,1)S(1)}, u32[]{:S(2)}, u32[]{:S(2)}) async-start(bf16[8,2,98304]{2,1,0:T(2,128)(2,1)} %reshape.29), calls=%async_computation | async-start | bytes 6291456 | tf_op jit(solution)/shard_map/all_to_all | solution.py:29
  35.0 0.0 all-gather.2.cloned.1.call-start
  35.0 1.1 mul.56
  36.1 1.6 mul.57
  37.8 0.0 copy-done.1
  37.8 1.0 copy.37
  38.8 5.0 %mul.54 = f32[8,16,8,16,8]{4,3,2,1,0:T(8,128)} broadcast(f32[8,16,8,8]{3,2,1,0:T(8,128)} %bitcast.32), dimensions={0,1,2,4} | broadcast | bytes 557056 | tf_op jit(solution)/shard_map/mul | solution.py:14
  43.8 7.1 %mul.55 = f32[8,128,128]{2,1,0:T(8,128)} reshape(f32[8,16,8,16,8]{4,3,2,1,0:T(8,128)} %mul.54) | data formatting | bytes 1048576 | tf_op jit(solution)/shard_map/mul | solution.py:14
  50.9 1.1 copy.39
  51.9 0.0 copy-start.2
  51.9 1.3 fusion.6
  53.2 1.3 fusion.5
  54.6 1.0 copy.26
  55.6 1.9 %convert_element_type.52 = bf16[3,64,1024]{2,1,0:T(8,128)(2,1)} reshape(bf16[192,8,128]{2,1,0:T(8,128)(2,1)} %copy.26) | data formatting | bytes 786432 | tf_op jit(solution)/shard_map/convert_element_type | solution.py:24
  57.5 0.0 all-gather.2.cloned.1.call-update
  57.5 0.0 copy-done.2
  57.5 1.0 copy.38
  58.5 5.0 %mul.61 = f32[8,16,8,16,8]{4,3,2,1,0:T(8,128)} broadcast(f32[8,16,8,8]{3,2,1,0:T(8,128)} %bitcast.33), dimensions={0,1,2,4} | broadcast | bytes 557056 | tf_op jit(solution)/shard_map/mul | solution.py:14
  63.4 7.2 %mul.62 = f32[8,128,128]{2,1,0:T(8,128)} reshape(f32[8,16,8,16,8]{4,3,2,1,0:T(8,128)} %mul.61) | data formatting | bytes 1048576 | tf_op jit(solution)/shard_map/mul | solution.py:14
  70.6 59.9 %all-to-all-done = bf16[8,2,98304]{2,1,0:T(2,128)(2,1)S(1)} async-done(((bf16[8,2,98304]{2,1,0:T(2,128)(2,1)}), bf16[8,2,98304]{2,1,0:T(2,128)(2,1)S(1)}, u32[]{:S(2)}, u32[]{:S(2)}) %all-to-all-start) | async-done | bytes 3145760 | tf_op jit(solution)/shard_map/all_to_all | solution.py:29
  130.5 7.0 %reshape.30 = bf16[8192,3,64]{2,1,0:T(4,128)(2,1)} reshape(bf16[8,2,98304]{2,1,0:T(2,128)(2,1)S(1)} %all-to-all-done) | data formatting | bytes 6291456
  137.5 10.6 %copy.29 = bf16[3,64,8,1024]{3,1,2,0:T(8,128)(2,1)S(1)} copy(bf16[3,64,8,1024]{1,0,3,2:T(4,128)(2,1)} %bitcast.25) | data formatting | bytes 6291456 | tf_op jit(solution)/shard_map/all_to_all | solution.py:29
  148.2 0.0 copy-start
  148.2 0.8 copy.40
  149.0 0.2 copy-done
  149.2 1.1 fusion.2
  150.3 3.0 %fusion = bf16[1536,8,128]{0,2,1:T(8,128)(2,1)} fusion(f32[8,128,1536]{2,1,0:T(8,128)S(1)} %fusion.2, bf16[1536,8,128]{2,1,0:T(8,128)(2,1)S(1)} %bitcast.28, f32[8,128,128]{2,1,0:T(8,128)S(1)} %copy-done, f32[128,128]{1,0:T(8,128)S(1)} %mul.57), kind=kOutput, calls=%fused_computation.2 | convolution fusion | flops 406454272 | bytes 13172736 | tf_op jit(solution)/shard_map/rgp,gpq->rgq/dot_general | solution.py:21
  153.3 3.8 %copy.34 = bf16[1536,8,128]{2,1,0:T(8,128)(2,1)S(1)} copy(bf16[1536,8,128]{0,2,1:T(8,128)(2,1)} %fusion) | data formatting | bytes 6291456 | tf_op jit(solution)/shard_map/convert_element_type | solution.py:24
  157.2 3.3 %convert_element_type.58 = bf16[3,512,1024]{2,1,0:T(8,128)(2,1)} reshape(bf16[1536,8,128]{2,1,0:T(8,128)(2,1)S(1)} %copy.34) | data formatting | bytes 6291456 | tf_op jit(solution)/shard_map/convert_element_type | solution.py:24
  160.5 0.0 all-gather.2.cloned.1.call-done
  160.5 9.1 %multiply_reduce_fusion = f32[1024,1024]{1,0:T(8,128)} fusion(bf16[3,512,1024]{2,1,0:T(8,128)(2,1)} %all-gather.2.cloned.1.call-done, bf16[3,512,1024]{2,1,0:T(8,128)(2,1)} %convert_element_type.58), kind=kOutput, calls=%fused_computation | convolution fusion | flops 3229614080 | bytes 10485760 | tf_op jit(solution)/shard_map/sto,sti->soi/dot_general | solution.py:34
  (1 shorter events, 0.0 us)
Async XLA Ops:
  27.6 10.2 %copy-start.1 = (f32[128,8,8]{0,2,1:T(8,128)S(1)}, f32[128,8,8]{0,2,1:T(8,128)}, u32[]{:S(2)}) copy-start(f32[128,8,8]{0,2,1:T(8,128)} %param.7) | copy-start | bytes 98308
  27.6 102.9 %all-to-all-start = ((bf16[8,2,98304]{2,1,0:T(2,128)(2,1)}), bf16[8,2,98304]{2,1,0:T(2,128)(2,1)S(1)}, u32[]{:S(2)}, u32[]{:S(2)}) async-start(bf16[8,2,98304]{2,1,0:T(2,128)(2,1)} %reshape.29), calls=%async_computation | async-start | bytes 6291456 | tf_op jit(solution)/shard_map/all_to_all | solution.py:29
  35.0 125.5 %all-gather.2.cloned.1.call-start = ((), (), s32[]{:S(2)}) async-start(), calls=%async_computation.1 | async-start | bytes 3538944 | tf_op jit(solution)/shard_map/all_gather | solution.py:36
  51.9 5.6 %copy-start.2 = (f32[128,8,8]{0,2,1:T(8,128)S(1)}, f32[128,8,8]{0,2,1:T(8,128)}, u32[]{:S(2)}) copy-start(f32[128,8,8]{0,2,1:T(8,128)} %param.6) | copy-start | bytes 98308
  148.2 1.0 copy-start
Sparse Core Ops, SparseCore 0:
  57.6 86.5 all-gather.1
where the time goes:
time: 178 us; the launch traced here: 176 us
  local copies, waits for them, and re-layouts  79.8 us (45%)
  waiting for transfers between devices  59.9 us (34%)
  matrix products  15.8 us (9%)
  between operations  13.5 us (8%)
  starting transfers between devices  7.45 us (4%)
    all_to_all x1, waiting for transfers between devices, shards(): lax.all_to_all(acts, 'tok', split_axis=2, concat_axis=1, tiled=True)  59.9 us
    unnamed x11, local copies, waits for them, and re-layouts  30.2 us
    mul x8, local copies, waits for them, and re-layouts, rotate_local(): blocks[:, :, :, None, :] * identity[None, :, None, :, None]  28.9 us
    all_to_all x1, local copies, waits for them, and re-layouts, shards(): lax.all_to_all(acts, 'tok', split_axis=2, concat_axis=1, tiled=True)  10.6 us
    convert_element_type x4, local copies, waits for them, and re-layouts, rotate_local(): return turned.reshape(seqs, rows, width).astype(jnp.bfloat16)  10.1 us
    dot_general x1, matrix products, shards(): jnp.einsum('sto,sti->soi', lax.all_gather(turned_grads, 'tok', axis=1, ti...  9.11 us
    all_to_all x1, starting transfers between devices, shards(): lax.all_to_all(acts, 'tok', split_axis=2, concat_axis=1, tiled=True)  7.41 us
    dot_general x2, matrix products, rotate_local(): jnp.einsum('rgp,gpq->rgq', spread, low_part, preferred_element_type=jnp.f...  4.35 us
  transfers between devices with their start and end apart: 2, of which 1 were waited for; matrix products, arithmetic and copies ran while one was open for 37% of the time, Pallas kernels for 0%

commit v1 on v0

v1 whole, which is shorter than its diff:
```python
import functools

import jax
import jax.numpy as jnp
from jax import lax
from jax.experimental import pallas as pl
from jax.experimental.pallas import tpu as pltpu
from jax.sharding import PartitionSpec as P

BF, F32 = jnp.bfloat16, jnp.float32


def dot(a, b, contract):
    return lax.dot_general(a, b, (contract, ((), ())), preferred_element_type=F32)


def split(value):
    high = value.astype(BF)
    return high, (value - high.astype(F32)).astype(BF)


def spread_kernel(transposed, basis_ref, high_ref, low_ref):
    groups, span, _ = high_ref.shape
    blocks = basis_ref.shape[1]
    parts = split(basis_ref[...])
    iota = lambda shape, dim: lax.broadcasted_iota(jnp.int32, shape, dim)
    pq_row, pq_col = (
        (iota((span, 64), 1) % 8, iota((64, span), 0) // 8)
        if transposed
        else (iota((span, 64), 1) // 8, iota((64, span), 0) % 8)
    )
    keep = pq_row == iota((span, 64), 0) % 8
    repeat = (pq_col == iota((64, span), 1) % 8).astype(BF)
    diagonal = iota((span, span), 0) // 8 == iota((span, span), 1) // 8
    for g in range(groups):
        pick = iota((span, blocks), 0) // 8 + g * (span // 8) == iota((span, blocks), 1)
        pick = pick.astype(BF)
        for part, out_ref in zip(parts, (high_ref, low_ref)):
            rows = dot(pick, part, ((1,), (1,)))
            rows = jnp.where(keep, rows, 0.0).astype(BF)
            full = dot(rows, repeat, ((1,), (0,)))
            out_ref[g] = jnp.where(diagonal, full, 0.0).astype(BF)


def spread(basis, transposed):
    blocks = basis.shape[0]
    span = min(256, blocks * 8)
    groups = blocks * 8 // span
    flat = jnp.transpose(basis, (1, 2, 0)).reshape(64, blocks)
    shape = jax.ShapeDtypeStruct((groups, span, span), BF)
    return pl.pallas_call(
        functools.partial(spread_kernel, transposed), out_shape=(shape, shape)
    )(flat)


def main_kernel(n, m, scale, place_ref, *refs):
    n_acts = n // 2 * m
    acts = refs[:n_acts]
    grads = refs[n_acts : n_acts + n]
    wa_high, wa_low, wg_high, wg_low, out_ref, a_raw, g_raw, a_rot, sems = refs[n_acts + n :]
    seqs, length, width = a_raw.shape
    quarter = length // (n * m)
    rows = length // n
    span = wa_high.shape[1]
    tile = out_ref.shape[0]

    def copies():
        index = 0
        for k in range(n // 2):
            for j in range(m):
                for y in range(2):
                    start = (2 * k + y) * rows + (place_ref[0] ^ j) * quarter
                    yield pltpu.make_async_copy(
                        acts[k * m + j].at[y],
                        a_raw.at[:, pl.ds(pl.multiple_of(start, quarter), quarter), :],
                        sems.at[index],
                    )
                    index += 1
        for k in range(n):
            yield pltpu.make_async_copy(
                grads[k], g_raw.at[:, pl.ds(k * rows, rows), :], sems.at[index]
            )
            index += 1

    @pl.when(pl.program_id(0) == 0)
    def _():
        for copy in copies():
            copy.start()
        for copy in copies():
            copy.wait()
        for s in range(seqs):
            for g in range(width // span):
                columns = pl.ds(g * span, span)
                block = a_raw[s, :, columns]
                turned = dot(block, wa_high[g], ((1,), (0,))) + dot(block, wa_low[g], ((1,), (0,)))
                a_rot[s, :, columns] = turned.astype(BF)

    step = pl.program_id(0)
    columns = pl.ds(pl.multiple_of(step * tile, tile), tile)
    total = None
    for s in range(seqs):
        block = g_raw[s, :, columns]
        turned = dot(wg_high[step], block, ((1,), (1,))) + dot(wg_low[step], block, ((1,), (1,)))
        corr = dot(turned.astype(BF), a_rot[s], ((1,), (0,))) * scale
        total = corr * corr if total is None else total + corr * corr
    out_ref[...] = total


def multiply(n, m, place, acts, grads, wa, wg):
    rows, outs = grads[0].shape[1:]
    seqs, width = acts[0].shape[1], acts[0].shape[-1]
    length = rows * n
    tile = wg[0].shape[1]
    anywhere = pl.BlockSpec(memory_space=pl.ANY)
    vmem = pl.BlockSpec(memory_space=pltpu.VMEM)
    return pl.pallas_call(
        functools.partial(main_kernel, n, m, length ** (-0.5)),
        grid=(outs // tile,),
        in_specs=[pl.BlockSpec(memory_space=pltpu.SMEM)]
        + [anywhere] * (len(acts) + len(grads))
        + [vmem] * 4,
        out_specs=pl.BlockSpec((tile, width), lambda i: (i, 0)),
        out_shape=jax.ShapeDtypeStruct((outs, width), F32),
        scratch_shapes=[
            pltpu.VMEM((seqs, length, width), BF),
            pltpu.VMEM((seqs, length, outs), BF),
            pltpu.VMEM((seqs, length, width), BF),
            pltpu.SemaphoreType.DMA((2 * len(acts) + len(grads),)),
        ],
        compiler_params=pltpu.CompilerParams(vmem_limit_bytes=48 * 2**20),
    )(place, *acts, *grads, *wa, *wg)


def shards(acts, grads, act_basis, grad_basis):
    n, m = lax.axis_size("tok"), lax.axis_size("out")
    half = n // 2
    t, q = lax.axis_index("tok"), lax.axis_index("out")
    z, y = t // 2, t % 2
    seqs, rows, total = acts.shape
    width, quarter = total // n, rows // m

    def over_y(value):
        return lax.ppermute(value, "tok", [(i, i ^ 1) for i in range(n)])

    def over_z(value, shift):
        return lax.ppermute(
            value, "tok", [(i, (i // 2 + shift) % half * 2 + i % 2) for i in range(n)]
        )

    def over_out(value, bit):
        return lax.ppermute(value, "out", [(i, i ^ bit) for i in range(m)])

    wa = spread(act_basis, False)
    wg = spread(grad_basis, True)

    part = lax.dynamic_slice_in_dim(acts, q * quarter, quarter, 1)
    part = part.reshape(seqs, quarter, half, 2, width).transpose(3, 2, 0, 1, 4)
    mine = lax.dynamic_index_in_dim(part, y, 0)
    other = over_y(lax.dynamic_index_in_dim(part, 1 - y, 0))
    both = jnp.concatenate([mine, other], 0)

    ring = {0: grads}
    for k in range(1, half // 2 + 1):
        ring[k] = over_z(ring[k - 1], 1)
    for k in range(1, (half - 1) // 2 + 1):
        ring[half - k] = over_z(ring[(half - k + 1) % half], -1)
    all_grads = []
    for k in range(half):
        all_grads += [ring[k], over_y(ring[k])]

    all_acts = []
    for k in range(half):
        sent = lax.dynamic_index_in_dim(both, (z + k) % half, 1, keepdims=False)
        have = [sent if k == 0 else over_z(sent, k)]
        bit = m // 2
        held = {0: have[0]}
        while bit:
            held.update({j | bit: over_out(value, bit) for j, value in list(held.items())})
            bit //= 2
        all_acts += [held[j] for j in range(m)]

    place = q.astype(jnp.int32).reshape(1)
    return multiply(n, m, place, all_acts, all_grads, wa, wg)


def solution(mesh):
    placed = (
        P(None, "tok", None),
        P(None, "tok", "out"),
        P("tok", None, None),
        P("out", None, None),
    )
    return jax.shard_map(
        shards, mesh=mesh, in_specs=placed, out_specs=P("out", "tok"), check_vma=False
    )
```

time: 178 us -> 96.9 us (0.54)
  local copies, waits for them, and re-layouts: 79.8 us -> 22.2 us
  waiting for transfers between devices: 59.9 us -> 25.4 us
  Pallas kernels: 0 us -> 19.8 us
  starting transfers between devices: 7.45 us -> 23.8 us
  matrix products: 15.8 us -> 0 us
  between operations: 13.5 us -> 0.32 us
  other arithmetic: 0.01 us -> 4.79 us
    all_to_all x1 -> x0, waiting for transfers between devices: 59.9 us -> none  [shards(): lax.all_to_all(acts, 'tok', split_axis=2, concat_axis=1, tiled=True)]
    mul x8 -> x0, local copies, waits for them, and re-layouts: 28.9 us -> none  [rotate_local(): blocks[:, :, :, None, :] * identity[None, :, None, :, None]]
    ppermute x0 -> x23, waiting for transfers between devices: none -> 25.4 us  [the longest x6 14.1 us: over_z(): lax.ppermute(value, 'tok', [(i, (i // 2 + shift) % half * 2 + i % 2) for...]
    ppermute x0 -> x23, starting transfers between devices: none -> 23.8 us  [the longest x6 11.9 us: over_z(): lax.ppermute(value, 'tok', [(i, (i // 2 + shift) % half * 2 + i % 2) for...]
    unnamed x11 -> x26, local copies, waits for them, and re-layouts: 30.2 us -> 10.1 us
    pallas_call x0 -> x3, Pallas kernels: none -> 19.8 us  [the longest x1 14.4 us: multiply(): pl.pallas_call(functools.partial(main_kernel, n, m, length ** (-0.5)), gr...]
    dot_general x5 -> x0, matrix products: 15.8 us -> none  [the longest x1 9.11 us: shards(): jnp.einsum('sto,sti->soi', lax.all_gather(turned_grads, 'tok', axis=1, ti...]
    all_to_all x1 -> x0, local copies, waits for them, and re-layouts: 10.6 us -> none  [shards(): lax.all_to_all(acts, 'tok', split_axis=2, concat_axis=1, tiled=True)]
  transfers between devices with their start and end apart: 2 -> 23, of which waited for: 1 -> 7; matrix products, arithmetic and copies ran while one was open for 37% -> 9% of each run, Pallas kernels for 0% -> 6%
where the time goes in v1:
time: 96.9 us; the launch traced here: 96.2 us
  waiting for transfers between devices  25.4 us (26%)
  starting transfers between devices  23.8 us (25%)
  local copies, waits for them, and re-layouts  22.2 us (23%)
  Pallas kernels  19.8 us (20%)
  other arithmetic  4.79 us (5%)
    pallas_call x1, Pallas kernels, multiply(): pl.pallas_call(functools.partial(main_kernel, n, m, length ** (-0.5)), gr...  14.4 us
    ppermute x6, waiting for transfers between devices, over_z(): lax.ppermute(value, 'tok', [(i, (i // 2 + shift) % half * 2 + i % 2) for...  14.1 us
    ppermute x6, starting transfers between devices, over_z(): lax.ppermute(value, 'tok', [(i, (i // 2 + shift) % half * 2 + i % 2) for...  11.9 us
    unnamed x26, local copies, waits for them, and re-layouts  10.1 us
    ppermute x5, starting transfers between devices, over_y(): return lax.ppermute(value, 'tok', [(i, i ^ 1) for i in range(n)])  7.25 us
    ppermute x5, waiting for transfers between devices, over_y(): return lax.ppermute(value, 'tok', [(i, i ^ 1) for i in range(n)])  5.95 us
    pallas_call x2, Pallas kernels, spread(): pl.pallas_call(functools.partial(spread_kernel, transposed), out_shape=(s...  5.42 us
    ppermute x12, waiting for transfers between devices, over_out(): return lax.ppermute(value, 'out', [(i, i ^ bit) for i in range(m)])  5.29 us
  transfers between devices with their start and end apart: 23, of which 7 were waited for; matrix products, arithmetic and copies ran while one was open for 9% of the time, Pallas kernels for 6%

profile of v1, /device:TPU:0, one launch (start us, length us, event | category | flops | bytes accessed | tf_op | source)
XLA Modules:
  0.0 96.2 jit_solution(1419552329507601354)
XLA Ops:
  0.0 1.9 %copy-done = bf16[3,64,8192]{2,1,0:T(8,128)(2,1)S(1)} copy-done((bf16[3,64,8192]{2,1,0:T(8,128)(2,1)S(1)}, bf16[3,64,8192]{2,1,0:T(8,128)(2,1)}, u32[]{:S(2)}) %copy-start) | copy-done | bytes 3145752
  1.9 0.9 constant_dynamic-slice_fusion
  2.8 3.2 %reshape.13 = bf16[3,16,4,2,1024]{4,3,2,1,0:T(2,128)(2,1)} reshape(bf16[3,16,8192]{2,1,0:T(8,128)(2,1)} %constant_dynamic-slice_fusion) | data formatting | bytes 1572864 | tf_op jit(solution)/shard_map/reshape | solution.py:157
  6.1 4.0 %dynamic-slice_bitcast_fusion.1 = (bf16[1,4,3,16,1024]{4,0,1,3,2:T(2,128)(2,1)}, bf16[1,4,3,16,1024]{4,0,1,3,2:T(2,128)(2,1)S(1)}) fusion(bf16[3,16,4,2,1024]{4,3,2,1,0:T(2,128)(2,1)} %reshape.13, s32[]{:T(128)S(6)} %select_n.52, s32[]{:T(128)S(6)} %select_n.53), kind=kLoop, calls=%fused_computation.1 | loop fusion | bytes 1572872 | tf_op jit(solution)/shard_map/jit(dynamic_index_in_dim)/dynamic_slice | solution.py:158
  10.0 0.4 copy.9
  10.5 3.0 %collective-permute-start = (bf16[1,4,3,16,1024]{4,3,2,1,0:T(8,128)(2,1)S(1)}, bf16[1,4,3,16,1024]{4,3,2,1,0:T(8,128)(2,1)}, u32[]{:S(2)}, u32[]{:S(2)}) collective-permute-start(bf16[1,4,3,16,1024]{4,3,2,1,0:T(8,128)(2,1)S(1)} %copy.9), channel_id=1, source_target_pairs={{0,4},{4,0},{8,12},{12,8},{16,20},{20,16},{24,28},{28,24},{1,5},{5... | collective-permute-start | bytes 1179656 | tf_op jit(solution)/shard_map/ppermute | solution.py:143
  13.5 1.6 %collective-permute-start.17 = (bf16[3,64,1024]{2,1,0:T(8,128)(2,1)}, bf16[3,64,1024]{2,1,0:T(8,128)(2,1)}, u32[]{:S(2)}, u32[]{:S(2)}) collective-permute-start(bf16[3,64,1024]{2,1,0:T(8,128)(2,1)} %refs_16_.1), channel_id=1, source_target_pairs={{0,8},{4,12},{8,16},{12,20},{16,24},{20,28},{24,0},{28,4},{1,9},{5... | collective-permute-start | bytes 1179656 | tf_op jit(solution)/shard_map/ppermute | solution.py:146
  15.1 0.5 collective-permute-start.16
  15.6 2.0 %collective-permute-start.21 = (bf16[3,64,1024]{2,1,0:T(8,128)(2,1)}, bf16[3,64,1024]{2,1,0:T(8,128)(2,1)}, u32[]{:S(2)}, u32[]{:S(2)}) collective-permute-start(bf16[3,64,1024]{2,1,0:T(8,128)(2,1)} %refs_16_.1), channel_id=1, source_target_pairs={{0,24},{4,28},{8,0},{12,4},{16,8},{20,12},{24,16},{28,20},{1,25},{... | collective-permute-start | bytes 1179656 | tf_op jit(solution)/shard_map/ppermute | solution.py:146
  17.6 5.9 %collective-permute-done = bf16[1,4,3,16,1024]{4,3,2,1,0:T(8,128)(2,1)} collective-permute-done((bf16[1,4,3,16,1024]{4,3,2,1,0:T(8,128)(2,1)S(1)}, bf16[1,4,3,16,1024]{4,3,2,1,0:T(8,128)(2,1)}, u32[]{:S(2)}, u32[]{:S(2)}) %collective-permute-start) | collective-permute-done | bytes 393248 | tf_op jit(solution)/shard_map/ppermute | solution.py:143
  23.5 1.8 %copy.10 = bf16[1,4,3,16,1024]{4,0,1,3,2:T(2,128)(2,1)S(1)} copy(bf16[1,4,3,16,1024]{4,3,2,1,0:T(8,128)(2,1)} %collective-permute-done) | data formatting | bytes 786432 | tf_op jit(solution)/shard_map/ppermute | solution.py:143
  25.4 3.3 %dynamic-slice_maximum_fusion = (bf16[2,1,3,16,1024]{4,0,1,3,2:T(2,128)(2,1)}, bf16[2,1,3,16,1024]{4,0,1,3,2:T(2,128)(2,1)S(1)}, bf16[2,1,3,16,1024]{4,0,1,3,2:T(2,128)(2,1)S(1)}) fusion(s32[]{:T(128)S(6)} %select_n.62, bf16[1,4,3,16,1024]{4,0,1,3,2:T(2,128)(2,1)S(1)} %copy.10, bf16[1,4,3,16,1024]{4,0,1,3,2:T(2,128)(2,1)} %get-tuple-element.16, ...), kind=kLoop, calls=%fused_computation.2 | loop fusion | flops 1179648 | bytes 1376268 | tf_op jit(solution)/shard_map/concatenate | solution.py:160
  28.7 0.7 copy.21
  29.4 2.1 %collective-permute-start.4 = (bf16[2,3,16,1024]{3,2,1,0:T(8,128)(2,1)}, bf16[2,3,16,1024]{3,2,1,0:T(8,128)(2,1)S(1)}, u32[]{:S(2)}, u32[]{:S(2)}) collective-permute-start(bf16[2,3,16,1024]{3,2,1,0:T(8,128)(2,1)} %bitcast.21), channel_id=1, source_target_pairs={{0,8},{4,12},{8,16},{12,20},{16,24},{20,28},{24,0},{28,4},{1,9},{5... | collective-permute-start | bytes 589832 | tf_op jit(solution)/shard_map/ppermute | solution.py:146
  31.6 1.5 %collective-permute-start.2 = (bf16[2,3,16,1024]{3,2,1,0:T(8,128)(2,1)S(1)}, bf16[2,3,16,1024]{3,2,1,0:T(8,128)(2,1)}, u32[]{:S(2)}, u32[]{:S(2)}) collective-permute-start(bf16[2,3,16,1024]{3,2,1,0:T(8,128)(2,1)S(1)} %bitcast.23), channel_id=1, source_target_pairs={{0,2},{1,3},{2,0},{3,1},{4,6},{5,7},{6,4},{7,5},{8,10},{9,11},{10,... | collective-permute-start | bytes 589832 | tf_op jit(solution)/shard_map/ppermute | solution.py:151
  33.1 1.0 %copy.19 = bf16[2,1,3,16,1024]{4,3,2,0,1:T(8,128)(2,1)S(1)} copy(bf16[2,1,3,16,1024]{4,0,1,3,2:T(2,128)(2,1)} %get-tuple-element.13) | data formatting | bytes 393216 | tf_op jit(solution)/shard_map/jit(dynamic_index_in_dim)/dynamic_slice | solution.py:173
  34.1 1.5 %dynamic-slice_maximum_fusion.1 = bf16[2,1,3,16,1024]{4,0,1,3,2:T(2,128)(2,1)S(1)} fusion(s32[]{:T(128)S(6)} %select_n.60, bf16[1,4,3,16,1024]{4,0,1,3,2:T(2,128)(2,1)} %copy-done.11, bf16[1,4,3,16,1024]{4,0,1,3,2:T(2,128)(2,1)} %get-tuple-element.16), kind=kLoop, calls=%fused_computation.3 | loop fusion | flops 393216 | bytes 983044 | tf_op jit(solution)/shard_map/concatenate | solution.py:160
  35.6 2.7 %collective-permute-start.8 = (bf16[2,3,16,1024]{3,2,1,0:T(8,128)(2,1)S(1)}, bf16[2,3,16,1024]{3,2,1,0:T(8,128)(2,1)S(1)}, u32[]{:S(2)}, u32[]{:S(2)}) collective-permute-start(bf16[2,3,16,1024]{3,2,1,0:T(8,128)(2,1)S(1)} %bitcast.27), channel_id=1, source_target_pairs={{0,16},{4,20},{8,24},{12,28},{16,0},{20,4},{24,8},{28,12},{1,17},{... | collective-permute-start | bytes 589832 | tf_op jit(solution)/shard_map/ppermute | solution.py:146
  38.3 0.2 collective-permute-start.19
  38.5 0.3 collective-permute-done.4.refs_4_
  38.8 1.2 %collective-permute-start.18 = (bf16[3,64,1024]{2,1,0:T(8,128)(2,1)}, bf16[3,64,1024]{2,1,0:T(8,128)(2,1)S(1)}, u32[]{:S(2)}, u32[]{:S(2)}) collective-permute-start(bf16[3,64,1024]{2,1,0:T(8,128)(2,1)} %collective-permute-done.17.refs_18_), channel_id=1, source_target_pairs={{0,4},{4,0},{8,12},{12,8},{16,20},{20,16},{24,28},{28,24},{1,5},{5... | collective-permute-start | bytes 1179656 | tf_op jit(solution)/shard_map/ppermute | solution.py:143
  40.0 0.8 collective-permute-start.22
  40.8 3.3 %collective-permute-start.12 = (bf16[2,3,16,1024]{3,2,1,0:T(8,128)(2,1)S(1)}, bf16[2,3,16,1024]{3,2,1,0:T(8,128)(2,1)}, u32[]{:S(2)}, u32[]{:S(2)}) collective-permute-start(bf16[2,3,16,1024]{3,2,1,0:T(8,128)(2,1)S(1)} %bitcast.26), channel_id=1, source_target_pairs={{0,24},{4,28},{8,0},{12,4},{16,8},{20,12},{24,16},{28,20},{1,25},{... | collective-permute-start | bytes 589832 | tf_op jit(solution)/shard_map/ppermute | solution.py:146
  44.1 12.8 %collective-permute-done.8.refs_8_ = bf16[2,3,16,1024]{3,2,1,0:T(8,128)(2,1)S(1)} collective-permute-done((bf16[2,3,16,1024]{3,2,1,0:T(8,128)(2,1)S(1)}, bf16[2,3,16,1024]{3,2,1,0:T(8,128)(2,1)S(1)}, u32[]{:S(2)}, u32[]{:S(2)}) %collective-permute-start.8) | collective-permute-done | bytes 196640 | tf_op jit(solution)/shard_map/ppermute | solution.py:146
  56.9 0.5 collective-permute-start.6
  57.5 1.0 %collective-permute-done.12.refs_12_ = bf16[2,3,16,1024]{3,2,1,0:T(8,128)(2,1)} collective-permute-done((bf16[2,3,16,1024]{3,2,1,0:T(8,128)(2,1)S(1)}, bf16[2,3,16,1024]{3,2,1,0:T(8,128)(2,1)}, u32[]{:S(2)}, u32[]{:S(2)}) %collective-permute-start.12) | collective-permute-done | bytes 196640 | tf_op jit(solution)/shard_map/ppermute | solution.py:146
  58.5 0.5 collective-permute-start.3
  59.0 0.7 copy-done.1
  59.7 1.3 %collective-permute-start.10 = (bf16[2,3,16,1024]{3,2,1,0:T(8,128)(2,1)S(1)}, bf16[2,3,16,1024]{3,2,1,0:T(8,128)(2,1)}, u32[]{:S(2)}, u32[]{:S(2)}) collective-permute-start(bf16[2,3,16,1024]{3,2,1,0:T(8,128)(2,1)S(1)} %collective-permute-done.8.refs_8_), channel_id=1, source_target_pairs={{0,2},{1,3},{2,0},{3,1},{4,6},{5,7},{6,4},{7,5},{8,10},{9,11},{10,... | collective-permute-start | bytes 589832 | tf_op jit(solution)/shard_map/ppermute | solution.py:151
  61.0 0.7 copy-done.3
  61.7 2.0 %collective-permute-done.6.refs_6_ = bf16[2,3,16,1024]{3,2,1,0:T(8,128)(2,1)} collective-permute-done((bf16[2,3,16,1024]{3,2,1,0:T(8,128)(2,1)S(1)}, bf16[2,3,16,1024]{3,2,1,0:T(8,128)(2,1)}, u32[]{:S(2)}, u32[]{:S(2)}) %collective-permute-start.6) | collective-permute-done | bytes 196640 | tf_op jit(solution)/shard_map/ppermute | solution.py:151
  63.8 0.3 collective-permute-start.14
  64.1 0.7 copy-done.5
  64.8 1.7 %collective-permute-start.20 = (bf16[3,64,1024]{2,1,0:T(8,128)(2,1)}, bf16[3,64,1024]{2,1,0:T(8,128)(2,1)}, u32[]{:S(2)}, u32[]{:S(2)}) collective-permute-start(bf16[3,64,1024]{2,1,0:T(8,128)(2,1)} %collective-permute-done.19.refs_20_), channel_id=1, source_target_pairs={{0,4},{4,0},{8,12},{12,8},{16,20},{20,16},{24,28},{28,24},{1,5},{5... | collective-permute-start | bytes 1179656 | tf_op jit(solution)/shard_map/ppermute | solution.py:143
  66.5 0.7 copy-done.7
  67.1 0.8 collective-permute-done.10.refs_10_
  68.0 0.7 copy-done.9
  68.7 0.5 collective-permute-start.11
  69.2 2.4 %collective-permute-done.14.refs_14_ = bf16[2,3,16,1024]{3,2,1,0:T(8,128)(2,1)} collective-permute-done((bf16[2,3,16,1024]{3,2,1,0:T(8,128)(2,1)}, bf16[2,3,16,1024]{3,2,1,0:T(8,128)(2,1)}, u32[]{:S(2)}, u32[]{:S(2)}) %collective-permute-start.14) | collective-permute-done | bytes 196640 | tf_op jit(solution)/shard_map/ppermute | solution.py:151
  71.6 2.7 %shard_map.46 = (bf16[4,256,256]{2,1,0:T(8,128)(2,1)}, bf16[4,256,256]{2,1,0:T(8,128)(2,1)}) custom-call(f32[64,128]{1,0:T(8,128)} %bitcast.28), custom_call_target="tpu_custom_call" | custom-call | tf_op jit(solution)/shard_map/pallas_call | solution.py:51
  74.3 2.7 %shard_map.47 = (bf16[4,256,256]{2,1,0:T(8,128)(2,1)}, bf16[4,256,256]{2,1,0:T(8,128)(2,1)}) custom-call(f32[64,128]{1,0:T(8,128)} %bitcast.29), custom_call_target="tpu_custom_call" | custom-call | tf_op jit(solution)/shard_map/pallas_call | solution.py:51
  77.0 0.0 copy-start.2
  77.0 1.0 %copy-done.2 = bf16[3,64,1024]{2,1,0:T(8,128)(2,1)S(1)} copy-done((bf16[3,64,1024]{2,1,0:T(8,128)(2,1)S(1)}, bf16[3,64,1024]{2,1,0:T(8,128)(2,1)}, u32[]{:S(2)}) %copy-start.2) | copy-done | bytes 393240
  78.0 0.9 copy-done.4
  78.9 0.9 copy-done.6
  79.9 0.9 copy-done.8
  80.8 0.9 copy-done.10
  81.7 14.4 %shard_map.48 = f32[1024,1024]{1,0:T(8,128)} custom-call(s32[1]{0:T(128)} %bitcast.place_ref, bf16[2,3,16,1024]{3,2,1,0:T(8,128)(2,1)S(1)} %bitcast.25, bf16[2,3,16,1024]{3,2,1,0:T(8,128)(2,1)} %collective-permute-done.1.refs_1_, bf16[2,3,16,1024]{3,2,1,0:T(8,128)(2,1)} %collective-permute-done.2.refs_2_, bf16[2,3,16,1024]{3,2,1,0:T(8,128)(2,1)S(1)} %copy-done.8, ...), custom_call_target="tpu_custom_call" | custom-call | tf_op jit(solution)/shard_map/pallas_call | solution.py:116
  (38 shorter events, 0.2 us)
Async XLA Ops:
  0.0 1.9 %copy-start = (bf16[3,64,8192]{2,1,0:T(8,128)(2,1)S(1)}, bf16[3,64,8192]{2,1,0:T(8,128)(2,1)}, u32[]{:S(2)}) copy-start(bf16[3,64,8192]{2,1,0:T(8,128)(2,1)} %param.4) | copy-start | bytes 9437188
  10.5 13.1 %collective-permute-start = (bf16[1,4,3,16,1024]{4,3,2,1,0:T(8,128)(2,1)S(1)}, bf16[1,4,3,16,1024]{4,3,2,1,0:T(8,128)(2,1)}, u32[]{:S(2)}, u32[]{:S(2)}) collective-permute-start(bf16[1,4,3,16,1024]{4,3,2,1,0:T(8,128)(2,1)S(1)} %copy.9), channel_id=1, source_target_pairs={{0,4},{4,0},{8,12},{12,8},{16,20},{20,16},{24,28},{28,24},{1,5},{5... | collective-permute-start | bytes 1179656 | tf_op jit(solution)/shard_map/ppermute | solution.py:143
  13.5 19.6 %collective-permute-start.17 = (bf16[3,64,1024]{2,1,0:T(8,128)(2,1)}, bf16[3,64,1024]{2,1,0:T(8,128)(2,1)}, u32[]{:S(2)}, u32[]{:S(2)}) collective-permute-start(bf16[3,64,1024]{2,1,0:T(8,128)(2,1)} %refs_16_.1), channel_id=1, source_target_pairs={{0,8},{4,12},{8,16},{12,20},{16,24},{20,28},{24,0},{28,4},{1,9},{5... | collective-permute-start | bytes 1179656 | tf_op jit(solution)/shard_map/ppermute | solution.py:146
  15.1 20.5 %collective-permute-start.16 = (bf16[3,64,1024]{2,1,0:T(8,128)(2,1)}, bf16[3,64,1024]{2,1,0:T(8,128)(2,1)}, u32[]{:S(2)}, u32[]{:S(2)}) collective-permute-start(bf16[3,64,1024]{2,1,0:T(8,128)(2,1)} %refs_16_.1), channel_id=1, source_target_pairs={{0,4},{4,0},{8,12},{12,8},{16,20},{20,16},{24,28},{28,24},{1,5},{5... | collective-permute-start | bytes 1179656 | tf_op jit(solution)/shard_map/ppermute | solution.py:143
  15.6 22.7 %collective-permute-start.21 = (bf16[3,64,1024]{2,1,0:T(8,128)(2,1)}, bf16[3,64,1024]{2,1,0:T(8,128)(2,1)}, u32[]{:S(2)}, u32[]{:S(2)}) collective-permute-start(bf16[3,64,1024]{2,1,0:T(8,128)(2,1)} %refs_16_.1), channel_id=1, source_target_pairs={{0,24},{4,28},{8,0},{12,4},{16,8},{20,12},{24,16},{28,20},{1,25},{... | collective-permute-start | bytes 1179656 | tf_op jit(solution)/shard_map/ppermute | solution.py:146
  25.4 7.7 %copy-start.11 = (bf16[1,4,3,16,1024]{4,0,1,3,2:T(2,128)(2,1)}, bf16[1,4,3,16,1024]{4,0,1,3,2:T(2,128)(2,1)S(1)}, u32[]{:S(2)}) copy-start(bf16[1,4,3,16,1024]{4,0,1,3,2:T(2,128)(2,1)S(1)} %copy.10) | copy-start | bytes 1179652
  29.4 9.4 %collective-permute-start.4 = (bf16[2,3,16,1024]{3,2,1,0:T(8,128)(2,1)}, bf16[2,3,16,1024]{3,2,1,0:T(8,128)(2,1)S(1)}, u32[]{:S(2)}, u32[]{:S(2)}) collective-permute-start(bf16[2,3,16,1024]{3,2,1,0:T(8,128)(2,1)} %bitcast.21), channel_id=1, source_target_pairs={{0,8},{4,12},{8,16},{12,20},{16,24},{20,28},{24,0},{28,4},{1,9},{5... | collective-permute-start | bytes 589832 | tf_op jit(solution)/shard_map/ppermute | solution.py:146
  31.6 8.4 %collective-permute-start.2 = (bf16[2,3,16,1024]{3,2,1,0:T(8,128)(2,1)S(1)}, bf16[2,3,16,1024]{3,2,1,0:T(8,128)(2,1)}, u32[]{:S(2)}, u32[]{:S(2)}) collective-permute-start(bf16[2,3,16,1024]{3,2,1,0:T(8,128)(2,1)S(1)} %bitcast.23), channel_id=1, source_target_pairs={{0,2},{1,3},{2,0},{3,1},{4,6},{5,7},{6,4},{7,5},{8,10},{9,11},{10,... | collective-permute-start | bytes 589832 | tf_op jit(solution)/shard_map/ppermute | solution.py:151
  33.1 7.8 %collective-permute-start.1 = (bf16[2,3,16,1024]{3,2,1,0:T(8,128)(2,1)S(1)}, bf16[2,3,16,1024]{3,2,1,0:T(8,128)(2,1)}, u32[]{:S(2)}, u32[]{:S(2)}) collective-permute-start(bf16[2,3,16,1024]{3,2,1,0:T(8,128)(2,1)S(1)} %bitcast.24), channel_id=1, source_target_pairs={{0,1},{1,0},{2,3},{3,2},{4,5},{5,4},{6,7},{7,6},{8,9},{9,8},{10,11... | collective-permute-start | bytes 589832 | tf_op jit(solution)/shard_map/ppermute | solution.py:151
  35.6 21.4 %collective-permute-start.8 = (bf16[2,3,16,1024]{3,2,1,0:T(8,128)(2,1)S(1)}, bf16[2,3,16,1024]{3,2,1,0:T(8,128)(2,1)S(1)}, u32[]{:S(2)}, u32[]{:S(2)}) collective-permute-start(bf16[2,3,16,1024]{3,2,1,0:T(8,128)(2,1)S(1)} %bitcast.27), channel_id=1, source_target_pairs={{0,16},{4,20},{8,24},{12,28},{16,0},{20,4},{24,8},{28,12},{1,17},{... | collective-permute-start | bytes 589832 | tf_op jit(solution)/shard_map/ppermute | solution.py:146
  38.3 20.2 %collective-permute-start.19 = (bf16[3,64,1024]{2,1,0:T(8,128)(2,1)}, bf16[3,64,1024]{2,1,0:T(8,128)(2,1)}, u32[]{:S(2)}, u32[]{:S(2)}) collective-permute-start(bf16[3,64,1024]{2,1,0:T(8,128)(2,1)} %collective-permute-done.17.refs_18_), channel_id=1, source_target_pairs={{0,8},{4,12},{8,16},{12,20},{16,24},{20,28},{24,0},{28,4},{1,9},{5... | collective-permute-start | bytes 1179656 | tf_op jit(solution)/shard_map/ppermute | solution.py:146
  38.8 20.2 %collective-permute-start.18 = (bf16[3,64,1024]{2,1,0:T(8,128)(2,1)}, bf16[3,64,1024]{2,1,0:T(8,128)(2,1)S(1)}, u32[]{:S(2)}, u32[]{:S(2)}) collective-permute-start(bf16[3,64,1024]{2,1,0:T(8,128)(2,1)} %collective-permute-done.17.refs_18_), channel_id=1, source_target_pairs={{0,4},{4,0},{8,12},{12,8},{16,20},{20,16},{24,28},{28,24},{1,5},{5... | collective-permute-start | bytes 1179656 | tf_op jit(solution)/shard_map/ppermute | solution.py:143
  40.0 21.0 %collective-permute-start.22 = (bf16[3,64,1024]{2,1,0:T(8,128)(2,1)}, bf16[3,64,1024]{2,1,0:T(8,128)(2,1)S(1)}, u32[]{:S(2)}, u32[]{:S(2)}) collective-permute-start(bf16[3,64,1024]{2,1,0:T(8,128)(2,1)} %collective-permute-done.21.refs_22_), channel_id=1, source_target_pairs={{0,4},{4,0},{8,12},{12,8},{16,20},{20,16},{24,28},{28,24},{1,5},{5... | collective-permute-start | bytes 1179656 | tf_op jit(solution)/shard_map/ppermute | solution.py:143
  40.8 17.6 %collective-permute-start.12 = (bf16[2,3,16,1024]{3,2,1,0:T(8,128)(2,1)S(1)}, bf16[2,3,16,1024]{3,2,1,0:T(8,128)(2,1)}, u32[]{:S(2)}, u32[]{:S(2)}) collective-permute-start(bf16[2,3,16,1024]{3,2,1,0:T(8,128)(2,1)S(1)} %bitcast.26), channel_id=1, source_target_pairs={{0,24},{4,28},{8,0},{12,4},{16,8},{20,12},{24,16},{28,20},{1,25},{... | collective-permute-start | bytes 589832 | tf_op jit(solution)/shard_map/ppermute | solution.py:146
  56.9 6.8 %collective-permute-start.6 = (bf16[2,3,16,1024]{3,2,1,0:T(8,128)(2,1)S(1)}, bf16[2,3,16,1024]{3,2,1,0:T(8,128)(2,1)}, u32[]{:S(2)}, u32[]{:S(2)}) collective-permute-start(bf16[2,3,16,1024]{3,2,1,0:T(8,128)(2,1)S(1)} %collective-permute-done.4.refs_4_), channel_id=1, source_target_pairs={{0,2},{1,3},{2,0},{3,1},{4,6},{5,7},{6,4},{7,5},{8,10},{9,11},{10,... | collective-permute-start | bytes 589832 | tf_op jit(solution)/shard_map/ppermute | solution.py:151
  58.5 5.6 %collective-permute-start.5 = (bf16[2,3,16,1024]{3,2,1,0:T(8,128)(2,1)S(1)}, bf16[2,3,16,1024]{3,2,1,0:T(8,128)(2,1)S(1)}, u32[]{:S(2)}, u32[]{:S(2)}) collective-permute-start(bf16[2,3,16,1024]{3,2,1,0:T(8,128)(2,1)S(1)} %collective-permute-done.4.refs_4_), channel_id=1, source_target_pairs={{0,1},{1,0},{2,3},{3,2},{4,5},{5,4},{6,7},{7,6},{8,9},{9,8},{10,11... | collective-permute-start | bytes 589832 | tf_op jit(solution)/shard_map/ppermute | solution.py:151
  58.5 8.0 %collective-permute-start.3 = (bf16[2,3,16,1024]{3,2,1,0:T(8,128)(2,1)}, bf16[2,3,16,1024]{3,2,1,0:T(8,128)(2,1)S(1)}, u32[]{:S(2)}, u32[]{:S(2)}) collective-permute-start(bf16[2,3,16,1024]{3,2,1,0:T(8,128)(2,1)} %collective-permute-done.2.refs_2_), channel_id=1, source_target_pairs={{0,1},{1,0},{2,3},{3,2},{4,5},{5,4},{6,7},{7,6},{8,9},{9,8},{10,11... | collective-permute-start | bytes 589832 | tf_op jit(solution)/shard_map/ppermute | solution.py:151
  59.0 0.7 copy-start.1
  59.7 8.3 %collective-permute-start.10 = (bf16[2,3,16,1024]{3,2,1,0:T(8,128)(2,1)S(1)}, bf16[2,3,16,1024]{3,2,1,0:T(8,128)(2,1)}, u32[]{:S(2)}, u32[]{:S(2)}) collective-permute-start(bf16[2,3,16,1024]{3,2,1,0:T(8,128)(2,1)S(1)} %collective-permute-done.8.refs_8_), channel_id=1, source_target_pairs={{0,2},{1,3},{2,0},{3,1},{4,6},{5,7},{6,4},{7,5},{8,10},{9,11},{10,... | collective-permute-start | bytes 589832 | tf_op jit(solution)/shard_map/ppermute | solution.py:151
  61.0 7.0 %copy-start.12 = (bf16[3,64,1024]{2,1,0:T(8,128)(2,1)}, bf16[3,64,1024]{2,1,0:T(8,128)(2,1)S(1)}, u32[]{:S(2)}) copy-start(bf16[3,64,1024]{2,1,0:T(8,128)(2,1)S(1)} %collective-permute-done.22.refs_23_) | copy-start | bytes 1179652
  61.0 7.0 %collective-permute-start.9 = (bf16[2,3,16,1024]{3,2,1,0:T(8,128)(2,1)S(1)}, bf16[2,3,16,1024]{3,2,1,0:T(8,128)(2,1)S(1)}, u32[]{:S(2)}, u32[]{:S(2)}) collective-permute-start(bf16[2,3,16,1024]{3,2,1,0:T(8,128)(2,1)S(1)} %collective-permute-done.8.refs_8_), channel_id=1, source_target_pairs={{0,1},{1,0},{2,3},{3,2},{4,5},{5,4},{6,7},{7,6},{8,9},{9,8},{10,11... | collective-permute-start | bytes 589832 | tf_op jit(solution)/shard_map/ppermute | solution.py:151
  61.0 0.7 copy-start.3
  63.8 7.8 %collective-permute-start.14 = (bf16[2,3,16,1024]{3,2,1,0:T(8,128)(2,1)}, bf16[2,3,16,1024]{3,2,1,0:T(8,128)(2,1)}, u32[]{:S(2)}, u32[]{:S(2)}) collective-permute-start(bf16[2,3,16,1024]{3,2,1,0:T(8,128)(2,1)} %collective-permute-done.12.refs_12_), channel_id=1, source_target_pairs={{0,2},{1,3},{2,0},{3,1},{4,6},{5,7},{6,4},{7,5},{8,10},{9,11},{10,... | collective-permute-start | bytes 589832 | tf_op jit(solution)/shard_map/ppermute | solution.py:151
  64.1 0.7 copy-start.5
  64.8 12.2 %collective-permute-start.20 = (bf16[3,64,1024]{2,1,0:T(8,128)(2,1)}, bf16[3,64,1024]{2,1,0:T(8,128)(2,1)}, u32[]{:S(2)}, u32[]{:S(2)}) collective-permute-start(bf16[3,64,1024]{2,1,0:T(8,128)(2,1)} %collective-permute-done.19.refs_20_), channel_id=1, source_target_pairs={{0,4},{4,0},{8,12},{12,8},{16,20},{20,16},{24,28},{28,24},{1,5},{5... | collective-permute-start | bytes 1179656 | tf_op jit(solution)/shard_map/ppermute | solution.py:143
  66.5 0.7 copy-start.7
  67.1 9.8 %collective-permute-start.13 = (bf16[2,3,16,1024]{3,2,1,0:T(8,128)(2,1)}, bf16[2,3,16,1024]{3,2,1,0:T(8,128)(2,1)}, u32[]{:S(2)}, u32[]{:S(2)}) collective-permute-start(bf16[2,3,16,1024]{3,2,1,0:T(8,128)(2,1)} %collective-permute-done.12.refs_12_), channel_id=1, source_target_pairs={{0,1},{1,0},{2,3},{3,2},{4,5},{5,4},{6,7},{7,6},{8,9},{9,8},{10,11... | collective-permute-start | bytes 589832 | tf_op jit(solution)/shard_map/ppermute | solution.py:151
  68.0 9.0 %collective-permute-start.7 = (bf16[2,3,16,1024]{3,2,1,0:T(8,128)(2,1)}, bf16[2,3,16,1024]{3,2,1,0:T(8,128)(2,1)}, u32[]{:S(2)}, u32[]{:S(2)}) collective-permute-start(bf16[2,3,16,1024]{3,2,1,0:T(8,128)(2,1)} %collective-permute-done.6.refs_6_), channel_id=1, source_target_pairs={{0,1},{1,0},{2,3},{3,2},{4,5},{5,4},{6,7},{7,6},{8,9},{9,8},{10,11... | collective-permute-start | bytes 589832 | tf_op jit(solution)/shard_map/ppermute | solution.py:151
  68.0 0.7 copy-start.9
  68.7 8.3 %collective-permute-start.11 = (bf16[2,3,16,1024]{3,2,1,0:T(8,128)(2,1)}, bf16[2,3,16,1024]{3,2,1,0:T(8,128)(2,1)}, u32[]{:S(2)}, u32[]{:S(2)}) collective-permute-start(bf16[2,3,16,1024]{3,2,1,0:T(8,128)(2,1)} %collective-permute-done.10.refs_10_), channel_id=1, source_target_pairs={{0,1},{1,0},{2,3},{3,2},{4,5},{5,4},{6,7},{7,6},{8,9},{9,8},{10,11... | collective-permute-start | bytes 589832 | tf_op jit(solution)/shard_map/ppermute | solution.py:151
  71.6 5.4 %collective-permute-start.15 = (bf16[2,3,16,1024]{3,2,1,0:T(8,128)(2,1)}, bf16[2,3,16,1024]{3,2,1,0:T(8,128)(2,1)}, u32[]{:S(2)}, u32[]{:S(2)}) collective-permute-start(bf16[2,3,16,1024]{3,2,1,0:T(8,128)(2,1)} %collective-permute-done.14.refs_14_), channel_id=1, source_target_pairs={{0,1},{1,0},{2,3},{3,2},{4,5},{5,4},{6,7},{7,6},{8,9},{9,8},{10,11... | collective-permute-start | bytes 589832 | tf_op jit(solution)/shard_map/ppermute | solution.py:151
  77.0 1.0 %copy-start.2 = (bf16[3,64,1024]{2,1,0:T(8,128)(2,1)S(1)}, bf16[3,64,1024]{2,1,0:T(8,128)(2,1)}, u32[]{:S(2)}) copy-start(bf16[3,64,1024]{2,1,0:T(8,128)(2,1)} %copy-done.1) | copy-start | bytes 1179652
  78.0 0.9 copy-start.4
  78.9 0.9 copy-start.6
  79.9 0.9 copy-start.8
  80.8 0.9 copy-start.10

commit v2 on v0

v2 whole, which is shorter than its diff:
```python
import functools

import jax
import jax.numpy as jnp
from jax import lax
from jax.experimental import pallas as pl
from jax.experimental.pallas import tpu as pltpu
from jax.sharding import PartitionSpec as P

BF, F32 = jnp.bfloat16, jnp.float32
SCALARS = pl.BlockSpec(memory_space=pltpu.SMEM)
VECTORS = pl.BlockSpec(memory_space=pltpu.VMEM)


def dot(a, b, contract):
    return lax.dot_general(a, b, (contract, ((), ())), preferred_element_type=F32)


def split(value):
    high = value.astype(BF)
    return high, (value - high.astype(F32)).astype(BF)


def run_all(copies):
    for copy in copies:
        copy.start()
    for copy in copies:
        copy.wait()


def limit(*specs):
    total = sum(2 * s.size * jnp.dtype(s.dtype).itemsize for s in specs)
    return total + 8 * 2**20


def spread_one(transposed, basis_ref, high_ref, low_ref):
    groups, span, _ = high_ref.shape
    blocks = basis_ref.shape[1]
    parts = split(basis_ref[...])
    iota = lambda shape, dim: lax.broadcasted_iota(jnp.int32, shape, dim)
    pq_row, pq_col = (
        (iota((span, 64), 1) % 8, iota((64, span), 0) // 8)
        if transposed
        else (iota((span, 64), 1) // 8, iota((64, span), 0) % 8)
    )
    keep = pq_row == iota((span, 64), 0) % 8
    repeat = (pq_col == iota((64, span), 1) % 8).astype(BF)
    diagonal = iota((span, span), 0) // 8 == iota((span, span), 1) // 8
    for g in range(groups):
        pick = iota((span, blocks), 0) // 8 + g * (span // 8) == iota((span, blocks), 1)
        pick = pick.astype(BF)
        for part, out_ref in zip(parts, (high_ref, low_ref)):
            rows = dot(pick, part, ((1,), (1,)))
            rows = jnp.where(keep, rows, 0.0).astype(BF)
            full = dot(rows, repeat, ((1,), (0,)))
            out_ref[g] = jnp.where(diagonal, full, 0.0).astype(BF)


def spread_kernel(a_ref, g_ref, a_high, a_low, g_high, g_low):
    spread_one(False, a_ref, a_high, a_low)
    spread_one(True, g_ref, g_high, g_low)


def spread(act_basis, grad_basis):
    flat, shapes = [], []
    for basis in (act_basis, grad_basis):
        blocks = basis.shape[0]
        span = min(256, blocks * 8)
        flat.append(jnp.transpose(basis, (1, 2, 0)).reshape(64, blocks))
        shapes += [jax.ShapeDtypeStruct((blocks * 8 // span, span, span), BF)] * 2
    out = pl.pallas_call(
        spread_kernel,
        out_shape=tuple(shapes),
        compiler_params=pltpu.CompilerParams(vmem_limit_bytes=limit(*shapes)),
        name="spread",
    )(*flat)
    return out[:2], out[2:]


def cut_kernel(half, where_ref, acts_ref, *refs):
    *outs, sems = refs
    q, z, y = where_ref[0], where_ref[1], where_ref[2]
    _, _, quarter, width = outs[0].shape[0:4]
    copies = []
    for k in range(half):
        for other in range(2):
            column = ((z + k) % half * 2 + (y ^ other)) * width
            copies.append(
                pltpu.make_async_copy(
                    acts_ref.at[
                        :,
                        pl.ds(pl.multiple_of(q * quarter, quarter), quarter),
                        pl.ds(pl.multiple_of(column, width), width),
                    ],
                    outs[k].at[other],
                    sems.at[2 * k + other],
                )
            )
    run_all(copies)


def cut(acts, where, n, m):
    seqs, rows, total = acts.shape
    shape = jax.ShapeDtypeStruct((2, seqs, rows // m, total // n), BF)
    return pl.pallas_call(
        functools.partial(cut_kernel, n // 2),
        in_specs=[SCALARS, pl.BlockSpec(memory_space=pltpu.HBM)],
        out_specs=[VECTORS] * (n // 2),
        out_shape=[shape] * (n // 2),
        scratch_shapes=[pltpu.SemaphoreType.DMA((n,))],
        compiler_params=pltpu.CompilerParams(vmem_limit_bytes=limit(*[shape] * (n // 2))),
        name="cut",
    )(where, acts)


def part_kernel(*refs):
    *pieces, stay, go = refs
    for k, piece in enumerate(pieces):
        stay[k], go[k] = piece[0], piece[1]


def part(pieces):
    half = len(pieces)
    shape = jax.ShapeDtypeStruct((half, *pieces[0].shape[1:]), BF)
    return pl.pallas_call(
        part_kernel,
        in_specs=[VECTORS] * half,
        out_specs=[VECTORS] * 2,
        out_shape=[shape] * 2,
        compiler_params=pltpu.CompilerParams(vmem_limit_bytes=limit(shape, shape)),
        name="part",
    )(*pieces)


def turn_acts_kernel(order, m, where_ref, *refs):
    pieces, (high, low, out_ref) = refs[: 2 * m], refs[2 * m :]
    half, seqs, quarter, width = pieces[0].shape
    rows = quarter * m
    groups, span, _ = high.shape
    for j in range(m):
        place = pl.multiple_of((where_ref[0] ^ j) * quarter, quarter)
        for other in range(2):
            piece = pieces[2 * j + other]
            for g in range(groups):
                columns = pl.ds(g * span, span)
                block = piece[:, :, :, columns].reshape(half * seqs * quarter, span)
                turned = dot(block, high[g], ((1,), (0,))) + dot(block, low[g], ((1,), (0,)))
                turned = turned.astype(BF).reshape(half, seqs, quarter, span)
                for at, k in enumerate(order):
                    to = pl.ds(place + (2 * at + other) * rows, quarter)
                    out_ref[:, to, columns] = turned[k]


def turn_acts(where, pieces, parts, order, m):
    half, seqs, quarter, width = pieces[0].shape
    shape = jax.ShapeDtypeStruct((seqs, 2 * half * m * quarter, width), BF)
    return pl.pallas_call(
        functools.partial(turn_acts_kernel, order, m),
        in_specs=[SCALARS] + [VECTORS] * (2 * m + 2),
        out_specs=VECTORS,
        out_shape=shape,
        compiler_params=pltpu.CompilerParams(vmem_limit_bytes=limit(shape, shape)),
        name="turn_acts",
    )(where, *pieces, *parts)


def turn_pair(high, low, first, second):
    block = jnp.concatenate([first, second], 0)
    return (dot(high, block, ((1,), (1,))) + dot(low, block, ((1,), (1,)))).astype(BF)


def turn_grads_kernel(*refs):
    *pieces, high, low, out_ref = refs
    seqs, rows, width = pieces[0].shape
    groups, span, _ = high.shape
    for g in range(groups):
        columns = pl.ds(g * span, span)
        for s in range(seqs):
            for k in range(len(pieces) // 2):
                out_ref[s, columns, pl.ds(k * 2 * rows, 2 * rows)] = turn_pair(
                    high[g], low[g], pieces[2 * k][s, :, columns], pieces[2 * k + 1][s, :, columns]
                )


def turn_grads(pieces, parts):
    seqs, rows, width = pieces[0].shape
    shape = jax.ShapeDtypeStruct((seqs, width, len(pieces) * rows), BF)
    return pl.pallas_call(
        turn_grads_kernel,
        in_specs=[VECTORS] * (len(pieces) + 2),
        out_specs=VECTORS,
        out_shape=shape,
        compiler_params=pltpu.CompilerParams(vmem_limit_bytes=limit(shape, shape)),
        name="turn_grads",
    )(*pieces, *parts)


def multiply_kernel(scale, first, second, high, low, grads, acts, out_ref):
    total = None
    for s in range(acts.shape[0]):
        late = turn_pair(high[0], low[0], first[s], second[s])
        corr = dot(jnp.concatenate([grads[s], late], 1), acts[s], ((1,), (0,)))
        total = corr * corr if total is None else total + corr * corr
    out_ref[...] = total * scale


def multiply(last, parts, grads, acts):
    seqs, rows, outs = last[0].shape
    _, length, width = acts.shape
    tile = parts[0].shape[1]
    shape = jax.ShapeDtypeStruct((outs, width), F32)
    return pl.pallas_call(
        functools.partial(multiply_kernel, 1.0 / length),
        grid=(outs // tile,),
        in_specs=[pl.BlockSpec((seqs, rows, tile), lambda i: (0, 0, i))] * 2
        + [pl.BlockSpec((1, tile, tile), lambda i: (i, 0, 0))] * 2
        + [
            pl.BlockSpec((seqs, tile, grads.shape[2]), lambda i: (0, i, 0)),
            pl.BlockSpec((seqs, length, width), lambda i: (0, 0, 0)),
        ],
        out_specs=pl.BlockSpec((tile, width), lambda i: (i, 0)),
        out_shape=shape,
        compiler_params=pltpu.CompilerParams(
            vmem_limit_bytes=limit(acts, jax.ShapeDtypeStruct((seqs, tile, length), BF))
        ),
        name="multiply",
    )(*last, *parts, grads, acts)


def after(value, *earlier):
    return lax.optimization_barrier((value, *earlier))[0]


def shards(acts, grads, act_basis, grad_basis):
    n, m = lax.axis_size("tok"), lax.axis_size("out")
    half = n // 2
    t, q = lax.axis_index("tok"), lax.axis_index("out")
    where = jnp.stack([q, t // 2, t % 2]).astype(jnp.int32)

    def over_y(name, value):
        with jax.named_scope(name):
            return lax.ppermute(value, "tok", [(i, i ^ 1) for i in range(n)])

    def over_z(name, value, shift):
        with jax.named_scope(name):
            return lax.ppermute(
                value, "tok", [(i, (i // 2 + shift) % half * 2 + i % 2) for i in range(n)]
            )

    def over_out(name, value, bit):
        with jax.named_scope(name):
            return lax.ppermute(value, "out", [(i, i ^ bit) for i in range(m)])

    act_parts, grad_parts = spread(act_basis, grad_basis)

    cuts = cut(acts, where, n, m)
    came = [cuts[0]] + [over_z(f"acts_z{k}", cuts[k], k) for k in range(1, half)]
    stay, go = part(came)
    held = {0: [stay, over_y("acts_y", go)]}
    bit = m // 2
    while bit:
        for j, pair in list(held.items()):
            held[j | bit] = [over_out(f"acts_out{j | bit}", v, bit) for v in pair]
        bit //= 2

    ring = {0: grads}
    for k in range(1, (half - 1) // 2 + 1):
        ring[half - k] = over_z(f"grads_z{half - k}", ring[(half - k + 1) % half], -1)
    for k in range(1, half // 2 + 1):
        ring[k] = over_z(f"grads_z{k}", ring[k - 1], 1)
    order = [k for k in range(half) if k != half // 2] + [half // 2]
    pairs = [[ring[k], over_y(f"grads_y{k}", ring[k])] for k in order]

    pieces = [v for j in range(m) for v in held[j]]
    turned_acts = turn_acts(where, pieces, act_parts, order, m)
    turned_grads = turn_grads([v for pair in pairs[:-1] for v in pair], grad_parts)
    return multiply(pairs[-1], grad_parts, turned_grads, turned_acts)


def solution(mesh):
    placed = (
        P(None, "tok", None),
        P(None, "tok", "out"),
        P("tok", None, None),
        P("out", None, None),
    )
    return jax.shard_map(
        shards, mesh=mesh, in_specs=placed, out_specs=P("out", "tok"), check_vma=False
    )
```

time: 178 us -> 76.7 us (0.43)
  the two profiles are of different devices: /device:TPU:0 before, /device:TPU:8 now
where the time goes in v2:
time: 76.7 us; the launch traced here: 76.5 us
  waiting for transfers between devices  43.3 us (56%)
  starting transfers between devices  16.6 us (22%)
  Pallas kernels  14.6 us (19%)
  local copies, waits for them, and re-layouts  1.9 us (2%)
    ppermute x6, waiting for transfers between devices, over_z(): lax.ppermute(value, 'tok', [(i, (i // 2 + shift) % half * 2 + i % 2) for...  33 us
    ppermute x5, waiting for transfers between devices, over_y(): return lax.ppermute(value, 'tok', [(i, i ^ 1) for i in range(n)])  10.2 us
    ppermute x6, starting transfers between devices, over_z(): lax.ppermute(value, 'tok', [(i, (i // 2 + shift) % half * 2 + i % 2) for...  7.37 us
    pallas_call x1, Pallas kernels, multiply(): pl.pallas_call(functools.partial(multiply_kernel, 1.0 / length), grid=(ou...  6.8 us
    ppermute x5, starting transfers between devices, over_y(): return lax.ppermute(value, 'tok', [(i, i ^ 1) for i in range(n)])  5.25 us
    ppermute x6, starting transfers between devices, over_out(): return lax.ppermute(value, 'out', [(i, i ^ bit) for i in range(m)])  3.97 us
    pallas_call x1, Pallas kernels, turn_grads(): pl.pallas_call(turn_grads_kernel, in_specs=[VECTORS] * (len(pieces) + 2),...  2.63 us
    pallas_call x1, Pallas kernels, turn_acts(): pl.pallas_call(functools.partial(turn_acts_kernel, order, m), in_specs=[S...  2.5 us
  transfers between devices with their start and end apart: 17, of which 8 were waited for; matrix products, arithmetic and copies ran while one was open for 0% of the time, Pallas kernels for 9%

profile of v2, /device:TPU:8, one launch (start us, length us, event | category | flops | bytes accessed | tf_op | source)
XLA Modules:
  0.0 76.5 jit_solution(7322390757580636954)
XLA Ops:
  0.0 0.0 copy-start.2
  0.0 0.1 pad_add_fusion.where_ref
  0.1 0.0 copy-start
  0.1 1.9 %copy-done = bf16[3,64,8192]{2,1,0:T(8,128)(2,1)S(1)} copy-done((bf16[3,64,8192]{2,1,0:T(8,128)(2,1)S(1)}, bf16[3,64,8192]{2,1,0:T(8,128)(2,1)}, u32[]{:S(2)}) %copy-start) | copy-done | bytes 3145752
  2.0 0.0 copy-start.1
  2.0 0.8 %cut.1 = (bf16[2,3,16,1024]{3,2,1,0:T(8,128)(2,1)S(1)}, bf16[2,3,16,1024]{3,2,1,0:T(8,128)(2,1)S(1)}, bf16[2,3,16,1024]{3,2,1,0:T(8,128)(2,1)S(1)}, bf16[2,3,16,1024]{3,2,1,0:T(8,128)(2,1)S(1)}) custom-call(s32[3]{0:T(128)S(1)} %pad_add_fusion.where_ref, bf16[3,64,8192]{2,1,0:T(8,128)(2,1)S(1)} %copy-done), custom_call_target="tpu_custom_call" | custom-call | tf_op jit(solution)/shard_map/cut/pallas_call | solution.py:105
  2.8 1.6 %collective-permute-start.7 = (bf16[2,3,16,1024]{3,2,1,0:T(8,128)(2,1)S(1)}, bf16[2,3,16,1024]{3,2,1,0:T(8,128)(2,1)S(1)}, u32[]{:S(2)}, u32[]{:S(2)}) collective-permute-start(bf16[2,3,16,1024]{3,2,1,0:T(8,128)(2,1)S(1)} %get-tuple-element.18), channel_id=1, source_target_pairs={{0,8},{4,12},{8,16},{12,20},{16,24},{20,28},{24,0},{28,4},{1,9},{5... | collective-permute-start | bytes 589832 | tf_op jit(solution)/shard_map/acts_z1/ppermute | solution.py:246
  4.4 1.1 %collective-permute-start.8 = (bf16[2,3,16,1024]{3,2,1,0:T(8,128)(2,1)S(1)}, bf16[2,3,16,1024]{3,2,1,0:T(8,128)(2,1)S(1)}, u32[]{:S(2)}, u32[]{:S(2)}) collective-permute-start(bf16[2,3,16,1024]{3,2,1,0:T(8,128)(2,1)S(1)} %get-tuple-element.19), channel_id=1, source_target_pairs={{0,16},{4,20},{8,24},{12,28},{16,0},{20,4},{24,8},{28,12},{1,17},{... | collective-permute-start | bytes 589832 | tf_op jit(solution)/shard_map/acts_z2/ppermute | solution.py:246
  5.5 1.9 %collective-permute-start.9 = (bf16[2,3,16,1024]{3,2,1,0:T(8,128)(2,1)S(1)}, bf16[2,3,16,1024]{3,2,1,0:T(8,128)(2,1)S(1)}, u32[]{:S(2)}, u32[]{:S(2)}) collective-permute-start(bf16[2,3,16,1024]{3,2,1,0:T(8,128)(2,1)S(1)} %get-tuple-element.20), channel_id=1, source_target_pairs={{0,24},{4,28},{8,0},{12,4},{16,8},{20,12},{24,16},{28,20},{1,25},{... | collective-permute-start | bytes 589832 | tf_op jit(solution)/shard_map/acts_z3/ppermute | solution.py:246
  7.5 0.0 copy-done.1
  7.5 1.5 %collective-permute-start.3 = (bf16[3,64,1024]{2,1,0:T(8,128)(2,1)S(1)}, bf16[3,64,1024]{2,1,0:T(8,128)(2,1)S(1)}, u32[]{:S(2)}, u32[]{:S(2)}) collective-permute-start(bf16[3,64,1024]{2,1,0:T(8,128)(2,1)S(1)} %copy-done.1), channel_id=1, source_target_pairs={{0,4},{4,0},{8,12},{12,8},{16,20},{20,16},{24,28},{28,24},{1,5},{5... | collective-permute-start | bytes 1179656 | tf_op jit(solution)/shard_map/grads_y0/ppermute | solution.py:242
  9.0 0.2 collective-permute-start
  9.2 8.6 %collective-permute-done.7.refs_1_ = bf16[2,3,16,1024]{3,2,1,0:T(8,128)(2,1)S(1)} collective-permute-done((bf16[2,3,16,1024]{3,2,1,0:T(8,128)(2,1)S(1)}, bf16[2,3,16,1024]{3,2,1,0:T(8,128)(2,1)S(1)}, u32[]{:S(2)}, u32[]{:S(2)}) %collective-permute-start.7) | collective-permute-done | bytes 196640 | tf_op jit(solution)/shard_map/acts_z1/ppermute | solution.py:246
  17.8 4.6 %collective-permute-done.8.refs_2_ = bf16[2,3,16,1024]{3,2,1,0:T(8,128)(2,1)S(1)} collective-permute-done((bf16[2,3,16,1024]{3,2,1,0:T(8,128)(2,1)S(1)}, bf16[2,3,16,1024]{3,2,1,0:T(8,128)(2,1)S(1)}, u32[]{:S(2)}, u32[]{:S(2)}) %collective-permute-start.8) | collective-permute-done | bytes 196640 | tf_op jit(solution)/shard_map/acts_z2/ppermute | solution.py:246
  22.4 9.0 %collective-permute-done.9.refs_3_ = bf16[2,3,16,1024]{3,2,1,0:T(8,128)(2,1)S(1)} collective-permute-done((bf16[2,3,16,1024]{3,2,1,0:T(8,128)(2,1)S(1)}, bf16[2,3,16,1024]{3,2,1,0:T(8,128)(2,1)S(1)}, u32[]{:S(2)}, u32[]{:S(2)}) %collective-permute-start.9) | collective-permute-done | bytes 196640 | tf_op jit(solution)/shard_map/acts_z3/ppermute | solution.py:246
  31.4 0.1 part.1
  31.5 1.6 %collective-permute-start.10 = (bf16[4,3,16,1024]{3,2,1,0:T(8,128)(2,1)S(1)}, bf16[4,3,16,1024]{3,2,1,0:T(8,128)(2,1)S(1)}, u32[]{:S(2)}, u32[]{:S(2)}) collective-permute-start(bf16[4,3,16,1024]{3,2,1,0:T(8,128)(2,1)S(1)} %get-tuple-element.22), channel_id=1, source_target_pairs={{0,4},{4,0},{8,12},{12,8},{16,20},{20,16},{24,28},{28,24},{1,5},{5... | collective-permute-start | bytes 1179656 | tf_op jit(solution)/shard_map/acts_y/ppermute | solution.py:242
  33.1 0.0 collective-permute-start.5
  33.1 1.5 %collective-permute-start.13 = (bf16[4,3,16,1024]{3,2,1,0:T(8,128)(2,1)S(1)}, bf16[4,3,16,1024]{3,2,1,0:T(8,128)(2,1)S(1)}, u32[]{:S(2)}, u32[]{:S(2)}) collective-permute-start(bf16[4,3,16,1024]{3,2,1,0:T(8,128)(2,1)S(1)} %get-tuple-element.21.refs_0_), channel_id=1, source_target_pairs={{0,2},{1,3},{2,0},{3,1},{4,6},{5,7},{6,4},{7,5},{8,10},{9,11},{10,... | collective-permute-start | bytes 1179656 | tf_op jit(solution)/shard_map/acts_out2/ppermute | solution.py:252
  34.6 3.6 %collective-permute-done.refs_2_ = bf16[3,64,1024]{2,1,0:T(8,128)(2,1)S(1)} collective-permute-done((bf16[3,64,1024]{2,1,0:T(8,128)(2,1)S(1)}, bf16[3,64,1024]{2,1,0:T(8,128)(2,1)S(1)}, u32[]{:S(2)}, u32[]{:S(2)}) %collective-permute-start) | collective-permute-done | bytes 393248 | tf_op jit(solution)/shard_map/grads_z1/ppermute | solution.py:246
  38.1 1.5 %collective-permute-start.4 = (bf16[3,64,1024]{2,1,0:T(8,128)(2,1)S(1)}, bf16[3,64,1024]{2,1,0:T(8,128)(2,1)S(1)}, u32[]{:S(2)}, u32[]{:S(2)}) collective-permute-start(bf16[3,64,1024]{2,1,0:T(8,128)(2,1)S(1)} %collective-permute-done.refs_2_), channel_id=1, source_target_pairs={{0,4},{4,0},{8,12},{12,8},{16,20},{20,16},{24,28},{28,24},{1,5},{5... | collective-permute-start | bytes 1179656 | tf_op jit(solution)/shard_map/grads_y1/ppermute | solution.py:242
  39.7 0.0 collective-permute-done.3.refs_1_
  39.7 2.5 %collective-permute-start.1 = (bf16[3,64,1024]{2,1,0:T(8,128)(2,1)S(1)}, bf16[3,64,1024]{2,1,0:T(8,128)(2,1)S(1)}, u32[]{:S(2)}, u32[]{:S(2)}) collective-permute-start(bf16[3,64,1024]{2,1,0:T(8,128)(2,1)S(1)} %collective-permute-done.refs_2_), channel_id=1, source_target_pairs={{0,8},{4,12},{8,16},{12,20},{16,24},{20,28},{24,0},{28,4},{1,9},{5... | collective-permute-start | bytes 1179656 | tf_op jit(solution)/shard_map/grads_z2/ppermute | solution.py:246
  42.1 1.4 %collective-permute-done.10.refs_1_ = bf16[4,3,16,1024]{3,2,1,0:T(8,128)(2,1)S(1)} collective-permute-done((bf16[4,3,16,1024]{3,2,1,0:T(8,128)(2,1)S(1)}, bf16[4,3,16,1024]{3,2,1,0:T(8,128)(2,1)S(1)}, u32[]{:S(2)}, u32[]{:S(2)}) %collective-permute-start.10) | collective-permute-done | bytes 393248 | tf_op jit(solution)/shard_map/acts_y/ppermute | solution.py:242
  43.5 1.5 %collective-permute-start.14 = (bf16[4,3,16,1024]{3,2,1,0:T(8,128)(2,1)S(1)}, bf16[4,3,16,1024]{3,2,1,0:T(8,128)(2,1)S(1)}, u32[]{:S(2)}, u32[]{:S(2)}) collective-permute-start(bf16[4,3,16,1024]{3,2,1,0:T(8,128)(2,1)S(1)} %collective-permute-done.10.refs_1_), channel_id=1, source_target_pairs={{0,2},{1,3},{2,0},{3,1},{4,6},{5,7},{6,4},{7,5},{8,10},{9,11},{10,... | collective-permute-start | bytes 1179656 | tf_op jit(solution)/shard_map/acts_out2/ppermute | solution.py:252
  45.0 7.2 %collective-permute-done.5.refs_4_ = bf16[3,64,1024]{2,1,0:T(8,128)(2,1)S(1)} collective-permute-done((bf16[3,64,1024]{2,1,0:T(8,128)(2,1)S(1)}, bf16[3,64,1024]{2,1,0:T(8,128)(2,1)S(1)}, u32[]{:S(2)}, u32[]{:S(2)}) %collective-permute-start.5) | collective-permute-done | bytes 393248 | tf_op jit(solution)/shard_map/grads_z3/ppermute | solution.py:246
  52.2 0.5 collective-permute-start.6
  52.8 0.0 collective-permute-done.13.refs_4_
  52.8 0.0 collective-permute-start.11
  52.8 0.0 collective-permute-done.4.refs_3_
  52.8 0.5 collective-permute-start.12
  53.3 0.0 collective-permute-done.1.first
  53.3 0.1 collective-permute-start.15
  53.4 0.0 collective-permute-done.14.refs_5_
  53.4 0.4 collective-permute-start.16
  53.8 8.1 %collective-permute-done.6.refs_5_ = bf16[3,64,1024]{2,1,0:T(8,128)(2,1)S(1)} collective-permute-done((bf16[3,64,1024]{2,1,0:T(8,128)(2,1)S(1)}, bf16[3,64,1024]{2,1,0:T(8,128)(2,1)S(1)}, u32[]{:S(2)}, u32[]{:S(2)}) %collective-permute-start.6) | collective-permute-done | bytes 393248 | tf_op jit(solution)/shard_map/grads_y3/ppermute | solution.py:242
  61.9 0.1 collective-permute-start.2
  62.1 0.0 copy-done.2
  62.1 0.0 copy-done.3
  62.1 1.8 %spread.1 = (bf16[4,256,256]{2,1,0:T(8,128)(2,1)S(1)}, bf16[4,256,256]{2,1,0:T(8,128)(2,1)S(1)}, bf16[4,256,256]{2,1,0:T(8,128)(2,1)S(1)}, bf16[4,256,256]{2,1,0:T(8,128)(2,1)S(1)}) custom-call(f32[64,128]{1,0:T(8,128)S(1)} %bitcast.9, f32[64,128]{1,0:T(8,128)S(1)} %bitcast.10), custom_call_target="tpu_custom_call" | custom-call | tf_op jit(solution)/shard_map/spread/pallas_call | solution.py:71
  63.9 2.6 %turn_grads.1.grads = bf16[3,1024,384]{2,1,0:T(8,128)(2,1)S(1)} custom-call(bf16[3,64,1024]{2,1,0:T(8,128)(2,1)S(1)} %copy-done.1, bf16[3,64,1024]{2,1,0:T(8,128)(2,1)S(1)} %collective-permute-done.3.refs_1_, bf16[3,64,1024]{2,1,0:T(8,128)(2,1)S(1)} %collective-permute-done.refs_2_, bf16[3,64,1024]{2,1,0:T(8,128)(2,1)S(1)} %collective-permute-done.4.refs_3_, ...), custom_call_target="tpu_custom_call" | custom-call | tf_op jit(solution)/shard_map/turn_grads/pallas_call | solution.py:188
  66.5 0.0 collective-permute-done.11.refs_2_
  66.5 0.0 collective-permute-done.12.refs_3_
  66.5 0.0 collective-permute-done.15.refs_6_
  66.5 0.0 collective-permute-done.16.refs_7_
  66.5 2.5 %turn_acts.1.acts = bf16[3,512,1024]{2,1,0:T(8,128)(2,1)S(1)} custom-call(s32[3]{0:T(128)S(1)} %pad_add_fusion.where_ref, bf16[4,3,16,1024]{3,2,1,0:T(8,128)(2,1)S(1)} %get-tuple-element.21.refs_0_, bf16[4,3,16,1024]{3,2,1,0:T(8,128)(2,1)S(1)} %collective-permute-done.10.refs_1_, bf16[4,3,16,1024]{3,2,1,0:T(8,128)(2,1)S(1)} %collective-permute-done.11.refs_2_, ...), custom_call_target="tpu_custom_call" | custom-call | tf_op jit(solution)/shard_map/turn_acts/pallas_call | solution.py:157
  69.1 0.7 collective-permute-done.2.second
  69.7 6.8 %multiply.1 = f32[1024,1024]{1,0:T(8,128)} custom-call(bf16[3,64,1024]{2,1,0:T(8,128)(2,1)S(1)} %collective-permute-done.1.first, bf16[3,64,1024]{2,1,0:T(8,128)(2,1)S(1)} %collective-permute-done.2.second, bf16[4,256,256]{2,1,0:T(8,128)(2,1)S(1)} %get-tuple-element.15.refs_6_.high, bf16[4,256,256]{2,1,0:T(8,128)(2,1)S(1)} %get-tuple-element.16.refs_7_.low, ...), custom_call_target="tpu_custom_call" | custom-call | tf_op jit(solution)/shard_map/multiply/pallas_call | solution.py:212
  (1 shorter events, 0.0 us)
Async XLA Ops:
  0.0 62.1 %copy-start.2 = (f32[128,8,8]{0,2,1:T(8,128)S(1)}, f32[128,8,8]{0,2,1:T(8,128)}, u32[]{:S(2)}) copy-start(f32[128,8,8]{0,2,1:T(8,128)} %param.6) | copy-start | bytes 98308
  0.1 1.9 %copy-start = (bf16[3,64,8192]{2,1,0:T(8,128)(2,1)S(1)}, bf16[3,64,8192]{2,1,0:T(8,128)(2,1)}, u32[]{:S(2)}) copy-start(bf16[3,64,8192]{2,1,0:T(8,128)(2,1)} %acts_ref.1) | copy-start | bytes 9437188
  2.0 5.5 %copy-start.1 = (bf16[3,64,1024]{2,1,0:T(8,128)(2,1)S(1)}, bf16[3,64,1024]{2,1,0:T(8,128)(2,1)}, u32[]{:S(2)}) copy-start(bf16[3,64,1024]{2,1,0:T(8,128)(2,1)} %refs_0_.1) | copy-start | bytes 1179652
  2.0 60.1 %copy-start.3 = (f32[128,8,8]{0,2,1:T(8,128)S(1)}, f32[128,8,8]{0,2,1:T(8,128)}, u32[]{:S(2)}) copy-start(f32[128,8,8]{0,2,1:T(8,128)} %param.7) | copy-start | bytes 98308
  2.8 15.0 %collective-permute-start.7 = (bf16[2,3,16,1024]{3,2,1,0:T(8,128)(2,1)S(1)}, bf16[2,3,16,1024]{3,2,1,0:T(8,128)(2,1)S(1)}, u32[]{:S(2)}, u32[]{:S(2)}) collective-permute-start(bf16[2,3,16,1024]{3,2,1,0:T(8,128)(2,1)S(1)} %get-tuple-element.18), channel_id=1, source_target_pairs={{0,8},{4,12},{8,16},{12,20},{16,24},{20,28},{24,0},{28,4},{1,9},{5... | collective-permute-start | bytes 589832 | tf_op jit(solution)/shard_map/acts_z1/ppermute | solution.py:246
  4.4 18.0 %collective-permute-start.8 = (bf16[2,3,16,1024]{3,2,1,0:T(8,128)(2,1)S(1)}, bf16[2,3,16,1024]{3,2,1,0:T(8,128)(2,1)S(1)}, u32[]{:S(2)}, u32[]{:S(2)}) collective-permute-start(bf16[2,3,16,1024]{3,2,1,0:T(8,128)(2,1)S(1)} %get-tuple-element.19), channel_id=1, source_target_pairs={{0,16},{4,20},{8,24},{12,28},{16,0},{20,4},{24,8},{28,12},{1,17},{... | collective-permute-start | bytes 589832 | tf_op jit(solution)/shard_map/acts_z2/ppermute | solution.py:246
  5.5 25.9 %collective-permute-start.9 = (bf16[2,3,16,1024]{3,2,1,0:T(8,128)(2,1)S(1)}, bf16[2,3,16,1024]{3,2,1,0:T(8,128)(2,1)S(1)}, u32[]{:S(2)}, u32[]{:S(2)}) collective-permute-start(bf16[2,3,16,1024]{3,2,1,0:T(8,128)(2,1)S(1)} %get-tuple-element.20), channel_id=1, source_target_pairs={{0,24},{4,28},{8,0},{12,4},{16,8},{20,12},{24,16},{28,20},{1,25},{... | collective-permute-start | bytes 589832 | tf_op jit(solution)/shard_map/acts_z3/ppermute | solution.py:246
  7.5 32.2 %collective-permute-start.3 = (bf16[3,64,1024]{2,1,0:T(8,128)(2,1)S(1)}, bf16[3,64,1024]{2,1,0:T(8,128)(2,1)S(1)}, u32[]{:S(2)}, u32[]{:S(2)}) collective-permute-start(bf16[3,64,1024]{2,1,0:T(8,128)(2,1)S(1)} %copy-done.1), channel_id=1, source_target_pairs={{0,4},{4,0},{8,12},{12,8},{16,20},{20,16},{24,28},{28,24},{1,5},{5... | collective-permute-start | bytes 1179656 | tf_op jit(solution)/shard_map/grads_y0/ppermute | solution.py:242
  9.0 29.1 %collective-permute-start = (bf16[3,64,1024]{2,1,0:T(8,128)(2,1)S(1)}, bf16[3,64,1024]{2,1,0:T(8,128)(2,1)S(1)}, u32[]{:S(2)}, u32[]{:S(2)}) collective-permute-start(bf16[3,64,1024]{2,1,0:T(8,128)(2,1)S(1)} %copy-done.1), channel_id=1, source_target_pairs={{0,8},{4,12},{8,16},{12,20},{16,24},{20,28},{24,0},{28,4},{1,9},{5... | collective-permute-start | bytes 1179656 | tf_op jit(solution)/shard_map/grads_z1/ppermute | solution.py:246
  31.5 12.0 %collective-permute-start.10 = (bf16[4,3,16,1024]{3,2,1,0:T(8,128)(2,1)S(1)}, bf16[4,3,16,1024]{3,2,1,0:T(8,128)(2,1)S(1)}, u32[]{:S(2)}, u32[]{:S(2)}) collective-permute-start(bf16[4,3,16,1024]{3,2,1,0:T(8,128)(2,1)S(1)} %get-tuple-element.22), channel_id=1, source_target_pairs={{0,4},{4,0},{8,12},{12,8},{16,20},{20,16},{24,28},{28,24},{1,5},{5... | collective-permute-start | bytes 1179656 | tf_op jit(solution)/shard_map/acts_y/ppermute | solution.py:242
  33.1 19.2 %collective-permute-start.5 = (bf16[3,64,1024]{2,1,0:T(8,128)(2,1)S(1)}, bf16[3,64,1024]{2,1,0:T(8,128)(2,1)S(1)}, u32[]{:S(2)}, u32[]{:S(2)}) collective-permute-start(bf16[3,64,1024]{2,1,0:T(8,128)(2,1)S(1)} %copy-done.1), channel_id=1, source_target_pairs={{0,24},{4,28},{8,0},{12,4},{16,8},{20,12},{24,16},{28,20},{1,25},{... | collective-permute-start | bytes 1179656 | tf_op jit(solution)/shard_map/grads_z3/ppermute | solution.py:246
  33.1 19.7 %collective-permute-start.13 = (bf16[4,3,16,1024]{3,2,1,0:T(8,128)(2,1)S(1)}, bf16[4,3,16,1024]{3,2,1,0:T(8,128)(2,1)S(1)}, u32[]{:S(2)}, u32[]{:S(2)}) collective-permute-start(bf16[4,3,16,1024]{3,2,1,0:T(8,128)(2,1)S(1)} %get-tuple-element.21.refs_0_), channel_id=1, source_target_pairs={{0,2},{1,3},{2,0},{3,1},{4,6},{5,7},{6,4},{7,5},{8,10},{9,11},{10,... | collective-permute-start | bytes 1179656 | tf_op jit(solution)/shard_map/acts_out2/ppermute | solution.py:252
  38.1 14.7 %collective-permute-start.4 = (bf16[3,64,1024]{2,1,0:T(8,128)(2,1)S(1)}, bf16[3,64,1024]{2,1,0:T(8,128)(2,1)S(1)}, u32[]{:S(2)}, u32[]{:S(2)}) collective-permute-start(bf16[3,64,1024]{2,1,0:T(8,128)(2,1)S(1)} %collective-permute-done.refs_2_), channel_id=1, source_target_pairs={{0,4},{4,0},{8,12},{12,8},{16,20},{20,16},{24,28},{28,24},{1,5},{5... | collective-permute-start | bytes 1179656 | tf_op jit(solution)/shard_map/grads_y1/ppermute | solution.py:242
  39.7 13.6 %collective-permute-start.1 = (bf16[3,64,1024]{2,1,0:T(8,128)(2,1)S(1)}, bf16[3,64,1024]{2,1,0:T(8,128)(2,1)S(1)}, u32[]{:S(2)}, u32[]{:S(2)}) collective-permute-start(bf16[3,64,1024]{2,1,0:T(8,128)(2,1)S(1)} %collective-permute-done.refs_2_), channel_id=1, source_target_pairs={{0,8},{4,12},{8,16},{12,20},{16,24},{20,28},{24,0},{28,4},{1,9},{5... | collective-permute-start | bytes 1179656 | tf_op jit(solution)/shard_map/grads_z2/ppermute | solution.py:246
  43.5 9.8 %collective-permute-start.14 = (bf16[4,3,16,1024]{3,2,1,0:T(8,128)(2,1)S(1)}, bf16[4,3,16,1024]{3,2,1,0:T(8,128)(2,1)S(1)}, u32[]{:S(2)}, u32[]{:S(2)}) collective-permute-start(bf16[4,3,16,1024]{3,2,1,0:T(8,128)(2,1)S(1)} %collective-permute-done.10.refs_1_), channel_id=1, source_target_pairs={{0,2},{1,3},{2,0},{3,1},{4,6},{5,7},{6,4},{7,5},{8,10},{9,11},{10,... | collective-permute-start | bytes 1179656 | tf_op jit(solution)/shard_map/acts_out2/ppermute | solution.py:252
  52.2 9.7 %collective-permute-start.6 = (bf16[3,64,1024]{2,1,0:T(8,128)(2,1)S(1)}, bf16[3,64,1024]{2,1,0:T(8,128)(2,1)S(1)}, u32[]{:S(2)}, u32[]{:S(2)}) collective-permute-start(bf16[3,64,1024]{2,1,0:T(8,128)(2,1)S(1)} %collective-permute-done.5.refs_4_), channel_id=1, source_target_pairs={{0,4},{4,0},{8,12},{12,8},{16,20},{20,16},{24,28},{28,24},{1,5},{5... | collective-permute-start | bytes 1179656 | tf_op jit(solution)/shard_map/grads_y3/ppermute | solution.py:242
  52.8 13.7 %collective-permute-start.11 = (bf16[4,3,16,1024]{3,2,1,0:T(8,128)(2,1)S(1)}, bf16[4,3,16,1024]{3,2,1,0:T(8,128)(2,1)S(1)}, u32[]{:S(2)}, u32[]{:S(2)}) collective-permute-start(bf16[4,3,16,1024]{3,2,1,0:T(8,128)(2,1)S(1)} %get-tuple-element.21.refs_0_), channel_id=1, source_target_pairs={{0,1},{1,0},{2,3},{3,2},{4,5},{5,4},{6,7},{7,6},{8,9},{9,8},{10,11... | collective-permute-start | bytes 1179656 | tf_op jit(solution)/shard_map/acts_out1/ppermute | solution.py:252
  52.8 13.7 %collective-permute-start.12 = (bf16[4,3,16,1024]{3,2,1,0:T(8,128)(2,1)S(1)}, bf16[4,3,16,1024]{3,2,1,0:T(8,128)(2,1)S(1)}, u32[]{:S(2)}, u32[]{:S(2)}) collective-permute-start(bf16[4,3,16,1024]{3,2,1,0:T(8,128)(2,1)S(1)} %collective-permute-done.10.refs_1_), channel_id=1, source_target_pairs={{0,1},{1,0},{2,3},{3,2},{4,5},{5,4},{6,7},{7,6},{8,9},{9,8},{10,11... | collective-permute-start | bytes 1179656 | tf_op jit(solution)/shard_map/acts_out1/ppermute | solution.py:252
  53.3 13.2 %collective-permute-start.15 = (bf16[4,3,16,1024]{3,2,1,0:T(8,128)(2,1)S(1)}, bf16[4,3,16,1024]{3,2,1,0:T(8,128)(2,1)S(1)}, u32[]{:S(2)}, u32[]{:S(2)}) collective-permute-start(bf16[4,3,16,1024]{3,2,1,0:T(8,128)(2,1)S(1)} %collective-permute-done.13.refs_4_), channel_id=1, source_target_pairs={{0,1},{1,0},{2,3},{3,2},{4,5},{5,4},{6,7},{7,6},{8,9},{9,8},{10,11... | collective-permute-start | bytes 1179656 | tf_op jit(solution)/shard_map/acts_out3/ppermute | solution.py:252
  53.4 13.2 %collective-permute-start.16 = (bf16[4,3,16,1024]{3,2,1,0:T(8,128)(2,1)S(1)}, bf16[4,3,16,1024]{3,2,1,0:T(8,128)(2,1)S(1)}, u32[]{:S(2)}, u32[]{:S(2)}) collective-permute-start(bf16[4,3,16,1024]{3,2,1,0:T(8,128)(2,1)S(1)} %collective-permute-done.14.refs_5_), channel_id=1, source_target_pairs={{0,1},{1,0},{2,3},{3,2},{4,5},{5,4},{6,7},{7,6},{8,9},{9,8},{10,11... | collective-permute-start | bytes 1179656 | tf_op jit(solution)/shard_map/acts_out3/ppermute | solution.py:252
  61.9 7.8 %collective-permute-start.2 = (bf16[3,64,1024]{2,1,0:T(8,128)(2,1)S(1)}, bf16[3,64,1024]{2,1,0:T(8,128)(2,1)S(1)}, u32[]{:S(2)}, u32[]{:S(2)}) collective-permute-start(bf16[3,64,1024]{2,1,0:T(8,128)(2,1)S(1)} %collective-permute-done.1.first), channel_id=1, source_target_pairs={{0,4},{4,0},{8,12},{12,8},{16,20},{20,16},{24,28},{28,24},{1,5},{5... | collective-permute-start | bytes 1179656 | tf_op jit(solution)/shard_map/grads_y2/ppermute | solution.py:242

commit v3 on v2

--- a/solution.py
+++ b/solution.py
@@ -61,12 +61,11 @@
     spread_one(True, g_ref, g_high, g_low)
 
 
-def spread(act_basis, grad_basis):
-    flat, shapes = [], []
-    for basis in (act_basis, grad_basis):
-        blocks = basis.shape[0]
+def spread(*flat):
+    shapes = []
+    for basis in flat:
+        blocks = basis.shape[1]
         span = min(256, blocks * 8)
-        flat.append(jnp.transpose(basis, (1, 2, 0)).reshape(64, blocks))
         shapes += [jax.ShapeDtypeStruct((blocks * 8 // span, span, span), BF)] * 2
     out = pl.pallas_call(
         spread_kernel,
@@ -110,7 +109,7 @@
         scratch_shapes=[pltpu.SemaphoreType.DMA((n,))],
         compiler_params=pltpu.CompilerParams(vmem_limit_bytes=limit(*[shape] * (n // 2))),
         name="cut",
-    )(where, acts)
+    )(where, pltpu.with_memory_space_constraint(acts, pltpu.HBM))
 
 
 def part_kernel(*refs):
@@ -132,30 +131,30 @@
     )(*pieces)
 
 
-def turn_acts_kernel(order, m, where_ref, *refs):
+def turn_acts_kernel(place_of, m, where_ref, *refs):
     pieces, (high, low, out_ref) = refs[: 2 * m], refs[2 * m :]
     half, seqs, quarter, width = pieces[0].shape
-    rows = quarter * m
     groups, span, _ = high.shape
-    for j in range(m):
-        place = pl.multiple_of((where_ref[0] ^ j) * quarter, quarter)
-        for other in range(2):
+    q, z, y = where_ref[0], where_ref[1], where_ref[2]
+    for other in range(2):
+        starts = [place_of(z, y, lax.rem(z - k + half, half), y ^ other) * m for k in range(half)]
+        for j in range(m):
             piece = pieces[2 * j + other]
             for g in range(groups):
                 columns = pl.ds(g * span, span)
                 block = piece[:, :, :, columns].reshape(half * seqs * quarter, span)
                 turned = dot(block, high[g], ((1,), (0,))) + dot(block, low[g], ((1,), (0,)))
                 turned = turned.astype(BF).reshape(half, seqs, quarter, span)
-                for at, k in enumerate(order):
-                    to = pl.ds(place + (2 * at + other) * rows, quarter)
-                    out_ref[:, to, columns] = turned[k]
-
-
-def turn_acts(where, pieces, parts, order, m):
+                for k in range(half):
+                    start = pl.multiple_of((starts[k] + (q ^ j)) * quarter, quarter)
+                    out_ref[:, pl.ds(start, quarter), columns] = turned[k]
+
+
+def turn_acts(where, pieces, parts, place_of, m):
     half, seqs, quarter, width = pieces[0].shape
     shape = jax.ShapeDtypeStruct((seqs, 2 * half * m * quarter, width), BF)
     return pl.pallas_call(
-        functools.partial(turn_acts_kernel, order, m),
+        functools.partial(turn_acts_kernel, place_of, m),
         in_specs=[SCALARS] + [VECTORS] * (2 * m + 2),
         out_specs=VECTORS,
         out_shape=shape,
@@ -195,86 +194,148 @@
     )(*pieces, *parts)
 
 
-def multiply_kernel(scale, first, second, high, low, grads, acts, out_ref):
-    total = None
+def multiply_kernel(scale, first, second, high, low, grads, acts, *refs):
+    *before, out_ref = refs
+    total = before[0][...] if before else None
     for s in range(acts.shape[0]):
         late = turn_pair(high[0], low[0], first[s], second[s])
         corr = dot(jnp.concatenate([grads[s], late], 1), acts[s], ((1,), (0,)))
-        total = corr * corr if total is None else total + corr * corr
-    out_ref[...] = total * scale
-
-
-def multiply(last, parts, grads, acts):
-    seqs, rows, outs = last[0].shape
-    _, length, width = acts.shape
+        square = corr * corr * scale
+        total = square if total is None else total + square
+    out_ref[...] = total
+
+
+def multiply(begin, last, parts, grads, acts, before=()):
+    count, rows, outs = last[1].shape
+    seqs, length, width = acts.shape
     tile = parts[0].shape[1]
     shape = jax.ShapeDtypeStruct((outs, width), F32)
+    at = begin // count
+    assert at * count == begin
+    strip = pl.BlockSpec((tile, width), lambda i: (i, 0))
     return pl.pallas_call(
         functools.partial(multiply_kernel, 1.0 / length),
         grid=(outs // tile,),
-        in_specs=[pl.BlockSpec((seqs, rows, tile), lambda i: (0, 0, i))] * 2
+        in_specs=[
+            pl.BlockSpec((count, rows, tile), lambda i: (0, 0, i)),
+            pl.BlockSpec((count, rows, tile), lambda i: (0, 0, i)),
+        ]
         + [pl.BlockSpec((1, tile, tile), lambda i: (i, 0, 0))] * 2
         + [
-            pl.BlockSpec((seqs, tile, grads.shape[2]), lambda i: (0, i, 0)),
-            pl.BlockSpec((seqs, length, width), lambda i: (0, 0, 0)),
-        ],
-        out_specs=pl.BlockSpec((tile, width), lambda i: (i, 0)),
+            pl.BlockSpec((count, tile, grads.shape[2]), lambda i: (at, i, 0)),
+            pl.BlockSpec((count, length, width), lambda i: (at, 0, 0)),
+        ]
+        + [strip] * len(before),
+        out_specs=strip,
         out_shape=shape,
         compiler_params=pltpu.CompilerParams(
             vmem_limit_bytes=limit(acts, jax.ShapeDtypeStruct((seqs, tile, length), BF))
         ),
         name="multiply",
-    )(*last, *parts, grads, acts)
+    )(*last, *parts, grads, acts, *before)
 
 
 def after(value, *earlier):
     return lax.optimization_barrier((value, *earlier))[0]
 
 
+CAME = ("az1", "az2", "az3")
+TIES = {
+    "u2": CAME,
+    "d2": CAME,
+    "u3": ("ay", "as2"),
+    "d3": ("ay", "spread"),
+    "u": ("ag2", "as1"),
+    "d": ("tg",),
+}
+
+
 def shards(acts, grads, act_basis, grad_basis):
     n, m = lax.axis_size("tok"), lax.axis_size("out")
-    half = n // 2
+    half, seqs = n // 2, acts.shape[0]
     t, q = lax.axis_index("tok"), lax.axis_index("out")
     where = jnp.stack([q, t // 2, t % 2]).astype(jnp.int32)
-
-    def over_y(name, value):
-        with jax.named_scope(name):
-            return lax.ppermute(value, "tok", [(i, i ^ 1) for i in range(n)])
-
-    def over_z(name, value, shift):
-        with jax.named_scope(name):
-            return lax.ppermute(
-                value, "tok", [(i, (i // 2 + shift) % half * 2 + i % 2) for i in range(n)]
-            )
-
-    def over_out(name, value, bit):
-        with jax.named_scope(name):
-            return lax.ppermute(value, "out", [(i, i ^ bit) for i in range(m)])
-
-    act_parts, grad_parts = spread(act_basis, grad_basis)
-
-    cuts = cut(acts, where, n, m)
-    came = [cuts[0]] + [over_z(f"acts_z{k}", cuts[k], k) for k in range(1, half)]
-    stay, go = part(came)
-    held = {0: [stay, over_y("acts_y", go)]}
-    bit = m // 2
-    while bit:
-        for j, pair in list(held.items()):
-            held[j | bit] = [over_out(f"acts_out{j | bit}", v, bit) for v in pair]
-        bit //= 2
-
-    ring = {0: grads}
-    for k in range(1, (half - 1) // 2 + 1):
-        ring[half - k] = over_z(f"grads_z{half - k}", ring[(half - k + 1) % half], -1)
-    for k in range(1, half // 2 + 1):
-        ring[k] = over_z(f"grads_z{k}", ring[k - 1], 1)
-    order = [k for k in range(half) if k != half // 2] + [half // 2]
-    pairs = [[ring[k], over_y(f"grads_y{k}", ring[k])] for k in order]
-
-    pieces = [v for j in range(m) for v in held[j]]
-    turned_acts = turn_acts(where, pieces, act_parts, order, m)
-    turned_grads = turn_grads([v for pair in pairs[:-1] for v in pair], grad_parts)
-    return multiply(pairs[-1], grad_parts, turned_grads, turned_acts)
+    ops, done = {}, {}
+
+    def get(name):
+        if name not in done:
+            earlier = [get(e) for e in TIES.get(name, ()) if e in ops]
+            done[name] = ops[name](lambda v: after(v, *earlier) if earlier else v)
+        return done[name]
+
+    def send(name, source, axis, perm):
+        def run(tie):
+            value = tie(source())
+            with jax.named_scope(name):
+                return lax.ppermute(value, axis, perm)
+
+        ops[name] = run
+
+    def over_y(name, source):
+        send(name, source, "tok", [(i, i ^ 1) for i in range(n)])
+
+    def over_z(name, source, shift):
+        send(name, source, "tok", [(i, (i // 2 + shift) % half * 2 + i % 2) for i in range(n)])
+
+    def over_out(name, source, bit):
+        send(name, source, "out", [(i, i ^ bit) for i in range(m)])
+
+    flat = [jnp.transpose(b, (1, 2, 0)).reshape(64, -1) for b in (act_basis, grad_basis)]
+    ops["spread"] = lambda tie: spread(tie(flat[0]), flat[1])
+    ops["cut"] = lambda tie: cut(tie(acts), where, n, m)
+
+    for k in range(1, half):
+        over_z(f"az{k}", lambda k=k: get("cut")[k], k)
+    ops["part"] = lambda tie: part([get("cut")[0]] + [get(f"az{k}") for k in range(1, half)])
+    over_y("ay", lambda: get("part")[1])
+    ops["as0"] = lambda tie: get("part")[0]
+    ops["ag0"] = lambda tie: get("ay")
+    for letter in "sg":
+        bit = m // 2
+        held = [0]
+        while bit:
+            for j in list(held):
+                held.append(j | bit)
+                over_out(f"a{letter}{j | bit}", lambda x=f"a{letter}{j}": get(x), bit)
+            bit //= 2
+
+    ring = [2 * z for z in range(half)] + [2 * z + 1 for z in reversed(range(half))]
+
+    def round_ring(name, source, step):
+        perm = [(ring[i], ring[(i + step) % n]) for i in range(n)]
+        send(name, source, "tok", sorted(perm))
+
+    first = seqs - 1
+    ops["u0"] = ops["d0"] = lambda tie: grads
+    for i in range(1, half):
+        for way, step in (("u", 1), ("d", -1)):
+            round_ring(f"{way}{i}", lambda way=way, i=i: get(f"{way}{i - 1}"), step)
+    round_ring("u", lambda: get(f"u{half - 1}")[:first], 1)
+    round_ring("d", lambda: get(f"d{half - 1}")[first:], -1)
+
+    names = ["u0"] + [f"{way}{i}" for i in range(1, half) for way in "ud"]
+
+    def place_of(z, y, from_z, from_y):
+        mine = jnp.where(y == 0, z, n - 1 - z)
+        other = jnp.where(from_y == 0, from_z, n - 1 - from_z)
+        ahead = lax.rem(mine - other + n, n)
+        return jnp.where(
+            ahead == 0, 0, jnp.where(ahead <= half, 2 * ahead - 1, 2 * (n - ahead))
+        )
+
+    ops["ta"] = lambda tie: turn_acts(
+        where,
+        [get(f"a{letter}{j}") for j in range(m) for letter in "sg"],
+        get("spread")[0],
+        place_of,
+        m,
+    )
+    ops["tg"] = lambda tie: turn_grads([get(x) for x in names[:-1]], get("spread")[1])
+    late = get(names[-1])
+    total = ()
+    for last, part_of, lo in ((get("u"), late[:first], 0), (get("d"), late[first:], first)):
+        total = (multiply(lo, [part_of, last], get("spread")[1], get("tg"), get("ta"), total),)
+    return total[0]
 
 
 def solution(mesh):

time: 76.7 us -> 71.2 us (0.928)
  the two profiles are of different devices: /device:TPU:8 before, /device:TPU:0 now
where the time goes in v3:
time: 71.2 us; the launch traced here: 70.6 us
  waiting for transfers between devices  28.7 us (40%)
  starting transfers between devices  25 us (35%)
  Pallas kernels  16.6 us (23%)
    ppermute x18, waiting for transfers between devices, run(): return lax.ppermute(value, axis, perm)  28.7 us
    ppermute x18, starting transfers between devices, run(): return lax.ppermute(value, axis, perm)  25 us
    pallas_call x2, Pallas kernels, multiply(): pl.pallas_call(functools.partial(multiply_kernel, 1.0 / length), grid=(ou...  7.75 us
    pallas_call x1, Pallas kernels, turn_grads(): pl.pallas_call(turn_grads_kernel, in_specs=[VECTORS] * (len(pieces) + 2),...  2.62 us
    pallas_call x1, Pallas kernels, turn_acts(): pl.pallas_call(functools.partial(turn_acts_kernel, place_of, m), in_specs...  2.54 us
    pallas_call x1, Pallas kernels, cut(): pl.pallas_call(functools.partial(cut_kernel, n // 2), in_specs=[SCALARS,...  1.85 us
    pallas_call x1, Pallas kernels, spread(): pl.pallas_call(spread_kernel, out_shape=tuple(shapes), compiler_params=pl...  1.8 us
  transfers between devices with their start and end apart: 18, of which 7 were waited for; matrix products, arithmetic and copies ran while one was open for 0% of the time, Pallas kernels for 18%

profile of v3, /device:TPU:0, one launch (start us, length us, event | category | flops | bytes accessed | tf_op | source)
XLA Modules:
  0.0 70.6 jit_solution(14954830111371668932)
XLA Ops:
  0.0 0.0 copy-start
  0.0 3.1 %collective-permute-start.7 = (bf16[3,64,1024]{2,1,0:T(8,128)(2,1)}, bf16[3,64,1024]{2,1,0:T(8,128)(2,1)S(1)}, u32[]{:S(2)}, u32[]{:S(2)}) collective-permute-start(bf16[3,64,1024]{2,1,0:T(8,128)(2,1)} %refs_0_.1), channel_id=1, source_target_pairs={{0,8},{4,0},{8,16},{12,4},{16,24},{20,12},{24,28},{28,20},{1,9},{5... | collective-permute-start | bytes 1179656 | tf_op jit(solution)/shard_map/u1/ppermute | solution.py:270
  3.1 0.1 pad_add_fusion.where_ref
  3.2 1.8 %cut.1 = (bf16[2,3,16,1024]{3,2,1,0:T(8,128)(2,1)S(1)}, bf16[2,3,16,1024]{3,2,1,0:T(8,128)(2,1)S(1)}, bf16[2,3,16,1024]{3,2,1,0:T(8,128)(2,1)S(1)}, bf16[2,3,16,1024]{3,2,1,0:T(8,128)(2,1)S(1)}) custom-call(s32[3]{0:T(128)S(1)} %pad_add_fusion.where_ref, bf16[3,64,8192]{2,1,0:T(8,128)(2,1)} %acts_ref.1), custom_call_target="tpu_custom_call" | custom-call | tf_op jit(solution)/shard_map/cut/pallas_call | solution.py:104
  5.0 1.6 %collective-permute-start.1 = (bf16[2,3,16,1024]{3,2,1,0:T(8,128)(2,1)S(1)}, bf16[2,3,16,1024]{3,2,1,0:T(8,128)(2,1)S(1)}, u32[]{:S(2)}, u32[]{:S(2)}) collective-permute-start(bf16[2,3,16,1024]{3,2,1,0:T(8,128)(2,1)S(1)} %get-tuple-element.21), channel_id=1, source_target_pairs={{0,8},{4,12},{8,16},{12,20},{16,24},{20,28},{24,0},{28,4},{1,9},{5... | collective-permute-start | bytes 589832 | tf_op jit(solution)/shard_map/az1/ppermute | solution.py:270
  6.6 2.5 %collective-permute-start.2 = (bf16[2,3,16,1024]{3,2,1,0:T(8,128)(2,1)S(1)}, bf16[2,3,16,1024]{3,2,1,0:T(8,128)(2,1)S(1)}, u32[]{:S(2)}, u32[]{:S(2)}) collective-permute-start(bf16[2,3,16,1024]{3,2,1,0:T(8,128)(2,1)S(1)} %get-tuple-element.22), channel_id=1, source_target_pairs={{0,16},{4,20},{8,24},{12,28},{16,0},{20,4},{24,8},{28,12},{1,17},{... | collective-permute-start | bytes 589832 | tf_op jit(solution)/shard_map/az2/ppermute | solution.py:270
  9.2 1.4 %collective-permute-start.3 = (bf16[2,3,16,1024]{3,2,1,0:T(8,128)(2,1)S(1)}, bf16[2,3,16,1024]{3,2,1,0:T(8,128)(2,1)S(1)}, u32[]{:S(2)}, u32[]{:S(2)}) collective-permute-start(bf16[2,3,16,1024]{3,2,1,0:T(8,128)(2,1)S(1)} %get-tuple-element.23), channel_id=1, source_target_pairs={{0,24},{4,28},{8,0},{12,4},{16,8},{20,12},{24,16},{28,20},{1,25},{... | collective-permute-start | bytes 589832 | tf_op jit(solution)/shard_map/az3/ppermute | solution.py:270
  10.6 0.0 copy-done
  10.6 0.4 collective-permute-start
  11.0 6.1 %collective-permute-done.1.refs_1_ = bf16[2,3,16,1024]{3,2,1,0:T(8,128)(2,1)S(1)} collective-permute-done((bf16[2,3,16,1024]{3,2,1,0:T(8,128)(2,1)S(1)}, bf16[2,3,16,1024]{3,2,1,0:T(8,128)(2,1)S(1)}, u32[]{:S(2)}, u32[]{:S(2)}) %collective-permute-start.1) | collective-permute-done | bytes 196640 | tf_op jit(solution)/shard_map/az1/ppermute | solution.py:270
  17.0 4.8 %collective-permute-done.2.refs_2_ = bf16[2,3,16,1024]{3,2,1,0:T(8,128)(2,1)S(1)} collective-permute-done((bf16[2,3,16,1024]{3,2,1,0:T(8,128)(2,1)S(1)}, bf16[2,3,16,1024]{3,2,1,0:T(8,128)(2,1)S(1)}, u32[]{:S(2)}, u32[]{:S(2)}) %collective-permute-start.2) | collective-permute-done | bytes 196640 | tf_op jit(solution)/shard_map/az2/ppermute | solution.py:270
  21.8 2.6 %collective-permute-done.3.refs_3_ = bf16[2,3,16,1024]{3,2,1,0:T(8,128)(2,1)S(1)} collective-permute-done((bf16[2,3,16,1024]{3,2,1,0:T(8,128)(2,1)S(1)}, bf16[2,3,16,1024]{3,2,1,0:T(8,128)(2,1)S(1)}, u32[]{:S(2)}, u32[]{:S(2)}) %collective-permute-start.3) | collective-permute-done | bytes 196640 | tf_op jit(solution)/shard_map/az3/ppermute | solution.py:270
  24.4 0.1 part.1
  24.4 4.6 %collective-permute-start.5 = (bf16[4,3,16,1024]{3,2,1,0:T(8,128)(2,1)S(1)}, bf16[4,3,16,1024]{3,2,1,0:T(8,128)(2,1)S(1)}, u32[]{:S(2)}, u32[]{:S(2)}) collective-permute-start(bf16[4,3,16,1024]{3,2,1,0:T(8,128)(2,1)S(1)} %get-tuple-element.26), channel_id=1, source_target_pairs={{0,4},{4,0},{8,12},{12,8},{16,20},{20,16},{24,28},{28,24},{1,5},{5... | collective-permute-start | bytes 1179656 | tf_op jit(solution)/shard_map/ay/ppermute | solution.py:270
  29.0 1.5 %collective-permute-start.9 = (bf16[4,3,16,1024]{3,2,1,0:T(8,128)(2,1)S(1)}, bf16[4,3,16,1024]{3,2,1,0:T(8,128)(2,1)S(1)}, u32[]{:S(2)}, u32[]{:S(2)}) collective-permute-start(bf16[4,3,16,1024]{3,2,1,0:T(8,128)(2,1)S(1)} %get-tuple-element.33.refs_0_), channel_id=1, source_target_pairs={{0,2},{1,3},{2,0},{3,1},{4,6},{5,7},{6,4},{7,5},{8,10},{9,11},{10,... | collective-permute-start | bytes 1179656 | tf_op jit(solution)/shard_map/as2/ppermute | solution.py:270
  30.5 0.0 collective-permute-done.7.refs_1_
  30.5 3.6 %collective-permute-start.8 = (bf16[3,64,1024]{2,1,0:T(8,128)(2,1)S(1)}, bf16[3,64,1024]{2,1,0:T(8,128)(2,1)S(1)}, u32[]{:S(2)}, u32[]{:S(2)}) collective-permute-start(bf16[3,64,1024]{2,1,0:T(8,128)(2,1)S(1)} %collective-permute-done.7.refs_1_), channel_id=1, source_target_pairs={{0,8},{4,0},{8,16},{12,4},{16,24},{20,12},{24,28},{28,20},{1,9},{5... | collective-permute-start | bytes 1179656 | tf_op jit(solution)/shard_map/u2/ppermute | solution.py:270
  34.1 0.0 collective-permute-done.refs_2_
  34.1 0.0 collective-permute-start.4
  34.1 4.9 %collective-permute-done.5.refs_1_ = bf16[4,3,16,1024]{3,2,1,0:T(8,128)(2,1)S(1)} collective-permute-done((bf16[4,3,16,1024]{3,2,1,0:T(8,128)(2,1)S(1)}, bf16[4,3,16,1024]{3,2,1,0:T(8,128)(2,1)S(1)}, u32[]{:S(2)}, u32[]{:S(2)}) %collective-permute-start.5) | collective-permute-done | bytes 393248 | tf_op jit(solution)/shard_map/ay/ppermute | solution.py:270
  39.1 1.5 %collective-permute-start.14 = (bf16[4,3,16,1024]{3,2,1,0:T(8,128)(2,1)S(1)}, bf16[4,3,16,1024]{3,2,1,0:T(8,128)(2,1)S(1)}, u32[]{:S(2)}, u32[]{:S(2)}) collective-permute-start(bf16[4,3,16,1024]{3,2,1,0:T(8,128)(2,1)S(1)} %collective-permute-done.5.refs_1_), channel_id=1, source_target_pairs={{0,2},{1,3},{2,0},{3,1},{4,6},{5,7},{6,4},{7,5},{8,10},{9,11},{10,... | collective-permute-start | bytes 1179656 | tf_op jit(solution)/shard_map/ag2/ppermute | solution.py:270
  40.5 0.0 collective-permute-done.9.refs_4_
  40.5 4.2 %collective-permute-done.8.refs_3_ = bf16[3,64,1024]{2,1,0:T(8,128)(2,1)S(1)} collective-permute-done((bf16[3,64,1024]{2,1,0:T(8,128)(2,1)S(1)}, bf16[3,64,1024]{2,1,0:T(8,128)(2,1)S(1)}, u32[]{:S(2)}, u32[]{:S(2)}) %collective-permute-start.8) | collective-permute-done | bytes 393248 | tf_op jit(solution)/shard_map/u2/ppermute | solution.py:270
  44.7 0.0 collective-permute-start.10
  44.7 0.0 collective-permute-start.12
  44.7 0.0 copy-done.2
  44.7 0.0 copy-done.1
  44.7 1.8 %spread.1 = (bf16[4,256,256]{2,1,0:T(8,128)(2,1)S(1)}, bf16[4,256,256]{2,1,0:T(8,128)(2,1)S(1)}, bf16[4,256,256]{2,1,0:T(8,128)(2,1)S(1)}, bf16[4,256,256]{2,1,0:T(8,128)(2,1)S(1)}) custom-call(f32[64,128]{1,0:T(8,128)S(1)} %bitcast.9, f32[64,128]{1,0:T(8,128)S(1)} %bitcast.10), custom_call_target="tpu_custom_call" | custom-call | tf_op jit(solution)/shard_map/spread/pallas_call | solution.py:70
  46.5 0.0 collective-permute-done.4.refs_4_
  46.5 2.1 %collective-permute-start.6 = (bf16[3,64,1024]{2,1,0:T(8,128)(2,1)S(1)}, bf16[3,64,1024]{2,1,0:T(8,128)(2,1)S(1)}, u32[]{:S(2)}, u32[]{:S(2)}) collective-permute-start(bf16[3,64,1024]{2,1,0:T(8,128)(2,1)S(1)} %collective-permute-done.4.refs_4_), channel_id=1, source_target_pairs={{0,4},{4,12},{8,0},{12,20},{16,8},{20,28},{24,16},{28,24},{1,5},{5... | collective-permute-start | bytes 1179656 | tf_op jit(solution)/shard_map/d3/ppermute | solution.py:270
  48.6 0.2 collective-permute-start.13
  48.8 0.0 collective-permute-done.14.refs_5_
  48.8 0.3 collective-permute-start.15
  49.1 3.8 %collective-permute-done.10.refs_5_ = bf16[3,64,1024]{2,1,0:T(8,128)(2,1)S(1)} collective-permute-done((bf16[3,64,1024]{2,1,0:T(8,128)(2,1)S(1)}, bf16[3,64,1024]{2,1,0:T(8,128)(2,1)S(1)}, u32[]{:S(2)}, u32[]{:S(2)}) %collective-permute-start.10) | collective-permute-done | bytes 393248 | tf_op jit(solution)/shard_map/u3/ppermute | solution.py:270
  53.0 0.0 collective-permute-start.16
  53.0 0.0 collective-permute-done.12.refs_2_
  53.0 0.1 collective-permute-start.17
  53.1 2.6 %turn_grads.1.grads = bf16[3,1024,384]{2,1,0:T(8,128)(2,1)S(1)} custom-call(bf16[3,64,1024]{2,1,0:T(8,128)(2,1)S(1)} %copy-done, bf16[3,64,1024]{2,1,0:T(8,128)(2,1)S(1)} %collective-permute-done.7.refs_1_, bf16[3,64,1024]{2,1,0:T(8,128)(2,1)S(1)} %collective-permute-done.refs_2_, bf16[3,64,1024]{2,1,0:T(8,128)(2,1)S(1)} %collective-permute-done.8.refs_3_, ...), custom_call_target="tpu_custom_call" | custom-call | tf_op jit(solution)/shard_map/turn_grads/pallas_call | solution.py:187
  55.7 2.4 %collective-permute-done.6 = bf16[3,64,1024]{2,1,0:T(8,128)(2,1)S(1)} collective-permute-done((bf16[3,64,1024]{2,1,0:T(8,128)(2,1)S(1)}, bf16[3,64,1024]{2,1,0:T(8,128)(2,1)S(1)}, u32[]{:S(2)}, u32[]{:S(2)}) %collective-permute-start.6) | collective-permute-done | bytes 393248 | tf_op jit(solution)/shard_map/d3/ppermute | solution.py:270
  58.1 2.1 %collective-permute-start.11 = (bf16[1,64,1024]{2,1,0:T(8,128)(2,1)S(1)}, bf16[1,64,1024]{2,1,0:T(8,128)(2,1)S(1)}, u32[]{:S(2)}, u32[]{:S(2)}) collective-permute-start(bf16[1,64,1024]{2,1,0:T(8,128)(2,1)S(1)} %slice.13.first), channel_id=1, source_target_pairs={{0,4},{4,12},{8,0},{12,20},{16,8},{20,28},{24,16},{28,24},{1,5},{5... | collective-permute-start | bytes 393224 | tf_op jit(solution)/shard_map/d/ppermute | solution.py:270
  60.2 0.0 collective-permute-done.13.refs_3_
  60.2 0.0 collective-permute-done.15.refs_6_
  60.2 0.0 collective-permute-done.16.refs_7_
  60.2 2.5 %turn_acts.1.acts = bf16[3,512,1024]{2,1,0:T(8,128)(2,1)S(1)} custom-call(s32[3]{0:T(128)S(1)} %pad_add_fusion.where_ref, bf16[4,3,16,1024]{3,2,1,0:T(8,128)(2,1)S(1)} %get-tuple-element.33.refs_0_, bf16[4,3,16,1024]{3,2,1,0:T(8,128)(2,1)S(1)} %collective-permute-done.5.refs_1_, bf16[4,3,16,1024]{3,2,1,0:T(8,128)(2,1)S(1)} %collective-permute-done.12.refs_2_, ...), custom_call_target="tpu_custom_call" | custom-call | tf_op jit(solution)/shard_map/turn_acts/pallas_call | solution.py:156
  62.8 0.0 collective-permute-done.17.second
  62.8 4.2 %multiply.2.refs_0_ = f32[1024,1024]{1,0:T(8,128)S(1)} custom-call(bf16[2,64,1024]{2,1,0:T(8,128)(2,1)S(1)} %slice.14.first, bf16[2,64,1024]{2,1,0:T(8,128)(2,1)S(1)} %collective-permute-done.17.second, bf16[4,256,256]{2,1,0:T(8,128)(2,1)S(1)} %get-tuple-element.29.refs_6_.high, bf16[4,256,256]{2,1,0:T(8,128)(2,1)S(1)} %get-tuple-element.30.refs_7_.low, ...), custom_call_target="tpu_custom_call" | custom-call | tf_op jit(solution)/shard_map/multiply/pallas_call | solution.py:216
  67.0 0.0 collective-permute-done.11.second
  67.0 3.5 %multiply.3 = f32[1024,1024]{1,0:T(8,128)} custom-call(bf16[1,64,1024]{2,1,0:T(8,128)(2,1)S(1)} %slice.13.first, bf16[1,64,1024]{2,1,0:T(8,128)(2,1)S(1)} %collective-permute-done.11.second, bf16[4,256,256]{2,1,0:T(8,128)(2,1)S(1)} %get-tuple-element.29.refs_6_.high, bf16[4,256,256]{2,1,0:T(8,128)(2,1)S(1)} %get-tuple-element.30.refs_7_.low, ...), custom_call_target="tpu_custom_call" | custom-call | tf_op jit(solution)/shard_map/multiply/pallas_call | solution.py:216
  (5 shorter events, 0.0 us)
Async XLA Ops:
  0.0 10.6 %copy-start = (bf16[3,64,1024]{2,1,0:T(8,128)(2,1)S(1)}, bf16[3,64,1024]{2,1,0:T(8,128)(2,1)}, u32[]{:S(2)}) copy-start(bf16[3,64,1024]{2,1,0:T(8,128)(2,1)} %refs_0_.1) | copy-start | bytes 1179652
  0.0 44.7 %copy-start.2 = (f32[128,8,8]{0,2,1:T(8,128)S(1)}, f32[128,8,8]{0,2,1:T(8,128)}, u32[]{:S(2)}) copy-start(f32[128,8,8]{0,2,1:T(8,128)} %param.7) | copy-start | bytes 98308
  0.0 44.7 %copy-start.1 = (f32[128,8,8]{0,2,1:T(8,128)S(1)}, f32[128,8,8]{0,2,1:T(8,128)}, u32[]{:S(2)}) copy-start(f32[128,8,8]{0,2,1:T(8,128)} %param.6) | copy-start | bytes 98308
  0.0 30.5 %collective-permute-start.7 = (bf16[3,64,1024]{2,1,0:T(8,128)(2,1)}, bf16[3,64,1024]{2,1,0:T(8,128)(2,1)S(1)}, u32[]{:S(2)}, u32[]{:S(2)}) collective-permute-start(bf16[3,64,1024]{2,1,0:T(8,128)(2,1)} %refs_0_.1), channel_id=1, source_target_pairs={{0,8},{4,0},{8,16},{12,4},{16,24},{20,12},{24,28},{28,20},{1,9},{5... | collective-permute-start | bytes 1179656 | tf_op jit(solution)/shard_map/u1/ppermute | solution.py:270
  5.0 12.0 %collective-permute-start.1 = (bf16[2,3,16,1024]{3,2,1,0:T(8,128)(2,1)S(1)}, bf16[2,3,16,1024]{3,2,1,0:T(8,128)(2,1)S(1)}, u32[]{:S(2)}, u32[]{:S(2)}) collective-permute-start(bf16[2,3,16,1024]{3,2,1,0:T(8,128)(2,1)S(1)} %get-tuple-element.21), channel_id=1, source_target_pairs={{0,8},{4,12},{8,16},{12,20},{16,24},{20,28},{24,0},{28,4},{1,9},{5... | collective-permute-start | bytes 589832 | tf_op jit(solution)/shard_map/az1/ppermute | solution.py:270
  6.6 15.2 %collective-permute-start.2 = (bf16[2,3,16,1024]{3,2,1,0:T(8,128)(2,1)S(1)}, bf16[2,3,16,1024]{3,2,1,0:T(8,128)(2,1)S(1)}, u32[]{:S(2)}, u32[]{:S(2)}) collective-permute-start(bf16[2,3,16,1024]{3,2,1,0:T(8,128)(2,1)S(1)} %get-tuple-element.22), channel_id=1, source_target_pairs={{0,16},{4,20},{8,24},{12,28},{16,0},{20,4},{24,8},{28,12},{1,17},{... | collective-permute-start | bytes 589832 | tf_op jit(solution)/shard_map/az2/ppermute | solution.py:270
  9.2 15.2 %collective-permute-start.3 = (bf16[2,3,16,1024]{3,2,1,0:T(8,128)(2,1)S(1)}, bf16[2,3,16,1024]{3,2,1,0:T(8,128)(2,1)S(1)}, u32[]{:S(2)}, u32[]{:S(2)}) collective-permute-start(bf16[2,3,16,1024]{3,2,1,0:T(8,128)(2,1)S(1)} %get-tuple-element.23), channel_id=1, source_target_pairs={{0,24},{4,28},{8,0},{12,4},{16,8},{20,12},{24,16},{28,20},{1,25},{... | collective-permute-start | bytes 589832 | tf_op jit(solution)/shard_map/az3/ppermute | solution.py:270
  10.6 23.6 %collective-permute-start = (bf16[3,64,1024]{2,1,0:T(8,128)(2,1)S(1)}, bf16[3,64,1024]{2,1,0:T(8,128)(2,1)S(1)}, u32[]{:S(2)}, u32[]{:S(2)}) collective-permute-start(bf16[3,64,1024]{2,1,0:T(8,128)(2,1)S(1)} %copy-done), channel_id=1, source_target_pairs={{0,4},{4,12},{8,0},{12,20},{16,8},{20,28},{24,16},{28,24},{1,5},{5... | collective-permute-start | bytes 1179656 | tf_op jit(solution)/shard_map/d1/ppermute | solution.py:270
  24.4 14.6 %collective-permute-start.5 = (bf16[4,3,16,1024]{3,2,1,0:T(8,128)(2,1)S(1)}, bf16[4,3,16,1024]{3,2,1,0:T(8,128)(2,1)S(1)}, u32[]{:S(2)}, u32[]{:S(2)}) collective-permute-start(bf16[4,3,16,1024]{3,2,1,0:T(8,128)(2,1)S(1)} %get-tuple-element.26), channel_id=1, source_target_pairs={{0,4},{4,0},{8,12},{12,8},{16,20},{20,16},{24,28},{28,24},{1,5},{5... | collective-permute-start | bytes 1179656 | tf_op jit(solution)/shard_map/ay/ppermute | solution.py:270
  29.0 11.5 %collective-permute-start.9 = (bf16[4,3,16,1024]{3,2,1,0:T(8,128)(2,1)S(1)}, bf16[4,3,16,1024]{3,2,1,0:T(8,128)(2,1)S(1)}, u32[]{:S(2)}, u32[]{:S(2)}) collective-permute-start(bf16[4,3,16,1024]{3,2,1,0:T(8,128)(2,1)S(1)} %get-tuple-element.33.refs_0_), channel_id=1, source_target_pairs={{0,2},{1,3},{2,0},{3,1},{4,6},{5,7},{6,4},{7,5},{8,10},{9,11},{10,... | collective-permute-start | bytes 1179656 | tf_op jit(solution)/shard_map/as2/ppermute | solution.py:270
  30.5 14.2 %collective-permute-start.8 = (bf16[3,64,1024]{2,1,0:T(8,128)(2,1)S(1)}, bf16[3,64,1024]{2,1,0:T(8,128)(2,1)S(1)}, u32[]{:S(2)}, u32[]{:S(2)}) collective-permute-start(bf16[3,64,1024]{2,1,0:T(8,128)(2,1)S(1)} %collective-permute-done.7.refs_1_), channel_id=1, source_target_pairs={{0,8},{4,0},{8,16},{12,4},{16,24},{20,12},{24,28},{28,20},{1,9},{5... | collective-permute-start | bytes 1179656 | tf_op jit(solution)/shard_map/u2/ppermute | solution.py:270
  34.1 12.4 %collective-permute-start.4 = (bf16[3,64,1024]{2,1,0:T(8,128)(2,1)S(1)}, bf16[3,64,1024]{2,1,0:T(8,128)(2,1)S(1)}, u32[]{:S(2)}, u32[]{:S(2)}) collective-permute-start(bf16[3,64,1024]{2,1,0:T(8,128)(2,1)S(1)} %collective-permute-done.refs_2_), channel_id=1, source_target_pairs={{0,4},{4,12},{8,0},{12,20},{16,8},{20,28},{24,16},{28,24},{1,5},{5... | collective-permute-start | bytes 1179656 | tf_op jit(solution)/shard_map/d2/ppermute | solution.py:270
  39.1 9.8 %collective-permute-start.14 = (bf16[4,3,16,1024]{3,2,1,0:T(8,128)(2,1)S(1)}, bf16[4,3,16,1024]{3,2,1,0:T(8,128)(2,1)S(1)}, u32[]{:S(2)}, u32[]{:S(2)}) collective-permute-start(bf16[4,3,16,1024]{3,2,1,0:T(8,128)(2,1)S(1)} %collective-permute-done.5.refs_1_), channel_id=1, source_target_pairs={{0,2},{1,3},{2,0},{3,1},{4,6},{5,7},{6,4},{7,5},{8,10},{9,11},{10,... | collective-permute-start | bytes 1179656 | tf_op jit(solution)/shard_map/ag2/ppermute | solution.py:270
  44.7 8.3 %collective-permute-start.10 = (bf16[3,64,1024]{2,1,0:T(8,128)(2,1)S(1)}, bf16[3,64,1024]{2,1,0:T(8,128)(2,1)S(1)}, u32[]{:S(2)}, u32[]{:S(2)}) collective-permute-start(bf16[3,64,1024]{2,1,0:T(8,128)(2,1)S(1)} %collective-permute-done.8.refs_3_), channel_id=1, source_target_pairs={{0,8},{4,0},{8,16},{12,4},{16,24},{20,12},{24,28},{28,20},{1,9},{5... | collective-permute-start | bytes 1179656 | tf_op jit(solution)/shard_map/u3/ppermute | solution.py:270
  44.7 8.3 %collective-permute-start.12 = (bf16[4,3,16,1024]{3,2,1,0:T(8,128)(2,1)S(1)}, bf16[4,3,16,1024]{3,2,1,0:T(8,128)(2,1)S(1)}, u32[]{:S(2)}, u32[]{:S(2)}) collective-permute-start(bf16[4,3,16,1024]{3,2,1,0:T(8,128)(2,1)S(1)} %get-tuple-element.33.refs_0_), channel_id=1, source_target_pairs={{0,1},{1,0},{2,3},{3,2},{4,5},{5,4},{6,7},{7,6},{8,9},{9,8},{10,11... | collective-permute-start | bytes 1179656 | tf_op jit(solution)/shard_map/as1/ppermute | solution.py:270
  46.5 11.6 %collective-permute-start.6 = (bf16[3,64,1024]{2,1,0:T(8,128)(2,1)S(1)}, bf16[3,64,1024]{2,1,0:T(8,128)(2,1)S(1)}, u32[]{:S(2)}, u32[]{:S(2)}) collective-permute-start(bf16[3,64,1024]{2,1,0:T(8,128)(2,1)S(1)} %collective-permute-done.4.refs_4_), channel_id=1, source_target_pairs={{0,4},{4,12},{8,0},{12,20},{16,8},{20,28},{24,16},{28,24},{1,5},{5... | collective-permute-start | bytes 1179656 | tf_op jit(solution)/shard_map/d3/ppermute | solution.py:270
  48.6 11.6 %collective-permute-start.13 = (bf16[4,3,16,1024]{3,2,1,0:T(8,128)(2,1)S(1)}, bf16[4,3,16,1024]{3,2,1,0:T(8,128)(2,1)S(1)}, u32[]{:S(2)}, u32[]{:S(2)}) collective-permute-start(bf16[4,3,16,1024]{3,2,1,0:T(8,128)(2,1)S(1)} %collective-permute-done.5.refs_1_), channel_id=1, source_target_pairs={{0,1},{1,0},{2,3},{3,2},{4,5},{5,4},{6,7},{7,6},{8,9},{9,8},{10,11... | collective-permute-start | bytes 1179656 | tf_op jit(solution)/shard_map/ag1/ppermute | solution.py:270
  48.8 11.4 %collective-permute-start.15 = (bf16[4,3,16,1024]{3,2,1,0:T(8,128)(2,1)S(1)}, bf16[4,3,16,1024]{3,2,1,0:T(8,128)(2,1)S(1)}, u32[]{:S(2)}, u32[]{:S(2)}) collective-permute-start(bf16[4,3,16,1024]{3,2,1,0:T(8,128)(2,1)S(1)} %collective-permute-done.9.refs_4_), channel_id=1, source_target_pairs={{0,1},{1,0},{2,3},{3,2},{4,5},{5,4},{6,7},{7,6},{8,9},{9,8},{10,11... | collective-permute-start | bytes 1179656 | tf_op jit(solution)/shard_map/as3/ppermute | solution.py:270
  53.0 7.3 %collective-permute-start.16 = (bf16[4,3,16,1024]{3,2,1,0:T(8,128)(2,1)S(1)}, bf16[4,3,16,1024]{3,2,1,0:T(8,128)(2,1)S(1)}, u32[]{:S(2)}, u32[]{:S(2)}) collective-permute-start(bf16[4,3,16,1024]{3,2,1,0:T(8,128)(2,1)S(1)} %collective-permute-done.14.refs_5_), channel_id=1, source_target_pairs={{0,1},{1,0},{2,3},{3,2},{4,5},{5,4},{6,7},{7,6},{8,9},{9,8},{10,11... | collective-permute-start | bytes 1179656 | tf_op jit(solution)/shard_map/ag3/ppermute | solution.py:270
  53.0 9.8 %collective-permute-start.17 = (bf16[2,64,1024]{2,1,0:T(8,128)(2,1)S(1)}, bf16[2,64,1024]{2,1,0:T(8,128)(2,1)S(1)}, u32[]{:S(2)}, u32[]{:S(2)}) collective-permute-start(bf16[2,64,1024]{2,1,0:T(8,128)(2,1)S(1)} %slice.15), channel_id=1, source_target_pairs={{0,8},{4,0},{8,16},{12,4},{16,24},{20,12},{24,28},{28,20},{1,9},{5... | collective-permute-start | bytes 786440 | tf_op jit(solution)/shard_map/u/ppermute | solution.py:270
  58.1 8.9 %collective-permute-start.11 = (bf16[1,64,1024]{2,1,0:T(8,128)(2,1)S(1)}, bf16[1,64,1024]{2,1,0:T(8,128)(2,1)S(1)}, u32[]{:S(2)}, u32[]{:S(2)}) collective-permute-start(bf16[1,64,1024]{2,1,0:T(8,128)(2,1)S(1)} %slice.13.first), channel_id=1, source_target_pairs={{0,4},{4,12},{8,0},{12,20},{16,8},{20,28},{24,16},{28,24},{1,5},{5... | collective-permute-start | bytes 393224 | tf_op jit(solution)/shard_map/d/ppermute | solution.py:270

commit v4 on v3

--- a/solution.py
+++ b/solution.py
@@ -8,6 +8,13 @@
 from jax.sharding import PartitionSpec as P
 
 BF, F32 = jnp.bfloat16, jnp.float32
+COSTS = {'turn_grads': 10000000000}
+
+
+def cost(name):
+    flops = COSTS.get(name)
+    return flops and pl.CostEstimate(flops=flops, bytes_accessed=0, transcendentals=0)
+
 SCALARS = pl.BlockSpec(memory_space=pltpu.SMEM)
 VECTORS = pl.BlockSpec(memory_space=pltpu.VMEM)
 
@@ -71,27 +78,24 @@
         spread_kernel,
         out_shape=tuple(shapes),
         compiler_params=pltpu.CompilerParams(vmem_limit_bytes=limit(*shapes)),
+        cost_estimate=cost("spread"),
         name="spread",
     )(*flat)
     return out[:2], out[2:]
 
 
-def cut_kernel(half, where_ref, acts_ref, *refs):
-    *outs, sems = refs
+def cut_kernel(where_ref, acts_ref, stay_ref, go_ref, sems):
+    half, _, quarter, width = stay_ref.shape
     q, z, y = where_ref[0], where_ref[1], where_ref[2]
-    _, _, quarter, width = outs[0].shape[0:4]
+    rows = pl.ds(pl.multiple_of(q * quarter, quarter), quarter)
     copies = []
     for k in range(half):
-        for other in range(2):
-            column = ((z + k) % half * 2 + (y ^ other)) * width
+        for other, out_ref in enumerate((stay_ref, go_ref)):
+            column = pl.multiple_of((lax.rem(z + k, half) * 2 + (y ^ other)) * width, width)
             copies.append(
                 pltpu.make_async_copy(
-                    acts_ref.at[
-                        :,
-                        pl.ds(pl.multiple_of(q * quarter, quarter), quarter),
-                        pl.ds(pl.multiple_of(column, width), width),
-                    ],
-                    outs[k].at[other],
+                    acts_ref.at[:, rows, pl.ds(column, width)],
+                    out_ref.at[k],
                     sems.at[2 * k + other],
                 )
             )
@@ -100,65 +104,91 @@
 
 def cut(acts, where, n, m):
     seqs, rows, total = acts.shape
-    shape = jax.ShapeDtypeStruct((2, seqs, rows // m, total // n), BF)
-    return pl.pallas_call(
-        functools.partial(cut_kernel, n // 2),
+    shape = jax.ShapeDtypeStruct((n // 2, seqs, rows // m, total // n), BF)
+    return pl.pallas_call(
+        cut_kernel,
         in_specs=[SCALARS, pl.BlockSpec(memory_space=pltpu.HBM)],
-        out_specs=[VECTORS] * (n // 2),
-        out_shape=[shape] * (n // 2),
+        out_specs=[VECTORS] * 2,
+        out_shape=[shape] * 2,
         scratch_shapes=[pltpu.SemaphoreType.DMA((n,))],
-        compiler_params=pltpu.CompilerParams(vmem_limit_bytes=limit(*[shape] * (n // 2))),
+        compiler_params=pltpu.CompilerParams(vmem_limit_bytes=limit(shape, shape)),
+        cost_estimate=cost("cut"),
         name="cut",
     )(where, pltpu.with_memory_space_constraint(acts, pltpu.HBM))
 
 
-def part_kernel(*refs):
-    *pieces, stay, go = refs
-    for k, piece in enumerate(pieces):
-        stay[k], go[k] = piece[0], piece[1]
-
-
-def part(pieces):
-    half = len(pieces)
-    shape = jax.ShapeDtypeStruct((half, *pieces[0].shape[1:]), BF)
-    return pl.pallas_call(
-        part_kernel,
-        in_specs=[VECTORS] * half,
-        out_specs=[VECTORS] * 2,
-        out_shape=[shape] * 2,
-        compiler_params=pltpu.CompilerParams(vmem_limit_bytes=limit(shape, shape)),
-        name="part",
+def pair_kernel(stay, came, *outs):
+    for k, out in enumerate(outs):
+        out[0], out[1] = stay[k], came[k]
+
+
+def pair(stay, came):
+    half = stay.shape[0]
+    shape = jax.ShapeDtypeStruct((2, *stay.shape[1:]), BF)
+    return pl.pallas_call(
+        pair_kernel,
+        in_specs=[VECTORS] * 2,
+        out_specs=[VECTORS] * half,
+        out_shape=[shape] * half,
+        compiler_params=pltpu.CompilerParams(vmem_limit_bytes=limit(*[shape] * half)),
+        cost_estimate=cost("pair"),
+        name="pair",
+    )(stay, came)
+
+
+def join_kernel(*refs):
+    *pieces, out = refs
+    begin = 0
+    for piece in pieces:
+        out[begin : begin + piece.shape[0]] = piece[...]
+        begin += piece.shape[0]
+
+
+def join(pieces):
+    count = sum(p.shape[0] for p in pieces)
+    shape = jax.ShapeDtypeStruct((count, *pieces[0].shape[1:]), BF)
+    return pl.pallas_call(
+        join_kernel,
+        in_specs=[VECTORS] * len(pieces),
+        out_specs=VECTORS,
+        out_shape=shape,
+        compiler_params=pltpu.CompilerParams(vmem_limit_bytes=limit(shape, shape)),
+        cost_estimate=cost("join"),
+        name="join",
     )(*pieces)
 
 
-def turn_acts_kernel(place_of, m, where_ref, *refs):
-    pieces, (high, low, out_ref) = refs[: 2 * m], refs[2 * m :]
-    half, seqs, quarter, width = pieces[0].shape
+def turn_acts_kernel(place_of, half, m, content, where_ref, *refs):
+    *pieces, high, low, out_ref = refs
     groups, span, _ = high.shape
     q, z, y = where_ref[0], where_ref[1], where_ref[2]
-    for other in range(2):
-        starts = [place_of(z, y, lax.rem(z - k + half, half), y ^ other) * m for k in range(half)]
-        for j in range(m):
-            piece = pieces[2 * j + other]
-            for g in range(groups):
-                columns = pl.ds(g * span, span)
-                block = piece[:, :, :, columns].reshape(half * seqs * quarter, span)
-                turned = dot(block, high[g], ((1,), (0,))) + dot(block, low[g], ((1,), (0,)))
-                turned = turned.astype(BF).reshape(half, seqs, quarter, span)
-                for k in range(half):
-                    start = pl.multiple_of((starts[k] + (q ^ j)) * quarter, quarter)
-                    out_ref[:, pl.ds(start, quarter), columns] = turned[k]
-
-
-def turn_acts(where, pieces, parts, place_of, m):
-    half, seqs, quarter, width = pieces[0].shape
+    seqs, quarter, width = pieces[0].shape[1:]
+    start_of = {}
+    for piece, blocks in zip(pieces, content):
+        for j, k, other in blocks:
+            if (k, other) not in start_of:
+                place = place_of(z, y, lax.rem(z - k + half, half), y ^ other)
+                start_of[k, other] = place * m
+        for g in range(groups):
+            columns = pl.ds(g * span, span)
+            block = piece[:, :, :, columns].reshape(len(blocks) * seqs * quarter, span)
+            turned = dot(block, high[g], ((1,), (0,))) + dot(block, low[g], ((1,), (0,)))
+            turned = turned.astype(BF).reshape(len(blocks), seqs, quarter, span)
+            for i, (j, k, other) in enumerate(blocks):
+                start = pl.multiple_of((start_of[k, other] + (q ^ j)) * quarter, quarter)
+                out_ref[:, pl.ds(start, quarter), columns] = turned[i]
+
+
+def turn_acts(where, pieces, content, parts, place_of, half, m):
+    seqs, quarter, width = pieces[0].shape[1:]
     shape = jax.ShapeDtypeStruct((seqs, 2 * half * m * quarter, width), BF)
     return pl.pallas_call(
-        functools.partial(turn_acts_kernel, place_of, m),
-        in_specs=[SCALARS] + [VECTORS] * (2 * m + 2),
+        functools.partial(turn_acts_kernel, place_of, half, m, content),
+        in_specs=[SCALARS] + [VECTORS] * (len(pieces) + 2),
         out_specs=VECTORS,
         out_shape=shape,
         compiler_params=pltpu.CompilerParams(vmem_limit_bytes=limit(shape, shape)),
+        cost_estimate=cost("turn_acts"),
         name="turn_acts",
     )(where, *pieces, *parts)
 
@@ -190,64 +220,50 @@
         out_specs=VECTORS,
         out_shape=shape,
         compiler_params=pltpu.CompilerParams(vmem_limit_bytes=limit(shape, shape)),
+        cost_estimate=cost("turn_grads"),
         name="turn_grads",
     )(*pieces, *parts)
 
 
-def multiply_kernel(scale, first, second, high, low, grads, acts, *refs):
-    *before, out_ref = refs
-    total = before[0][...] if before else None
-    for s in range(acts.shape[0]):
-        late = turn_pair(high[0], low[0], first[s], second[s])
-        corr = dot(jnp.concatenate([grads[s], late], 1), acts[s], ((1,), (0,)))
+def multiply_kernel(scale, begin, count, first, second, high, low, acts, *refs):
+    grads, before, out_ref = refs[:count], refs[count:-1], refs[-1]
+    step = pl.program_id(0)
+    tile = high.shape[1]
+    columns = pl.ds(pl.multiple_of(step * tile, tile), tile)
+    total = before[0][columns, :] if before else None
+    for i in range(second.shape[0]):
+        s = begin + i
+        late = turn_pair(high[step], low[step], first[s, :, columns], second[i, :, columns])
+        turned = jnp.concatenate([*(g[s, columns, :] for g in grads), late], 1)
+        corr = dot(turned, acts[s], ((1,), (0,)))
         square = corr * corr * scale
         total = square if total is None else total + square
-    out_ref[...] = total
+    out_ref[(columns if out_ref.shape[0] > tile else slice(None)), :] = total
 
 
 def multiply(begin, last, parts, grads, acts, before=()):
-    count, rows, outs = last[1].shape
-    seqs, length, width = acts.shape
+    outs = last[1].shape[2]
+    _, length, width = acts.shape
     tile = parts[0].shape[1]
     shape = jax.ShapeDtypeStruct((outs, width), F32)
-    at = begin // count
-    assert at * count == begin
     strip = pl.BlockSpec((tile, width), lambda i: (i, 0))
     return pl.pallas_call(
-        functools.partial(multiply_kernel, 1.0 / length),
+        functools.partial(multiply_kernel, 1.0 / length, begin, len(grads)),
         grid=(outs // tile,),
-        in_specs=[
-            pl.BlockSpec((count, rows, tile), lambda i: (0, 0, i)),
-            pl.BlockSpec((count, rows, tile), lambda i: (0, 0, i)),
-        ]
-        + [pl.BlockSpec((1, tile, tile), lambda i: (i, 0, 0))] * 2
-        + [
-            pl.BlockSpec((count, tile, grads.shape[2]), lambda i: (at, i, 0)),
-            pl.BlockSpec((count, length, width), lambda i: (at, 0, 0)),
-        ]
-        + [strip] * len(before),
-        out_specs=strip,
+        in_specs=[VECTORS] * (5 + len(grads) + len(before)),
+        out_specs=strip if before else VECTORS,
         out_shape=shape,
-        compiler_params=pltpu.CompilerParams(
-            vmem_limit_bytes=limit(acts, jax.ShapeDtypeStruct((seqs, tile, length), BF))
-        ),
+        compiler_params=pltpu.CompilerParams(vmem_limit_bytes=limit(shape, shape)),
+        cost_estimate=cost("multiply"),
         name="multiply",
-    )(*last, *parts, grads, acts, *before)
+    )(*last, *parts, acts, *grads, *before)
 
 
 def after(value, *earlier):
     return lax.optimization_barrier((value, *earlier))[0]
 
 
-CAME = ("az1", "az2", "az3")
-TIES = {
-    "u2": CAME,
-    "d2": CAME,
-    "u3": ("ay", "as2"),
-    "d3": ("ay", "spread"),
-    "u": ("ag2", "as1"),
-    "d": ("tg",),
-}
+TIES = {'x22': ('u2', 'd2'), 'x12': ('x02',), 'az2': ('u1', 'd1'), 'u3': ('x12',)}
 
 
 def shards(acts, grads, act_basis, grad_basis):
@@ -284,20 +300,32 @@
     ops["spread"] = lambda tie: spread(tie(flat[0]), flat[1])
     ops["cut"] = lambda tie: cut(tie(acts), where, n, m)
 
+    over_y("ay", lambda: get("cut")[1])
+    ops["pair"] = lambda tie: pair(get("cut")[0], get("ay"))
     for k in range(1, half):
-        over_z(f"az{k}", lambda k=k: get("cut")[k], k)
-    ops["part"] = lambda tie: part([get("cut")[0]] + [get(f"az{k}") for k in range(1, half)])
-    over_y("ay", lambda: get("part")[1])
-    ops["as0"] = lambda tie: get("part")[0]
-    ops["ag0"] = lambda tie: get("ay")
-    for letter in "sg":
+        over_z(f"az{k}", lambda k=k: get("pair")[k], k)
+    come = lambda k: get(f"az{k}") if k else get("pair")[0]
+    pieces, content = [], []
+    middle = half // 2
+    for g, ks in enumerate(([0], [k for k in range(1, half) if k != middle], [middle])):
+        held = f"g{g}"
+        blocks = [(0, k, other) for k in ks for other in range(2)]
+        ops[held] = lambda tie, ks=ks: join([come(k) for k in ks]) if len(ks) > 1 else come(ks[0])
         bit = m // 2
-        held = [0]
         while bit:
-            for j in list(held):
-                held.append(j | bit)
-                over_out(f"a{letter}{j | bit}", lambda x=f"a{letter}{j}": get(x), bit)
+            got = f"x{g}{bit}"
+            over_out(got, lambda held=held: get(held), bit)
+            theirs = [(j ^ bit, k, other) for j, k, other in blocks]
             bit //= 2
+            if not bit:
+                pieces.append(got)
+                content.append(theirs)
+                break
+            both = f"{held}+"
+            ops[both] = lambda tie, held=held, got=got: join([get(held), get(got)])
+            held, blocks = both, blocks + theirs
+        pieces.append(held)
+        content.append(blocks)
 
     ring = [2 * z for z in range(half)] + [2 * z + 1 for z in reversed(range(half))]
 
@@ -324,17 +352,18 @@
         )
 
     ops["ta"] = lambda tie: turn_acts(
-        where,
-        [get(f"a{letter}{j}") for j in range(m) for letter in "sg"],
-        get("spread")[0],
-        place_of,
-        m,
+        tie(where), [get(x) for x in pieces], content, get("spread")[0], place_of, half, m
     )
-    ops["tg"] = lambda tie: turn_grads([get(x) for x in names[:-1]], get("spread")[1])
+    turned = {"tg1": names[:-3], "tg2": names[-3:-1]}
+    for name, of in turned.items():
+        ops[name] = lambda tie, of=of: turn_grads(
+            [tie(get(of[0]))] + [get(x) for x in of[1:]], get("spread")[1]
+        )
     late = get(names[-1])
     total = ()
-    for last, part_of, lo in ((get("u"), late[:first], 0), (get("d"), late[first:], first)):
-        total = (multiply(lo, [part_of, last], get("spread")[1], get("tg"), get("ta"), total),)
+    for name, lo in (("d", first), ("u", 0)):
+        last = [late, get(name)]
+        total = (multiply(lo, last, get("spread")[1], [get(x) for x in turned], get("ta"), total),)
     return total[0]
 
 

time: 71.2 us -> 67.3 us (0.945)
  starting transfers between devices: 25 us -> 21.9 us
    ppermute x18, starting transfers between devices: 25 us -> 21.9 us  [run(): return lax.ppermute(value, axis, perm)]
    pallas_call x5 -> x9, Pallas kernels: 12.2 us -> 11.6 us  [the longest x2 6.99 us: multiply(): pl.pallas_call(functools.partial(multiply_kernel, 1.0 / length, begin, le...]
    pallas_call x1 -> x2, Pallas kernels: 2.62 us -> 2.77 us  [turn_grads(): pl.pallas_call(turn_grads_kernel, in_specs=[VECTORS] * (len(pieces) + 2),...]
  transfers between devices with their start and end apart: 18 -> 18, of which waited for: 7 -> 8; matrix products, arithmetic and copies ran while one was open for 0% -> 0% of each run, Pallas kernels for 18% -> 14%
where the time goes in v4:
time: 67.3 us; the launch traced here: 67.2 us
  waiting for transfers between devices  28.9 us (43%)
  starting transfers between devices  21.9 us (33%)
  Pallas kernels  16.1 us (24%)
    ppermute x18, waiting for transfers between devices, run(): return lax.ppermute(value, axis, perm)  28.9 us
    ppermute x18, starting transfers between devices, run(): return lax.ppermute(value, axis, perm)  21.9 us
    pallas_call x2, Pallas kernels, multiply(): pl.pallas_call(functools.partial(multiply_kernel, 1.0 / length, begin, le...  6.99 us
    pallas_call x2, Pallas kernels, turn_grads(): pl.pallas_call(turn_grads_kernel, in_specs=[VECTORS] * (len(pieces) + 2),...  2.77 us
    pallas_call x1, Pallas kernels, turn_acts(): pl.pallas_call(functools.partial(turn_acts_kernel, place_of, half, m, con...  2.55 us
    pallas_call x1, Pallas kernels, cut(): pl.pallas_call(cut_kernel, in_specs=[SCALARS, pl.BlockSpec(memory_space=p...  1.84 us
    pallas_call x1, Pallas kernels, spread(): pl.pallas_call(spread_kernel, out_shape=tuple(shapes), compiler_params=pl...  1.79 us
  transfers between devices with their start and end apart: 18, of which 8 were waited for; matrix products, arithmetic and copies ran while one was open for 0% of the time, Pallas kernels for 14%

profile of v4, /device:TPU:0, one launch (start us, length us, event | category | flops | bytes accessed | tf_op | source)
XLA Modules:
  0.0 67.2 jit_solution(4112886375928375942)
XLA Ops:
  0.0 0.1 pad_add_fusion.where_ref
  0.1 1.8 %cut.1 = (bf16[4,3,16,1024]{3,2,1,0:T(8,128)(2,1)S(1)}, bf16[4,3,16,1024]{3,2,1,0:T(8,128)(2,1)S(1)}) custom-call(s32[3]{0:T(128)S(1)} %pad_add_fusion.where_ref, bf16[3,64,8192]{2,1,0:T(8,128)(2,1)} %acts_ref.1), custom_call_target="tpu_custom_call" | custom-call | tf_op jit(solution)/shard_map/cut/pallas_call | solution.py:108
  1.9 3.1 %collective-permute-start.5 = (bf16[4,3,16,1024]{3,2,1,0:T(8,128)(2,1)S(1)}, bf16[4,3,16,1024]{3,2,1,0:T(8,128)(2,1)S(1)}, u32[]{:S(2)}, u32[]{:S(2)}) collective-permute-start(bf16[4,3,16,1024]{3,2,1,0:T(8,128)(2,1)S(1)} %get-tuple-element.20), channel_id=1, source_target_pairs={{0,4},{4,0},{8,12},{12,8},{16,20},{20,16},{24,28},{28,24},{1,5},{5... | collective-permute-start | bytes 1179656 | tf_op jit(solution)/shard_map/ay/ppermute | solution.py:286
  5.0 0.0 copy-done.2
  5.0 0.1 collective-permute-start
  5.1 2.0 %collective-permute-start.3 = (bf16[3,64,1024]{2,1,0:T(8,128)(2,1)S(1)}, bf16[3,64,1024]{2,1,0:T(8,128)(2,1)S(1)}, u32[]{:S(2)}, u32[]{:S(2)}) collective-permute-start(bf16[3,64,1024]{2,1,0:T(8,128)(2,1)S(1)} %copy-done.2), channel_id=1, source_target_pairs={{0,8},{4,0},{8,16},{12,4},{16,24},{20,12},{24,28},{28,20},{1,9},{5... | collective-permute-start | bytes 1179656 | tf_op jit(solution)/shard_map/u1/ppermute | solution.py:286
  7.0 7.9 %collective-permute-done.5.came = bf16[4,3,16,1024]{3,2,1,0:T(8,128)(2,1)S(1)} collective-permute-done((bf16[4,3,16,1024]{3,2,1,0:T(8,128)(2,1)S(1)}, bf16[4,3,16,1024]{3,2,1,0:T(8,128)(2,1)S(1)}, u32[]{:S(2)}, u32[]{:S(2)}) %collective-permute-start.5) | collective-permute-done | bytes 393248 | tf_op jit(solution)/shard_map/ay/ppermute | solution.py:286
  14.9 0.1 pair.1
  15.0 1.0 %collective-permute-start.6 = (bf16[2,3,16,1024]{3,2,1,0:T(8,128)(2,1)S(1)}, bf16[2,3,16,1024]{3,2,1,0:T(8,128)(2,1)S(1)}, u32[]{:S(2)}, u32[]{:S(2)}) collective-permute-start(bf16[2,3,16,1024]{3,2,1,0:T(8,128)(2,1)S(1)} %get-tuple-element.21), channel_id=1, source_target_pairs={{0,8},{4,12},{8,16},{12,20},{16,24},{20,28},{24,0},{28,4},{1,9},{5... | collective-permute-start | bytes 589832 | tf_op jit(solution)/shard_map/az1/ppermute | solution.py:286
  16.0 3.2 %collective-permute-start.7 = (bf16[2,3,16,1024]{3,2,1,0:T(8,128)(2,1)S(1)}, bf16[2,3,16,1024]{3,2,1,0:T(8,128)(2,1)S(1)}, u32[]{:S(2)}, u32[]{:S(2)}) collective-permute-start(bf16[2,3,16,1024]{3,2,1,0:T(8,128)(2,1)S(1)} %get-tuple-element.22), channel_id=1, source_target_pairs={{0,24},{4,28},{8,0},{12,4},{16,8},{20,12},{24,16},{28,20},{1,25},{... | collective-permute-start | bytes 589832 | tf_op jit(solution)/shard_map/az3/ppermute | solution.py:286
  19.2 1.6 %collective-permute-start.8 = (bf16[2,3,16,1024]{3,2,1,0:T(8,128)(2,1)S(1)}, bf16[2,3,16,1024]{3,2,1,0:T(8,128)(2,1)S(1)}, u32[]{:S(2)}, u32[]{:S(2)}) collective-permute-start(bf16[2,3,16,1024]{3,2,1,0:T(8,128)(2,1)S(1)} %get-tuple-element.23.refs_0_), channel_id=1, source_target_pairs={{0,2},{1,3},{2,0},{3,1},{4,6},{5,7},{6,4},{7,5},{8,10},{9,11},{10,... | collective-permute-start | bytes 589832 | tf_op jit(solution)/shard_map/x02/ppermute | solution.py:286
  20.9 0.9 %collective-permute-done.refs_2_ = bf16[3,64,1024]{2,1,0:T(8,128)(2,1)S(1)} collective-permute-done((bf16[3,64,1024]{2,1,0:T(8,128)(2,1)S(1)}, bf16[3,64,1024]{2,1,0:T(8,128)(2,1)S(1)}, u32[]{:S(2)}, u32[]{:S(2)}) %collective-permute-start) | collective-permute-done | bytes 393248 | tf_op jit(solution)/shard_map/d1/ppermute | solution.py:286
  21.8 2.5 %collective-permute-start.1 = (bf16[3,64,1024]{2,1,0:T(8,128)(2,1)S(1)}, bf16[3,64,1024]{2,1,0:T(8,128)(2,1)S(1)}, u32[]{:S(2)}, u32[]{:S(2)}) collective-permute-start(bf16[3,64,1024]{2,1,0:T(8,128)(2,1)S(1)} %collective-permute-done.refs_2_), channel_id=1, source_target_pairs={{0,4},{4,12},{8,0},{12,20},{16,8},{20,28},{24,16},{28,24},{1,5},{5... | collective-permute-start | bytes 1179656 | tf_op jit(solution)/shard_map/d2/ppermute | solution.py:286
  24.3 0.0 collective-permute-done.3.refs_1_
  24.3 0.0 collective-permute-start.4
  24.3 0.1 collective-permute-done.6.refs_0_
  24.4 2.1 %collective-permute-done.7.refs_1_ = bf16[2,3,16,1024]{3,2,1,0:T(8,128)(2,1)S(1)} collective-permute-done((bf16[2,3,16,1024]{3,2,1,0:T(8,128)(2,1)S(1)}, bf16[2,3,16,1024]{3,2,1,0:T(8,128)(2,1)S(1)}, u32[]{:S(2)}, u32[]{:S(2)}) %collective-permute-start.7) | collective-permute-done | bytes 196640 | tf_op jit(solution)/shard_map/az3/ppermute | solution.py:286
  26.6 0.0 collective-permute-done.8.refs_1_
  26.6 1.5 %collective-permute-start.9 = (bf16[4,3,16,1024]{3,2,1,0:T(8,128)(2,1)S(1)}, bf16[4,3,16,1024]{3,2,1,0:T(8,128)(2,1)S(1)}, u32[]{:S(2)}, u32[]{:S(2)}) collective-permute-start(bf16[4,3,16,1024]{3,2,1,0:T(8,128)(2,1)S(1)} %join.4.refs_0_), channel_id=1, source_target_pairs={{0,2},{1,3},{2,0},{3,1},{4,6},{5,7},{6,4},{7,5},{8,10},{9,11},{10,... | collective-permute-start | bytes 1179656 | tf_op jit(solution)/shard_map/x12/ppermute | solution.py:286
  28.1 0.6 collective-permute-start.14
  28.7 0.0 copy-done.1
  28.7 1.8 %spread.1 = (bf16[4,256,256]{2,1,0:T(8,128)(2,1)S(1)}, bf16[4,256,256]{2,1,0:T(8,128)(2,1)S(1)}, bf16[4,256,256]{2,1,0:T(8,128)(2,1)S(1)}, bf16[4,256,256]{2,1,0:T(8,128)(2,1)S(1)}) custom-call(f32[64,128]{1,0:T(8,128)S(1)} %bitcast.9, f32[64,128]{1,0:T(8,128)S(1)} %bitcast.10), custom_call_target="tpu_custom_call" | custom-call | tf_op jit(solution)/shard_map/spread/pallas_call | solution.py:77
  30.5 0.1 collective-permute-start.12
  30.6 12.6 %collective-permute-done.14.refs_0_ = bf16[2,3,16,1024]{3,2,1,0:T(8,128)(2,1)S(1)} collective-permute-done((bf16[2,3,16,1024]{3,2,1,0:T(8,128)(2,1)S(1)}, bf16[2,3,16,1024]{3,2,1,0:T(8,128)(2,1)S(1)}, u32[]{:S(2)}, u32[]{:S(2)}) %collective-permute-start.14) | collective-permute-done | bytes 196640 | tf_op jit(solution)/shard_map/az2/ppermute | solution.py:286
  43.2 0.0 collective-permute-done.1.refs_0_
  43.2 0.0 collective-permute-done.4.refs_3_
  43.2 1.5 %collective-permute-start.15 = (bf16[2,3,16,1024]{3,2,1,0:T(8,128)(2,1)S(1)}, bf16[2,3,16,1024]{3,2,1,0:T(8,128)(2,1)S(1)}, u32[]{:S(2)}, u32[]{:S(2)}) collective-permute-start(bf16[2,3,16,1024]{3,2,1,0:T(8,128)(2,1)S(1)} %collective-permute-done.14.refs_0_), channel_id=1, source_target_pairs={{0,2},{1,3},{2,0},{3,1},{4,6},{5,7},{6,4},{7,5},{8,10},{9,11},{10,... | collective-permute-start | bytes 589832 | tf_op jit(solution)/shard_map/x22/ppermute | solution.py:286
  44.6 1.5 %collective-permute-start.2 = (bf16[3,64,1024]{2,1,0:T(8,128)(2,1)S(1)}, bf16[3,64,1024]{2,1,0:T(8,128)(2,1)S(1)}, u32[]{:S(2)}, u32[]{:S(2)}) collective-permute-start(bf16[3,64,1024]{2,1,0:T(8,128)(2,1)S(1)} %collective-permute-done.1.refs_0_), channel_id=1, source_target_pairs={{0,4},{4,12},{8,0},{12,20},{16,8},{20,28},{24,16},{28,24},{1,5},{5... | collective-permute-start | bytes 1179656 | tf_op jit(solution)/shard_map/d3/ppermute | solution.py:286
  46.2 0.0 collective-permute-done.9.refs_1_
  46.2 0.5 collective-permute-start.10
  46.7 1.8 %turn_grads.2.refs_0_ = bf16[3,1024,256]{2,1,0:T(8,128)(2,1)S(1)} custom-call(bf16[3,64,1024]{2,1,0:T(8,128)(2,1)S(1)} %copy-done.2, bf16[3,64,1024]{2,1,0:T(8,128)(2,1)S(1)} %collective-permute-done.3.refs_1_, bf16[3,64,1024]{2,1,0:T(8,128)(2,1)S(1)} %collective-permute-done.refs_2_, bf16[3,64,1024]{2,1,0:T(8,128)(2,1)S(1)} %collective-permute-done.4.refs_3_, ...), custom_call_target="tpu_custom_call" | custom-call | flops 10000000000 | tf_op jit(solution)/shard_map/turn_grads/pallas_call | solution.py:217
  48.5 0.5 collective-permute-done.15.refs_1_
  49.0 0.1 collective-permute-start.16
  49.1 0.1 join.6.refs_3_
  49.2 0.6 collective-permute-start.13
  49.7 4.5 %collective-permute-done.2.first = bf16[3,64,1024]{2,1,0:T(8,128)(2,1)S(1)} collective-permute-done((bf16[3,64,1024]{2,1,0:T(8,128)(2,1)S(1)}, bf16[3,64,1024]{2,1,0:T(8,128)(2,1)S(1)}, u32[]{:S(2)}, u32[]{:S(2)}) %collective-permute-start.2) | collective-permute-done | bytes 393248 | tf_op jit(solution)/shard_map/d3/ppermute | solution.py:286
  54.2 1.6 %collective-permute-start.17 = (bf16[1,64,1024]{2,1,0:T(8,128)(2,1)S(1)}, bf16[1,64,1024]{2,1,0:T(8,128)(2,1)S(1)}, u32[]{:S(2)}, u32[]{:S(2)}) collective-permute-start(bf16[1,64,1024]{2,1,0:T(8,128)(2,1)S(1)} %slice.9), channel_id=1, source_target_pairs={{0,4},{4,12},{8,0},{12,20},{16,8},{20,28},{24,16},{28,24},{1,5},{5... | collective-permute-start | bytes 393224 | tf_op jit(solution)/shard_map/d/ppermute | solution.py:286
  55.9 0.0 collective-permute-done.10.refs_1_
  55.9 0.5 collective-permute-start.11
  56.4 1.0 %turn_grads.3.refs_1_ = bf16[3,1024,128]{2,1,0:T(8,128)(2,1)S(1)} custom-call(bf16[3,64,1024]{2,1,0:T(8,128)(2,1)S(1)} %collective-permute-done.1.refs_0_, bf16[3,64,1024]{2,1,0:T(8,128)(2,1)S(1)} %collective-permute-done.10.refs_1_, bf16[4,256,256]{2,1,0:T(8,128)(2,1)S(1)} %get-tuple-element.26.refs_4_.refs_2_.high, ...), custom_call_target="tpu_custom_call" | custom-call | flops 10000000000 | tf_op jit(solution)/shard_map/turn_grads/pallas_call | solution.py:217
  57.4 0.0 collective-permute-done.12.refs_0_
  57.4 0.0 collective-permute-done.16.refs_4_
  57.4 0.0 collective-permute-done.13.refs_2_
  57.4 2.5 %turn_acts.1.acts = bf16[3,512,1024]{2,1,0:T(8,128)(2,1)S(1)} custom-call(s32[3]{0:T(128)S(1)} %pad_add_fusion.where_ref, bf16[4,3,16,1024]{3,2,1,0:T(8,128)(2,1)S(1)} %collective-permute-done.12.refs_0_, bf16[4,3,16,1024]{3,2,1,0:T(8,128)(2,1)S(1)} %join.5.refs_1_, bf16[8,3,16,1024]{3,2,1,0:T(8,128)(2,1)S(1)} %collective-permute-done.13.refs_2_, ...), custom_call_target="tpu_custom_call" | custom-call | tf_op jit(solution)/shard_map/turn_acts/pallas_call | solution.py:185
  60.0 0.0 collective-permute-done.17.second
  60.0 2.1 %multiply.2.refs_2_ = f32[1024,1024]{1,0:T(8,128)S(1)} custom-call(bf16[3,64,1024]{2,1,0:T(8,128)(2,1)S(1)} %collective-permute-done.2.first, bf16[1,64,1024]{2,1,0:T(8,128)(2,1)S(1)} %collective-permute-done.17.second, bf16[4,256,256]{2,1,0:T(8,128)(2,1)S(1)} %get-tuple-element.26.refs_4_.refs_2_.high, ...), custom_call_target="tpu_custom_call" | custom-call | tf_op jit(solution)/shard_map/multiply/pallas_call | solution.py:250
  62.1 0.2 collective-permute-done.11.second
  62.3 4.9 %multiply.3 = f32[1024,1024]{1,0:T(8,128)} custom-call(bf16[3,64,1024]{2,1,0:T(8,128)(2,1)S(1)} %collective-permute-done.2.first, bf16[2,64,1024]{2,1,0:T(8,128)(2,1)S(1)} %collective-permute-done.11.second, bf16[4,256,256]{2,1,0:T(8,128)(2,1)S(1)} %get-tuple-element.26.refs_4_.refs_2_.high, bf16[4,256,256]{2,1,0:T(8,128)(2,1)S(1)} %get-tuple-element.27.refs_5_.refs_3_.low, ...), custom_call_target="tpu_custom_call" | custom-call | tf_op jit(solution)/shard_map/multiply/pallas_call | solution.py:250
  (9 shorter events, 0.1 us)
Async XLA Ops:
  0.0 5.0 %copy-start.2 = (bf16[3,64,1024]{2,1,0:T(8,128)(2,1)S(1)}, bf16[3,64,1024]{2,1,0:T(8,128)(2,1)}, u32[]{:S(2)}) copy-start(bf16[3,64,1024]{2,1,0:T(8,128)(2,1)} %refs_0_.1) | copy-start | bytes 1179652
  0.0 28.7 %copy-start.1 = (f32[128,8,8]{0,2,1:T(8,128)S(1)}, f32[128,8,8]{0,2,1:T(8,128)}, u32[]{:S(2)}) copy-start(f32[128,8,8]{0,2,1:T(8,128)} %param.7) | copy-start | bytes 98308
  0.0 28.7 %copy-start = (f32[128,8,8]{0,2,1:T(8,128)S(1)}, f32[128,8,8]{0,2,1:T(8,128)}, u32[]{:S(2)}) copy-start(f32[128,8,8]{0,2,1:T(8,128)} %param.6) | copy-start | bytes 98308
  1.9 13.0 %collective-permute-start.5 = (bf16[4,3,16,1024]{3,2,1,0:T(8,128)(2,1)S(1)}, bf16[4,3,16,1024]{3,2,1,0:T(8,128)(2,1)S(1)}, u32[]{:S(2)}, u32[]{:S(2)}) collective-permute-start(bf16[4,3,16,1024]{3,2,1,0:T(8,128)(2,1)S(1)} %get-tuple-element.20), channel_id=1, source_target_pairs={{0,4},{4,0},{8,12},{12,8},{16,20},{20,16},{24,28},{28,24},{1,5},{5... | collective-permute-start | bytes 1179656 | tf_op jit(solution)/shard_map/ay/ppermute | solution.py:286
  5.0 16.8 %collective-permute-start = (bf16[3,64,1024]{2,1,0:T(8,128)(2,1)S(1)}, bf16[3,64,1024]{2,1,0:T(8,128)(2,1)S(1)}, u32[]{:S(2)}, u32[]{:S(2)}) collective-permute-start(bf16[3,64,1024]{2,1,0:T(8,128)(2,1)S(1)} %copy-done.2), channel_id=1, source_target_pairs={{0,4},{4,12},{8,0},{12,20},{16,8},{20,28},{24,16},{28,24},{1,5},{5... | collective-permute-start | bytes 1179656 | tf_op jit(solution)/shard_map/d1/ppermute | solution.py:286
  5.1 19.2 %collective-permute-start.3 = (bf16[3,64,1024]{2,1,0:T(8,128)(2,1)S(1)}, bf16[3,64,1024]{2,1,0:T(8,128)(2,1)S(1)}, u32[]{:S(2)}, u32[]{:S(2)}) collective-permute-start(bf16[3,64,1024]{2,1,0:T(8,128)(2,1)S(1)} %copy-done.2), channel_id=1, source_target_pairs={{0,8},{4,0},{8,16},{12,4},{16,24},{20,12},{24,28},{28,20},{1,9},{5... | collective-permute-start | bytes 1179656 | tf_op jit(solution)/shard_map/u1/ppermute | solution.py:286
  15.0 9.4 %collective-permute-start.6 = (bf16[2,3,16,1024]{3,2,1,0:T(8,128)(2,1)S(1)}, bf16[2,3,16,1024]{3,2,1,0:T(8,128)(2,1)S(1)}, u32[]{:S(2)}, u32[]{:S(2)}) collective-permute-start(bf16[2,3,16,1024]{3,2,1,0:T(8,128)(2,1)S(1)} %get-tuple-element.21), channel_id=1, source_target_pairs={{0,8},{4,12},{8,16},{12,20},{16,24},{20,28},{24,0},{28,4},{1,9},{5... | collective-permute-start | bytes 589832 | tf_op jit(solution)/shard_map/az1/ppermute | solution.py:286
  16.0 10.5 %collective-permute-start.7 = (bf16[2,3,16,1024]{3,2,1,0:T(8,128)(2,1)S(1)}, bf16[2,3,16,1024]{3,2,1,0:T(8,128)(2,1)S(1)}, u32[]{:S(2)}, u32[]{:S(2)}) collective-permute-start(bf16[2,3,16,1024]{3,2,1,0:T(8,128)(2,1)S(1)} %get-tuple-element.22), channel_id=1, source_target_pairs={{0,24},{4,28},{8,0},{12,4},{16,8},{20,12},{24,16},{28,20},{1,25},{... | collective-permute-start | bytes 589832 | tf_op jit(solution)/shard_map/az3/ppermute | solution.py:286
  19.2 7.3 %collective-permute-start.8 = (bf16[2,3,16,1024]{3,2,1,0:T(8,128)(2,1)S(1)}, bf16[2,3,16,1024]{3,2,1,0:T(8,128)(2,1)S(1)}, u32[]{:S(2)}, u32[]{:S(2)}) collective-permute-start(bf16[2,3,16,1024]{3,2,1,0:T(8,128)(2,1)S(1)} %get-tuple-element.23.refs_0_), channel_id=1, source_target_pairs={{0,2},{1,3},{2,0},{3,1},{4,6},{5,7},{6,4},{7,5},{8,10},{9,11},{10,... | collective-permute-start | bytes 589832 | tf_op jit(solution)/shard_map/x02/ppermute | solution.py:286
  21.8 21.4 %collective-permute-start.1 = (bf16[3,64,1024]{2,1,0:T(8,128)(2,1)S(1)}, bf16[3,64,1024]{2,1,0:T(8,128)(2,1)S(1)}, u32[]{:S(2)}, u32[]{:S(2)}) collective-permute-start(bf16[3,64,1024]{2,1,0:T(8,128)(2,1)S(1)} %collective-permute-done.refs_2_), channel_id=1, source_target_pairs={{0,4},{4,12},{8,0},{12,20},{16,8},{20,28},{24,16},{28,24},{1,5},{5... | collective-permute-start | bytes 1179656 | tf_op jit(solution)/shard_map/d2/ppermute | solution.py:286
  24.3 18.9 %collective-permute-start.4 = (bf16[3,64,1024]{2,1,0:T(8,128)(2,1)S(1)}, bf16[3,64,1024]{2,1,0:T(8,128)(2,1)S(1)}, u32[]{:S(2)}, u32[]{:S(2)}) collective-permute-start(bf16[3,64,1024]{2,1,0:T(8,128)(2,1)S(1)} %collective-permute-done.3.refs_1_), channel_id=1, source_target_pairs={{0,8},{4,0},{8,16},{12,4},{16,24},{20,12},{24,28},{28,20},{1,9},{5... | collective-permute-start | bytes 1179656 | tf_op jit(solution)/shard_map/u2/ppermute | solution.py:286
  26.6 19.6 %collective-permute-start.9 = (bf16[4,3,16,1024]{3,2,1,0:T(8,128)(2,1)S(1)}, bf16[4,3,16,1024]{3,2,1,0:T(8,128)(2,1)S(1)}, u32[]{:S(2)}, u32[]{:S(2)}) collective-permute-start(bf16[4,3,16,1024]{3,2,1,0:T(8,128)(2,1)S(1)} %join.4.refs_0_), channel_id=1, source_target_pairs={{0,2},{1,3},{2,0},{3,1},{4,6},{5,7},{6,4},{7,5},{8,10},{9,11},{10,... | collective-permute-start | bytes 1179656 | tf_op jit(solution)/shard_map/x12/ppermute | solution.py:286
  28.1 15.1 %collective-permute-start.14 = (bf16[2,3,16,1024]{3,2,1,0:T(8,128)(2,1)S(1)}, bf16[2,3,16,1024]{3,2,1,0:T(8,128)(2,1)S(1)}, u32[]{:S(2)}, u32[]{:S(2)}) collective-permute-start(bf16[2,3,16,1024]{3,2,1,0:T(8,128)(2,1)S(1)} %get-tuple-element.29), channel_id=1, source_target_pairs={{0,16},{4,20},{8,24},{12,28},{16,0},{20,4},{24,8},{28,12},{1,17},{... | collective-permute-start | bytes 589832 | tf_op jit(solution)/shard_map/az2/ppermute | solution.py:286
  30.5 26.9 %collective-permute-start.12 = (bf16[4,3,16,1024]{3,2,1,0:T(8,128)(2,1)S(1)}, bf16[4,3,16,1024]{3,2,1,0:T(8,128)(2,1)S(1)}, u32[]{:S(2)}, u32[]{:S(2)}) collective-permute-start(bf16[4,3,16,1024]{3,2,1,0:T(8,128)(2,1)S(1)} %join.5.refs_1_), channel_id=1, source_target_pairs={{0,1},{1,0},{2,3},{3,2},{4,5},{5,4},{6,7},{7,6},{8,9},{9,8},{10,11... | collective-permute-start | bytes 1179656 | tf_op jit(solution)/shard_map/x01/ppermute | solution.py:286
  43.2 5.8 %collective-permute-start.15 = (bf16[2,3,16,1024]{3,2,1,0:T(8,128)(2,1)S(1)}, bf16[2,3,16,1024]{3,2,1,0:T(8,128)(2,1)S(1)}, u32[]{:S(2)}, u32[]{:S(2)}) collective-permute-start(bf16[2,3,16,1024]{3,2,1,0:T(8,128)(2,1)S(1)} %collective-permute-done.14.refs_0_), channel_id=1, source_target_pairs={{0,2},{1,3},{2,0},{3,1},{4,6},{5,7},{6,4},{7,5},{8,10},{9,11},{10,... | collective-permute-start | bytes 589832 | tf_op jit(solution)/shard_map/x22/ppermute | solution.py:286
  44.6 9.6 %collective-permute-start.2 = (bf16[3,64,1024]{2,1,0:T(8,128)(2,1)S(1)}, bf16[3,64,1024]{2,1,0:T(8,128)(2,1)S(1)}, u32[]{:S(2)}, u32[]{:S(2)}) collective-permute-start(bf16[3,64,1024]{2,1,0:T(8,128)(2,1)S(1)} %collective-permute-done.1.refs_0_), channel_id=1, source_target_pairs={{0,4},{4,12},{8,0},{12,20},{16,8},{20,28},{24,16},{28,24},{1,5},{5... | collective-permute-start | bytes 1179656 | tf_op jit(solution)/shard_map/d3/ppermute | solution.py:286
  46.2 9.7 %collective-permute-start.10 = (bf16[3,64,1024]{2,1,0:T(8,128)(2,1)S(1)}, bf16[3,64,1024]{2,1,0:T(8,128)(2,1)S(1)}, u32[]{:S(2)}, u32[]{:S(2)}) collective-permute-start(bf16[3,64,1024]{2,1,0:T(8,128)(2,1)S(1)} %collective-permute-done.4.refs_3_), channel_id=1, source_target_pairs={{0,8},{4,0},{8,16},{12,4},{16,24},{20,12},{24,28},{28,20},{1,9},{5... | collective-permute-start | bytes 1179656 | tf_op jit(solution)/shard_map/u3/ppermute | solution.py:286
  49.0 8.4 %collective-permute-start.16 = (bf16[4,3,16,1024]{3,2,1,0:T(8,128)(2,1)S(1)}, bf16[4,3,16,1024]{3,2,1,0:T(8,128)(2,1)S(1)}, u32[]{:S(2)}, u32[]{:S(2)}) collective-permute-start(bf16[4,3,16,1024]{3,2,1,0:T(8,128)(2,1)S(1)} %join.7.refs_5_), channel_id=1, source_target_pairs={{0,1},{1,0},{2,3},{3,2},{4,5},{5,4},{6,7},{7,6},{8,9},{9,8},{10,11... | collective-permute-start | bytes 1179656 | tf_op jit(solution)/shard_map/x21/ppermute | solution.py:286
  49.2 8.3 %collective-permute-start.13 = (bf16[8,3,16,1024]{3,2,1,0:T(8,128)(2,1)S(1)}, bf16[8,3,16,1024]{3,2,1,0:T(8,128)(2,1)S(1)}, u32[]{:S(2)}, u32[]{:S(2)}) collective-permute-start(bf16[8,3,16,1024]{3,2,1,0:T(8,128)(2,1)S(1)} %join.6.refs_3_), channel_id=1, source_target_pairs={{0,1},{1,0},{2,3},{3,2},{4,5},{5,4},{6,7},{7,6},{8,9},{9,8},{10,11... | collective-permute-start | bytes 2359304 | tf_op jit(solution)/shard_map/x11/ppermute | solution.py:286
  54.2 5.7 %collective-permute-start.17 = (bf16[1,64,1024]{2,1,0:T(8,128)(2,1)S(1)}, bf16[1,64,1024]{2,1,0:T(8,128)(2,1)S(1)}, u32[]{:S(2)}, u32[]{:S(2)}) collective-permute-start(bf16[1,64,1024]{2,1,0:T(8,128)(2,1)S(1)} %slice.9), channel_id=1, source_target_pairs={{0,4},{4,12},{8,0},{12,20},{16,8},{20,28},{24,16},{28,24},{1,5},{5... | collective-permute-start | bytes 393224 | tf_op jit(solution)/shard_map/d/ppermute | solution.py:286
  55.9 6.4 %collective-permute-start.11 = (bf16[2,64,1024]{2,1,0:T(8,128)(2,1)S(1)}, bf16[2,64,1024]{2,1,0:T(8,128)(2,1)S(1)}, u32[]{:S(2)}, u32[]{:S(2)}) collective-permute-start(bf16[2,64,1024]{2,1,0:T(8,128)(2,1)S(1)} %slice.8), channel_id=1, source_target_pairs={{0,8},{4,0},{8,16},{12,4},{16,24},{20,12},{24,28},{28,20},{1,9},{5... | collective-permute-start | bytes 786440 | tf_op jit(solution)/shard_map/u/ppermute | solution.py:286

commit v5 on v4

--- a/solution.py
+++ b/solution.py
@@ -8,7 +8,7 @@
 from jax.sharding import PartitionSpec as P
 
 BF, F32 = jnp.bfloat16, jnp.float32
-COSTS = {'turn_grads': 10000000000}
+COSTS = {'tg1': 10000000000, 'tg2': 10000000000}
 
 
 def cost(name):
@@ -211,7 +211,7 @@
                 )
 
 
-def turn_grads(pieces, parts):
+def turn_grads(name, pieces, parts):
     seqs, rows, width = pieces[0].shape
     shape = jax.ShapeDtypeStruct((seqs, width, len(pieces) * rows), BF)
     return pl.pallas_call(
@@ -220,7 +220,7 @@
         out_specs=VECTORS,
         out_shape=shape,
         compiler_params=pltpu.CompilerParams(vmem_limit_bytes=limit(shape, shape)),
-        cost_estimate=cost("turn_grads"),
+        cost_estimate=cost(name),
         name="turn_grads",
     )(*pieces, *parts)
 
@@ -228,17 +228,26 @@
 def multiply_kernel(scale, begin, count, first, second, high, low, acts, *refs):
     grads, before, out_ref = refs[:count], refs[count:-1], refs[-1]
     step = pl.program_id(0)
-    tile = high.shape[1]
+    tile, width = high.shape[1], acts.shape[2]
     columns = pl.ds(pl.multiple_of(step * tile, tile), tile)
-    total = before[0][columns, :] if before else None
+    turned = []
     for i in range(second.shape[0]):
         s = begin + i
         late = turn_pair(high[step], low[step], first[s, :, columns], second[i, :, columns])
-        turned = jnp.concatenate([*(g[s, columns, :] for g in grads), late], 1)
-        corr = dot(turned, acts[s], ((1,), (0,)))
-        square = corr * corr * scale
-        total = square if total is None else total + square
-    out_ref[(columns if out_ref.shape[0] > tile else slice(None)), :] = total
+        turned.append(jnp.concatenate([*(g[s, columns, :] for g in grads), late], 1))
+    for c in range(0, width, min(512, width)):
+        for r in range(0, tile, 256):
+            to = pl.ds(c, min(512, width))
+            total = None
+            for i in range(second.shape[0]):
+                corr = dot(turned[i][r : r + 256], acts[begin + i, :, to], ((1,), (0,)))
+                total = corr * corr if total is None else total + corr * corr
+            total = total * scale
+            rows = pl.ds(pl.multiple_of(step * tile + r, 256), 256)
+            if before:
+                out_ref[r : r + 256, to] = total + before[0][rows, to]
+            else:
+                out_ref[rows, to] = total
 
 
 def multiply(begin, last, parts, grads, acts, before=()):
@@ -263,7 +272,7 @@
     return lax.optimization_barrier((value, *earlier))[0]
 
 
-TIES = {'x22': ('u2', 'd2'), 'x12': ('x02',), 'az2': ('u1', 'd1'), 'u3': ('x12',)}
+TIES = {'az1': ('u1', 'd1'), 'az3': ('u1', 'd1'), 'az2': ('d2',), 'x12': ('x02',), 'x22': ('u2',)}
 
 
 def shards(acts, grads, act_basis, grad_basis):
@@ -356,8 +365,8 @@
     )
     turned = {"tg1": names[:-3], "tg2": names[-3:-1]}
     for name, of in turned.items():
-        ops[name] = lambda tie, of=of: turn_grads(
-            [tie(get(of[0]))] + [get(x) for x in of[1:]], get("spread")[1]
+        ops[name] = lambda tie, name=name, of=of: turn_grads(
+            name, [tie(get(of[0]))] + [get(x) for x in of[1:]], get("spread")[1]
         )
     late = get(names[-1])
     total = ()

time: 67.3 us -> 63.8 us (0.948)
  starting transfers between devices: 21.9 us -> 19.7 us
  waiting for transfers between devices: 28.9 us -> 27.8 us
    ppermute x18, starting transfers between devices: 21.9 us -> 19.7 us  [run(): return lax.ppermute(value, axis, perm)]
    ppermute x18, waiting for transfers between devices: 28.9 us -> 27.8 us  [run(): return lax.ppermute(value, axis, perm)]
  transfers between devices with their start and end apart: 18 -> 18, of which waited for: 8 -> 9; matrix products, arithmetic and copies ran while one was open for 0% -> 0% of each run, Pallas kernels for 14% -> 18%
where the time goes in v5:
time: 63.8 us; the launch traced here: 63.7 us
  waiting for transfers between devices  27.8 us (44%)
  starting transfers between devices  19.7 us (31%)
  Pallas kernels  15.8 us (25%)
    ppermute x18, waiting for transfers between devices, run(): return lax.ppermute(value, axis, perm)  27.8 us
    ppermute x18, starting transfers between devices, run(): return lax.ppermute(value, axis, perm)  19.7 us
    pallas_call x2, Pallas kernels, multiply(): pl.pallas_call(functools.partial(multiply_kernel, 1.0 / length, begin, le...  6.7 us
    pallas_call x2, Pallas kernels, turn_grads(): pl.pallas_call(turn_grads_kernel, in_specs=[VECTORS] * (len(pieces) + 2),...  2.78 us
    pallas_call x1, Pallas kernels, turn_acts(): pl.pallas_call(functools.partial(turn_acts_kernel, place_of, half, m, con...  2.54 us
    pallas_call x1, Pallas kernels, cut(): pl.pallas_call(cut_kernel, in_specs=[SCALARS, pl.BlockSpec(memory_space=p...  1.84 us
    pallas_call x1, Pallas kernels, spread(): pl.pallas_call(spread_kernel, out_shape=tuple(shapes), compiler_params=pl...  1.8 us
  transfers between devices with their start and end apart: 18, of which 9 were waited for; matrix products, arithmetic and copies ran while one was open for 0% of the time, Pallas kernels for 18%

profile of v5, /device:TPU:0, one launch (start us, length us, event | category | flops | bytes accessed | tf_op | source)
XLA Modules:
  0.0 63.7 jit_solution(16151676063467198149)
XLA Ops:
  0.0 3.0 %collective-permute-start = (bf16[3,64,1024]{2,1,0:T(8,128)(2,1)}, bf16[3,64,1024]{2,1,0:T(8,128)(2,1)S(1)}, u32[]{:S(2)}, u32[]{:S(2)}) collective-permute-start(bf16[3,64,1024]{2,1,0:T(8,128)(2,1)} %refs_0_.1), channel_id=1, source_target_pairs={{0,4},{4,12},{8,0},{12,20},{16,8},{20,28},{24,16},{28,24},{1,5},{5... | collective-permute-start | bytes 1179656 | tf_op jit(solution)/shard_map/d1/ppermute | solution.py:295
  3.0 0.1 collective-permute-start.3
  3.2 0.1 pad_add_fusion.where_ref
  3.2 1.8 %cut.1 = (bf16[4,3,16,1024]{3,2,1,0:T(8,128)(2,1)S(1)}, bf16[4,3,16,1024]{3,2,1,0:T(8,128)(2,1)S(1)}) custom-call(s32[3]{0:T(128)S(1)} %pad_add_fusion.where_ref, bf16[3,64,8192]{2,1,0:T(8,128)(2,1)} %acts_ref.1), custom_call_target="tpu_custom_call" | custom-call | tf_op jit(solution)/shard_map/cut/pallas_call | solution.py:108
  5.1 2.0 %collective-permute-start.7 = (bf16[4,3,16,1024]{3,2,1,0:T(8,128)(2,1)S(1)}, bf16[4,3,16,1024]{3,2,1,0:T(8,128)(2,1)S(1)}, u32[]{:S(2)}, u32[]{:S(2)}) collective-permute-start(bf16[4,3,16,1024]{3,2,1,0:T(8,128)(2,1)S(1)} %get-tuple-element.23), channel_id=1, source_target_pairs={{0,4},{4,0},{8,12},{12,8},{16,20},{20,16},{24,28},{28,24},{1,5},{5... | collective-permute-start | bytes 1179656 | tf_op jit(solution)/shard_map/ay/ppermute | solution.py:295
  7.0 5.8 %collective-permute-done.refs_2_ = bf16[3,64,1024]{2,1,0:T(8,128)(2,1)S(1)} collective-permute-done((bf16[3,64,1024]{2,1,0:T(8,128)(2,1)}, bf16[3,64,1024]{2,1,0:T(8,128)(2,1)S(1)}, u32[]{:S(2)}, u32[]{:S(2)}) %collective-permute-start) | collective-permute-done | bytes 393248 | tf_op jit(solution)/shard_map/d1/ppermute | solution.py:295
  12.9 2.4 %collective-permute-start.1 = (bf16[3,64,1024]{2,1,0:T(8,128)(2,1)S(1)}, bf16[3,64,1024]{2,1,0:T(8,128)(2,1)S(1)}, u32[]{:S(2)}, u32[]{:S(2)}) collective-permute-start(bf16[3,64,1024]{2,1,0:T(8,128)(2,1)S(1)} %collective-permute-done.refs_2_), channel_id=1, source_target_pairs={{0,4},{4,12},{8,0},{12,20},{16,8},{20,28},{24,16},{28,24},{1,5},{5... | collective-permute-start | bytes 1179656 | tf_op jit(solution)/shard_map/d2/ppermute | solution.py:295
  15.2 0.0 collective-permute-done.3.refs_1_
  15.3 0.0 collective-permute-start.4
  15.3 8.4 %collective-permute-done.7.came = bf16[4,3,16,1024]{3,2,1,0:T(8,128)(2,1)S(1)} collective-permute-done((bf16[4,3,16,1024]{3,2,1,0:T(8,128)(2,1)S(1)}, bf16[4,3,16,1024]{3,2,1,0:T(8,128)(2,1)S(1)}, u32[]{:S(2)}, u32[]{:S(2)}) %collective-permute-start.7) | collective-permute-done | bytes 393248 | tf_op jit(solution)/shard_map/ay/ppermute | solution.py:295
  23.7 0.1 pair.1
  23.8 2.1 %collective-permute-start.11 = (bf16[2,3,16,1024]{3,2,1,0:T(8,128)(2,1)S(1)}, bf16[2,3,16,1024]{3,2,1,0:T(8,128)(2,1)S(1)}, u32[]{:S(2)}, u32[]{:S(2)}) collective-permute-start(bf16[2,3,16,1024]{3,2,1,0:T(8,128)(2,1)S(1)} %get-tuple-element.28), channel_id=1, source_target_pairs={{0,24},{4,28},{8,0},{12,4},{16,8},{20,12},{24,16},{28,20},{1,25},{... | collective-permute-start | bytes 589832 | tf_op jit(solution)/shard_map/az3/ppermute | solution.py:295
  25.9 0.0 collective-permute-start.10
  25.9 1.5 %collective-permute-start.8 = (bf16[2,3,16,1024]{3,2,1,0:T(8,128)(2,1)S(1)}, bf16[2,3,16,1024]{3,2,1,0:T(8,128)(2,1)S(1)}, u32[]{:S(2)}, u32[]{:S(2)}) collective-permute-start(bf16[2,3,16,1024]{3,2,1,0:T(8,128)(2,1)S(1)} %get-tuple-element.24.refs_0_), channel_id=1, source_target_pairs={{0,2},{1,3},{2,0},{3,1},{4,6},{5,7},{6,4},{7,5},{8,10},{9,11},{10,... | collective-permute-start | bytes 589832 | tf_op jit(solution)/shard_map/x02/ppermute | solution.py:295
  27.4 1.1 %collective-permute-done.1.refs_0_ = bf16[3,64,1024]{2,1,0:T(8,128)(2,1)S(1)} collective-permute-done((bf16[3,64,1024]{2,1,0:T(8,128)(2,1)S(1)}, bf16[3,64,1024]{2,1,0:T(8,128)(2,1)S(1)}, u32[]{:S(2)}, u32[]{:S(2)}) %collective-permute-start.1) | collective-permute-done | bytes 393248 | tf_op jit(solution)/shard_map/d2/ppermute | solution.py:295
  28.5 0.0 collective-permute-start.14
  28.5 0.0 copy-done
  28.5 1.8 %spread.1 = (bf16[4,256,256]{2,1,0:T(8,128)(2,1)S(1)}, bf16[4,256,256]{2,1,0:T(8,128)(2,1)S(1)}, bf16[4,256,256]{2,1,0:T(8,128)(2,1)S(1)}, bf16[4,256,256]{2,1,0:T(8,128)(2,1)S(1)}) custom-call(f32[64,128]{1,0:T(8,128)S(1)} %bitcast.9, f32[64,128]{1,0:T(8,128)S(1)} %bitcast.10), custom_call_target="tpu_custom_call" | custom-call | tf_op jit(solution)/shard_map/spread/pallas_call | solution.py:77
  30.3 3.0 %collective-permute-done.11.refs_1_ = bf16[2,3,16,1024]{3,2,1,0:T(8,128)(2,1)S(1)} collective-permute-done((bf16[2,3,16,1024]{3,2,1,0:T(8,128)(2,1)S(1)}, bf16[2,3,16,1024]{3,2,1,0:T(8,128)(2,1)S(1)}, u32[]{:S(2)}, u32[]{:S(2)}) %collective-permute-start.11) | collective-permute-done | bytes 196640 | tf_op jit(solution)/shard_map/az3/ppermute | solution.py:295
  33.3 1.4 %collective-permute-done.10.refs_0_ = bf16[2,3,16,1024]{3,2,1,0:T(8,128)(2,1)S(1)} collective-permute-done((bf16[2,3,16,1024]{3,2,1,0:T(8,128)(2,1)S(1)}, bf16[2,3,16,1024]{3,2,1,0:T(8,128)(2,1)S(1)}, u32[]{:S(2)}, u32[]{:S(2)}) %collective-permute-start.10) | collective-permute-done | bytes 196640 | tf_op jit(solution)/shard_map/az1/ppermute | solution.py:295
  34.7 0.0 collective-permute-done.8.refs_1_
  34.7 0.1 collective-permute-start.9
  34.8 1.6 %collective-permute-start.12 = (bf16[4,3,16,1024]{3,2,1,0:T(8,128)(2,1)S(1)}, bf16[4,3,16,1024]{3,2,1,0:T(8,128)(2,1)S(1)}, u32[]{:S(2)}, u32[]{:S(2)}) collective-permute-start(bf16[4,3,16,1024]{3,2,1,0:T(8,128)(2,1)S(1)} %join.5.refs_0_), channel_id=1, source_target_pairs={{0,2},{1,3},{2,0},{3,1},{4,6},{5,7},{6,4},{7,5},{8,10},{9,11},{10,... | collective-permute-start | bytes 1179656 | tf_op jit(solution)/shard_map/x12/ppermute | solution.py:295
  36.4 3.3 %collective-permute-start.2 = (bf16[3,64,1024]{2,1,0:T(8,128)(2,1)S(1)}, bf16[3,64,1024]{2,1,0:T(8,128)(2,1)S(1)}, u32[]{:S(2)}, u32[]{:S(2)}) collective-permute-start(bf16[3,64,1024]{2,1,0:T(8,128)(2,1)S(1)} %collective-permute-done.1.refs_0_), channel_id=1, source_target_pairs={{0,4},{4,12},{8,0},{12,20},{16,8},{20,28},{24,16},{28,24},{1,5},{5... | collective-permute-start | bytes 1179656 | tf_op jit(solution)/shard_map/d3/ppermute | solution.py:295
  39.6 0.0 collective-permute-done.4.refs_3_
  39.7 0.0 collective-permute-start.5
  39.7 2.6 %collective-permute-done.14.refs_0_ = bf16[2,3,16,1024]{3,2,1,0:T(8,128)(2,1)S(1)} collective-permute-done((bf16[2,3,16,1024]{3,2,1,0:T(8,128)(2,1)S(1)}, bf16[2,3,16,1024]{3,2,1,0:T(8,128)(2,1)S(1)}, u32[]{:S(2)}, u32[]{:S(2)}) %collective-permute-start.14) | collective-permute-done | bytes 196640 | tf_op jit(solution)/shard_map/az2/ppermute | solution.py:295
  42.3 1.5 %collective-permute-start.15 = (bf16[2,3,16,1024]{3,2,1,0:T(8,128)(2,1)S(1)}, bf16[2,3,16,1024]{3,2,1,0:T(8,128)(2,1)S(1)}, u32[]{:S(2)}, u32[]{:S(2)}) collective-permute-start(bf16[2,3,16,1024]{3,2,1,0:T(8,128)(2,1)S(1)} %collective-permute-done.14.refs_0_), channel_id=1, source_target_pairs={{0,2},{1,3},{2,0},{3,1},{4,6},{5,7},{6,4},{7,5},{8,10},{9,11},{10,... | collective-permute-start | bytes 589832 | tf_op jit(solution)/shard_map/x22/ppermute | solution.py:295
  43.8 0.0 copy-done.2
  43.8 1.8 %turn_grads.2.refs_0_ = bf16[3,1024,256]{2,1,0:T(8,128)(2,1)S(1)} custom-call(bf16[3,64,1024]{2,1,0:T(8,128)(2,1)S(1)} %copy-done.2, bf16[3,64,1024]{2,1,0:T(8,128)(2,1)S(1)} %collective-permute-done.3.refs_1_, bf16[3,64,1024]{2,1,0:T(8,128)(2,1)S(1)} %collective-permute-done.refs_2_, bf16[3,64,1024]{2,1,0:T(8,128)(2,1)S(1)} %collective-permute-done.4.refs_3_, ...), custom_call_target="tpu_custom_call" | custom-call | flops 10000000000 | tf_op jit(solution)/shard_map/turn_grads/pallas_call | solution.py:217
  45.6 1.2 %collective-permute-done.12.refs_1_ = bf16[4,3,16,1024]{3,2,1,0:T(8,128)(2,1)S(1)} collective-permute-done((bf16[4,3,16,1024]{3,2,1,0:T(8,128)(2,1)S(1)}, bf16[4,3,16,1024]{3,2,1,0:T(8,128)(2,1)S(1)}, u32[]{:S(2)}, u32[]{:S(2)}) %collective-permute-start.12) | collective-permute-done | bytes 393248 | tf_op jit(solution)/shard_map/x12/ppermute | solution.py:295
  46.8 0.1 join.6.refs_3_
  46.9 0.1 collective-permute-start.13
  46.9 3.4 %collective-permute-done.2.first = bf16[3,64,1024]{2,1,0:T(8,128)(2,1)S(1)} collective-permute-done((bf16[3,64,1024]{2,1,0:T(8,128)(2,1)S(1)}, bf16[3,64,1024]{2,1,0:T(8,128)(2,1)S(1)}, u32[]{:S(2)}, u32[]{:S(2)}) %collective-permute-start.2) | collective-permute-done | bytes 393248 | tf_op jit(solution)/shard_map/d3/ppermute | solution.py:295
  50.4 0.5 collective-permute-start.17
  50.9 0.0 collective-permute-done.5.refs_1_
  50.9 1.6 %collective-permute-start.6 = (bf16[2,64,1024]{2,1,0:T(8,128)(2,1)S(1)}, bf16[2,64,1024]{2,1,0:T(8,128)(2,1)S(1)}, u32[]{:S(2)}, u32[]{:S(2)}) collective-permute-start(bf16[2,64,1024]{2,1,0:T(8,128)(2,1)S(1)} %slice.8), channel_id=1, source_target_pairs={{0,8},{4,0},{8,16},{12,4},{16,24},{20,12},{24,28},{28,20},{1,9},{5... | collective-permute-start | bytes 786440 | tf_op jit(solution)/shard_map/u/ppermute | solution.py:295
  52.5 0.0 collective-permute-done.15.refs_1_
  52.6 0.1 collective-permute-start.16
  52.7 1.0 %turn_grads.3.refs_1_ = bf16[3,1024,128]{2,1,0:T(8,128)(2,1)S(1)} custom-call(bf16[3,64,1024]{2,1,0:T(8,128)(2,1)S(1)} %collective-permute-done.1.refs_0_, bf16[3,64,1024]{2,1,0:T(8,128)(2,1)S(1)} %collective-permute-done.5.refs_1_, bf16[4,256,256]{2,1,0:T(8,128)(2,1)S(1)} %get-tuple-element.20.refs_4_.refs_2_.high, ...), custom_call_target="tpu_custom_call" | custom-call | flops 10000000000 | tf_op jit(solution)/shard_map/turn_grads/pallas_call | solution.py:217
  53.7 0.0 collective-permute-done.9.refs_0_
  53.7 0.7 %collective-permute-done.16.refs_4_ = bf16[4,3,16,1024]{3,2,1,0:T(8,128)(2,1)S(1)} collective-permute-done((bf16[4,3,16,1024]{3,2,1,0:T(8,128)(2,1)S(1)}, bf16[4,3,16,1024]{3,2,1,0:T(8,128)(2,1)S(1)}, u32[]{:S(2)}, u32[]{:S(2)}) %collective-permute-start.16) | collective-permute-done | bytes 393248 | tf_op jit(solution)/shard_map/x21/ppermute | solution.py:295
  54.4 0.0 collective-permute-done.13.refs_2_
  54.4 2.5 %turn_acts.1.acts = bf16[3,512,1024]{2,1,0:T(8,128)(2,1)S(1)} custom-call(s32[3]{0:T(128)S(1)} %pad_add_fusion.where_ref, bf16[4,3,16,1024]{3,2,1,0:T(8,128)(2,1)S(1)} %collective-permute-done.9.refs_0_, bf16[4,3,16,1024]{3,2,1,0:T(8,128)(2,1)S(1)} %join.4.refs_1_, bf16[8,3,16,1024]{3,2,1,0:T(8,128)(2,1)S(1)} %collective-permute-done.13.refs_2_, ...), custom_call_target="tpu_custom_call" | custom-call | tf_op jit(solution)/shard_map/turn_acts/pallas_call | solution.py:185
  56.9 0.0 collective-permute-done.17.second
  56.9 2.1 %multiply.2.refs_2_ = f32[1024,1024]{1,0:T(8,128)S(1)} custom-call(bf16[3,64,1024]{2,1,0:T(8,128)(2,1)S(1)} %collective-permute-done.2.first, bf16[1,64,1024]{2,1,0:T(8,128)(2,1)S(1)} %collective-permute-done.17.second, bf16[4,256,256]{2,1,0:T(8,128)(2,1)S(1)} %get-tuple-element.20.refs_4_.refs_2_.high, ...), custom_call_target="tpu_custom_call" | custom-call | tf_op jit(solution)/shard_map/multiply/pallas_call | solution.py:259
  59.0 0.0 collective-permute-done.6.second
  59.1 4.6 %multiply.3 = f32[1024,1024]{1,0:T(8,128)} custom-call(bf16[3,64,1024]{2,1,0:T(8,128)(2,1)S(1)} %collective-permute-done.2.first, bf16[2,64,1024]{2,1,0:T(8,128)(2,1)S(1)} %collective-permute-done.6.second, bf16[4,256,256]{2,1,0:T(8,128)(2,1)S(1)} %get-tuple-element.20.refs_4_.refs_2_.high, bf16[4,256,256]{2,1,0:T(8,128)(2,1)S(1)} %get-tuple-element.21.refs_5_.refs_3_.low, ...), custom_call_target="tpu_custom_call" | custom-call | tf_op jit(solution)/shard_map/multiply/pallas_call | solution.py:259
  (9 shorter events, 0.1 us)
Async XLA Ops:
  0.0 43.8 %copy-start.2 = (bf16[3,64,1024]{2,1,0:T(8,128)(2,1)S(1)}, bf16[3,64,1024]{2,1,0:T(8,128)(2,1)}, u32[]{:S(2)}) copy-start(bf16[3,64,1024]{2,1,0:T(8,128)(2,1)} %refs_0_.1) | copy-start | bytes 1179652
  0.0 28.5 %copy-start.1 = (f32[128,8,8]{0,2,1:T(8,128)S(1)}, f32[128,8,8]{0,2,1:T(8,128)}, u32[]{:S(2)}) copy-start(f32[128,8,8]{0,2,1:T(8,128)} %param.7) | copy-start | bytes 98308
  0.0 28.5 %copy-start = (f32[128,8,8]{0,2,1:T(8,128)S(1)}, f32[128,8,8]{0,2,1:T(8,128)}, u32[]{:S(2)}) copy-start(f32[128,8,8]{0,2,1:T(8,128)} %param.6) | copy-start | bytes 98308
  0.0 12.9 %collective-permute-start = (bf16[3,64,1024]{2,1,0:T(8,128)(2,1)}, bf16[3,64,1024]{2,1,0:T(8,128)(2,1)S(1)}, u32[]{:S(2)}, u32[]{:S(2)}) collective-permute-start(bf16[3,64,1024]{2,1,0:T(8,128)(2,1)} %refs_0_.1), channel_id=1, source_target_pairs={{0,4},{4,12},{8,0},{12,20},{16,8},{20,28},{24,16},{28,24},{1,5},{5... | collective-permute-start | bytes 1179656 | tf_op jit(solution)/shard_map/d1/ppermute | solution.py:295
  3.0 12.2 %collective-permute-start.3 = (bf16[3,64,1024]{2,1,0:T(8,128)(2,1)}, bf16[3,64,1024]{2,1,0:T(8,128)(2,1)S(1)}, u32[]{:S(2)}, u32[]{:S(2)}) collective-permute-start(bf16[3,64,1024]{2,1,0:T(8,128)(2,1)} %refs_0_.1), channel_id=1, source_target_pairs={{0,8},{4,0},{8,16},{12,4},{16,24},{20,12},{24,28},{28,20},{1,9},{5... | collective-permute-start | bytes 1179656 | tf_op jit(solution)/shard_map/u1/ppermute | solution.py:295
  5.1 18.6 %collective-permute-start.7 = (bf16[4,3,16,1024]{3,2,1,0:T(8,128)(2,1)S(1)}, bf16[4,3,16,1024]{3,2,1,0:T(8,128)(2,1)S(1)}, u32[]{:S(2)}, u32[]{:S(2)}) collective-permute-start(bf16[4,3,16,1024]{3,2,1,0:T(8,128)(2,1)S(1)} %get-tuple-element.23), channel_id=1, source_target_pairs={{0,4},{4,0},{8,12},{12,8},{16,20},{20,16},{24,28},{28,24},{1,5},{5... | collective-permute-start | bytes 1179656 | tf_op jit(solution)/shard_map/ay/ppermute | solution.py:295
  12.9 15.6 %collective-permute-start.1 = (bf16[3,64,1024]{2,1,0:T(8,128)(2,1)S(1)}, bf16[3,64,1024]{2,1,0:T(8,128)(2,1)S(1)}, u32[]{:S(2)}, u32[]{:S(2)}) collective-permute-start(bf16[3,64,1024]{2,1,0:T(8,128)(2,1)S(1)} %collective-permute-done.refs_2_), channel_id=1, source_target_pairs={{0,4},{4,12},{8,0},{12,20},{16,8},{20,28},{24,16},{28,24},{1,5},{5... | collective-permute-start | bytes 1179656 | tf_op jit(solution)/shard_map/d2/ppermute | solution.py:295
  15.3 24.4 %collective-permute-start.4 = (bf16[3,64,1024]{2,1,0:T(8,128)(2,1)S(1)}, bf16[3,64,1024]{2,1,0:T(8,128)(2,1)S(1)}, u32[]{:S(2)}, u32[]{:S(2)}) collective-permute-start(bf16[3,64,1024]{2,1,0:T(8,128)(2,1)S(1)} %collective-permute-done.3.refs_1_), channel_id=1, source_target_pairs={{0,8},{4,0},{8,16},{12,4},{16,24},{20,12},{24,28},{28,20},{1,9},{5... | collective-permute-start | bytes 1179656 | tf_op jit(solution)/shard_map/u2/ppermute | solution.py:295
  23.8 9.5 %collective-permute-start.11 = (bf16[2,3,16,1024]{3,2,1,0:T(8,128)(2,1)S(1)}, bf16[2,3,16,1024]{3,2,1,0:T(8,128)(2,1)S(1)}, u32[]{:S(2)}, u32[]{:S(2)}) collective-permute-start(bf16[2,3,16,1024]{3,2,1,0:T(8,128)(2,1)S(1)} %get-tuple-element.28), channel_id=1, source_target_pairs={{0,24},{4,28},{8,0},{12,4},{16,8},{20,12},{24,16},{28,20},{1,25},{... | collective-permute-start | bytes 589832 | tf_op jit(solution)/shard_map/az3/ppermute | solution.py:295
  25.9 8.8 %collective-permute-start.10 = (bf16[2,3,16,1024]{3,2,1,0:T(8,128)(2,1)S(1)}, bf16[2,3,16,1024]{3,2,1,0:T(8,128)(2,1)S(1)}, u32[]{:S(2)}, u32[]{:S(2)}) collective-permute-start(bf16[2,3,16,1024]{3,2,1,0:T(8,128)(2,1)S(1)} %get-tuple-element.26), channel_id=1, source_target_pairs={{0,8},{4,12},{8,16},{12,20},{16,24},{20,28},{24,0},{28,4},{1,9},{5... | collective-permute-start | bytes 589832 | tf_op jit(solution)/shard_map/az1/ppermute | solution.py:295
  25.9 8.8 %collective-permute-start.8 = (bf16[2,3,16,1024]{3,2,1,0:T(8,128)(2,1)S(1)}, bf16[2,3,16,1024]{3,2,1,0:T(8,128)(2,1)S(1)}, u32[]{:S(2)}, u32[]{:S(2)}) collective-permute-start(bf16[2,3,16,1024]{3,2,1,0:T(8,128)(2,1)S(1)} %get-tuple-element.24.refs_0_), channel_id=1, source_target_pairs={{0,2},{1,3},{2,0},{3,1},{4,6},{5,7},{6,4},{7,5},{8,10},{9,11},{10,... | collective-permute-start | bytes 589832 | tf_op jit(solution)/shard_map/x02/ppermute | solution.py:295
  28.5 13.8 %collective-permute-start.14 = (bf16[2,3,16,1024]{3,2,1,0:T(8,128)(2,1)S(1)}, bf16[2,3,16,1024]{3,2,1,0:T(8,128)(2,1)S(1)}, u32[]{:S(2)}, u32[]{:S(2)}) collective-permute-start(bf16[2,3,16,1024]{3,2,1,0:T(8,128)(2,1)S(1)} %get-tuple-element.31), channel_id=1, source_target_pairs={{0,16},{4,20},{8,24},{12,28},{16,0},{20,4},{24,8},{28,12},{1,17},{... | collective-permute-start | bytes 589832 | tf_op jit(solution)/shard_map/az2/ppermute | solution.py:295
  34.7 18.9 %collective-permute-start.9 = (bf16[4,3,16,1024]{3,2,1,0:T(8,128)(2,1)S(1)}, bf16[4,3,16,1024]{3,2,1,0:T(8,128)(2,1)S(1)}, u32[]{:S(2)}, u32[]{:S(2)}) collective-permute-start(bf16[4,3,16,1024]{3,2,1,0:T(8,128)(2,1)S(1)} %join.4.refs_1_), channel_id=1, source_target_pairs={{0,1},{1,0},{2,3},{3,2},{4,5},{5,4},{6,7},{7,6},{8,9},{9,8},{10,11... | collective-permute-start | bytes 1179656 | tf_op jit(solution)/shard_map/x01/ppermute | solution.py:295
  34.8 12.0 %collective-permute-start.12 = (bf16[4,3,16,1024]{3,2,1,0:T(8,128)(2,1)S(1)}, bf16[4,3,16,1024]{3,2,1,0:T(8,128)(2,1)S(1)}, u32[]{:S(2)}, u32[]{:S(2)}) collective-permute-start(bf16[4,3,16,1024]{3,2,1,0:T(8,128)(2,1)S(1)} %join.5.refs_0_), channel_id=1, source_target_pairs={{0,2},{1,3},{2,0},{3,1},{4,6},{5,7},{6,4},{7,5},{8,10},{9,11},{10,... | collective-permute-start | bytes 1179656 | tf_op jit(solution)/shard_map/x12/ppermute | solution.py:295
  36.4 14.0 %collective-permute-start.2 = (bf16[3,64,1024]{2,1,0:T(8,128)(2,1)S(1)}, bf16[3,64,1024]{2,1,0:T(8,128)(2,1)S(1)}, u32[]{:S(2)}, u32[]{:S(2)}) collective-permute-start(bf16[3,64,1024]{2,1,0:T(8,128)(2,1)S(1)} %collective-permute-done.1.refs_0_), channel_id=1, source_target_pairs={{0,4},{4,12},{8,0},{12,20},{16,8},{20,28},{24,16},{28,24},{1,5},{5... | collective-permute-start | bytes 1179656 | tf_op jit(solution)/shard_map/d3/ppermute | solution.py:295
  39.7 11.3 %collective-permute-start.5 = (bf16[3,64,1024]{2,1,0:T(8,128)(2,1)S(1)}, bf16[3,64,1024]{2,1,0:T(8,128)(2,1)S(1)}, u32[]{:S(2)}, u32[]{:S(2)}) collective-permute-start(bf16[3,64,1024]{2,1,0:T(8,128)(2,1)S(1)} %collective-permute-done.4.refs_3_), channel_id=1, source_target_pairs={{0,8},{4,0},{8,16},{12,4},{16,24},{20,12},{24,28},{28,20},{1,9},{5... | collective-permute-start | bytes 1179656 | tf_op jit(solution)/shard_map/u3/ppermute | solution.py:295
  42.3 10.3 %collective-permute-start.15 = (bf16[2,3,16,1024]{3,2,1,0:T(8,128)(2,1)S(1)}, bf16[2,3,16,1024]{3,2,1,0:T(8,128)(2,1)S(1)}, u32[]{:S(2)}, u32[]{:S(2)}) collective-permute-start(bf16[2,3,16,1024]{3,2,1,0:T(8,128)(2,1)S(1)} %collective-permute-done.14.refs_0_), channel_id=1, source_target_pairs={{0,2},{1,3},{2,0},{3,1},{4,6},{5,7},{6,4},{7,5},{8,10},{9,11},{10,... | collective-permute-start | bytes 589832 | tf_op jit(solution)/shard_map/x22/ppermute | solution.py:295
  46.9 7.5 %collective-permute-start.13 = (bf16[8,3,16,1024]{3,2,1,0:T(8,128)(2,1)S(1)}, bf16[8,3,16,1024]{3,2,1,0:T(8,128)(2,1)S(1)}, u32[]{:S(2)}, u32[]{:S(2)}) collective-permute-start(bf16[8,3,16,1024]{3,2,1,0:T(8,128)(2,1)S(1)} %join.6.refs_3_), channel_id=1, source_target_pairs={{0,1},{1,0},{2,3},{3,2},{4,5},{5,4},{6,7},{7,6},{8,9},{9,8},{10,11... | collective-permute-start | bytes 2359304 | tf_op jit(solution)/shard_map/x11/ppermute | solution.py:295
  50.4 6.5 %collective-permute-start.17 = (bf16[1,64,1024]{2,1,0:T(8,128)(2,1)S(1)}, bf16[1,64,1024]{2,1,0:T(8,128)(2,1)S(1)}, u32[]{:S(2)}, u32[]{:S(2)}) collective-permute-start(bf16[1,64,1024]{2,1,0:T(8,128)(2,1)S(1)} %slice.9), channel_id=1, source_target_pairs={{0,4},{4,12},{8,0},{12,20},{16,8},{20,28},{24,16},{28,24},{1,5},{5... | collective-permute-start | bytes 393224 | tf_op jit(solution)/shard_map/d/ppermute | solution.py:295
  50.9 8.1 %collective-permute-start.6 = (bf16[2,64,1024]{2,1,0:T(8,128)(2,1)S(1)}, bf16[2,64,1024]{2,1,0:T(8,128)(2,1)S(1)}, u32[]{:S(2)}, u32[]{:S(2)}) collective-permute-start(bf16[2,64,1024]{2,1,0:T(8,128)(2,1)S(1)} %slice.8), channel_id=1, source_target_pairs={{0,8},{4,0},{8,16},{12,4},{16,24},{20,12},{24,28},{28,20},{1,9},{5... | collective-permute-start | bytes 786440 | tf_op jit(solution)/shard_map/u/ppermute | solution.py:295
  52.6 1.8 %collective-permute-start.16 = (bf16[4,3,16,1024]{3,2,1,0:T(8,128)(2,1)S(1)}, bf16[4,3,16,1024]{3,2,1,0:T(8,128)(2,1)S(1)}, u32[]{:S(2)}, u32[]{:S(2)}) collective-permute-start(bf16[4,3,16,1024]{3,2,1,0:T(8,128)(2,1)S(1)} %join.7.refs_5_), channel_id=1, source_target_pairs={{0,1},{1,0},{2,3},{3,2},{4,5},{5,4},{6,7},{7,6},{8,9},{9,8},{10,11... | collective-permute-start | bytes 1179656 | tf_op jit(solution)/shard_map/x21/ppermute | solution.py:295

commit v6 on v5

--- a/solution.py
+++ b/solution.py
@@ -8,7 +8,7 @@
 from jax.sharding import PartitionSpec as P
 
 BF, F32 = jnp.bfloat16, jnp.float32
-COSTS = {'tg1': 10000000000, 'tg2': 10000000000}
+COSTS = {'tg1': 10000000000, 'tg2': 10000000000, 'turn_acts': 2000000000}
 
 
 def cost(name):
@@ -229,25 +229,24 @@
     grads, before, out_ref = refs[:count], refs[count:-1], refs[-1]
     step = pl.program_id(0)
     tile, width = high.shape[1], acts.shape[2]
-    columns = pl.ds(pl.multiple_of(step * tile, tile), tile)
+    rows = pl.ds(pl.multiple_of(step * tile, tile), tile)
+    to = rows if out_ref.shape[0] > tile else slice(None)
     turned = []
     for i in range(second.shape[0]):
         s = begin + i
-        late = turn_pair(high[step], low[step], first[s, :, columns], second[i, :, columns])
-        turned.append(jnp.concatenate([*(g[s, columns, :] for g in grads), late], 1))
-    for c in range(0, width, min(512, width)):
-        for r in range(0, tile, 256):
-            to = pl.ds(c, min(512, width))
-            total = None
-            for i in range(second.shape[0]):
-                corr = dot(turned[i][r : r + 256], acts[begin + i, :, to], ((1,), (0,)))
-                total = corr * corr if total is None else total + corr * corr
-            total = total * scale
-            rows = pl.ds(pl.multiple_of(step * tile + r, 256), 256)
-            if before:
-                out_ref[r : r + 256, to] = total + before[0][rows, to]
-            else:
-                out_ref[rows, to] = total
+        late = turn_pair(high[step], low[step], first[s, :, rows], second[i, :, rows])
+        turned.append(jnp.concatenate([*(g[s, rows, :] for g in grads), late], 1))
+    block = min(512, width)
+    for c in range(0, width, block):
+        columns = pl.ds(c, block)
+        total = None
+        for i, left in enumerate(turned):
+            corr = dot(left, acts[begin + i, :, columns], ((1,), (0,)))
+            total = corr * corr if total is None else total + corr * corr
+        total = total * scale
+        if before:
+            total = total + before[0][rows, columns]
+        out_ref[to, columns] = total
 
 
 def multiply(begin, last, parts, grads, acts, before=()):
@@ -272,7 +271,7 @@
     return lax.optimization_barrier((value, *earlier))[0]
 
 
-TIES = {'az1': ('u1', 'd1'), 'az3': ('u1', 'd1'), 'az2': ('d2',), 'x12': ('x02',), 'x22': ('u2',)}
+TIES = {'az1': ('u1', 'd1'), 'az3': ('d1',), 'az2': ('d2',), 'x22': ('u2',), 'u': ('d1',), 'x11': ('u2',), 'x21': ('az1',)}
 
 
 def shards(acts, grads, act_basis, grad_basis):

time: 63.8 us -> 63.1 us (0.989)
  starting transfers between devices: 19.7 us -> 16.4 us
  waiting for transfers between devices: 27.8 us -> 30.3 us
    ppermute x18, starting transfers between devices: 19.7 us -> 16.4 us  [run(): return lax.ppermute(value, axis, perm)]
    ppermute x18, waiting for transfers between devices: 27.8 us -> 30.3 us  [run(): return lax.ppermute(value, axis, perm)]
  transfers between devices with their start and end apart: 18 -> 18, of which waited for: 9 -> 8; matrix products, arithmetic and copies ran while one was open for 0% -> 0% of each run, Pallas kernels for 18% -> 18%
where the time goes in v6:
time: 63.1 us; the launch traced here: 62.9 us
  waiting for transfers between devices  30.3 us (48%)
  starting transfers between devices  16.4 us (26%)
  Pallas kernels  15.9 us (25%)
    ppermute x18, waiting for transfers between devices, run(): return lax.ppermute(value, axis, perm)  30.3 us
    ppermute x18, starting transfers between devices, run(): return lax.ppermute(value, axis, perm)  16.4 us
    pallas_call x2, Pallas kernels, multiply(): pl.pallas_call(functools.partial(multiply_kernel, 1.0 / length, begin, le...  6.72 us
    pallas_call x2, Pallas kernels, turn_grads(): pl.pallas_call(turn_grads_kernel, in_specs=[VECTORS] * (len(pieces) + 2),...  2.77 us
    pallas_call x1, Pallas kernels, turn_acts(): pl.pallas_call(functools.partial(turn_acts_kernel, place_of, half, m, con...  2.53 us
    pallas_call x1, Pallas kernels, cut(): pl.pallas_call(cut_kernel, in_specs=[SCALARS, pl.BlockSpec(memory_space=p...  1.84 us
    pallas_call x1, Pallas kernels, spread(): pl.pallas_call(spread_kernel, out_shape=tuple(shapes), compiler_params=pl...  1.8 us
  transfers between devices with their start and end apart: 18, of which 8 were waited for; matrix products, arithmetic and copies ran while one was open for 0% of the time, Pallas kernels for 18%

profile of v6, /device:TPU:0, one launch (start us, length us, event | category | flops | bytes accessed | tf_op | source)
XLA Modules:
  0.0 62.9 jit_solution(16467948011938436926)
XLA Ops:
  0.0 3.0 %collective-permute-start = (bf16[3,64,1024]{2,1,0:T(8,128)(2,1)}, bf16[3,64,1024]{2,1,0:T(8,128)(2,1)S(1)}, u32[]{:S(2)}, u32[]{:S(2)}) collective-permute-start(bf16[3,64,1024]{2,1,0:T(8,128)(2,1)} %refs_0_.1), channel_id=1, source_target_pairs={{0,4},{4,12},{8,0},{12,20},{16,8},{20,28},{24,16},{28,24},{1,5},{5... | collective-permute-start | bytes 1179656 | tf_op jit(solution)/shard_map/d1/ppermute | solution.py:294
  3.0 0.1 collective-permute-start.3
  3.2 0.1 pad_add_fusion.where_ref
  3.2 1.8 %cut.1 = (bf16[4,3,16,1024]{3,2,1,0:T(8,128)(2,1)S(1)}, bf16[4,3,16,1024]{3,2,1,0:T(8,128)(2,1)S(1)}) custom-call(s32[3]{0:T(128)S(1)} %pad_add_fusion.where_ref, bf16[3,64,8192]{2,1,0:T(8,128)(2,1)} %acts_ref.1), custom_call_target="tpu_custom_call" | custom-call | tf_op jit(solution)/shard_map/cut/pallas_call | solution.py:108
  5.1 2.0 %collective-permute-start.7 = (bf16[4,3,16,1024]{3,2,1,0:T(8,128)(2,1)S(1)}, bf16[4,3,16,1024]{3,2,1,0:T(8,128)(2,1)S(1)}, u32[]{:S(2)}, u32[]{:S(2)}) collective-permute-start(bf16[4,3,16,1024]{3,2,1,0:T(8,128)(2,1)S(1)} %get-tuple-element.26), channel_id=1, source_target_pairs={{0,4},{4,0},{8,12},{12,8},{16,20},{20,16},{24,28},{28,24},{1,5},{5... | collective-permute-start | bytes 1179656 | tf_op jit(solution)/shard_map/ay/ppermute | solution.py:294
  7.0 5.8 %collective-permute-done.refs_2_ = bf16[3,64,1024]{2,1,0:T(8,128)(2,1)S(1)} collective-permute-done((bf16[3,64,1024]{2,1,0:T(8,128)(2,1)}, bf16[3,64,1024]{2,1,0:T(8,128)(2,1)S(1)}, u32[]{:S(2)}, u32[]{:S(2)}) %collective-permute-start) | collective-permute-done | bytes 393248 | tf_op jit(solution)/shard_map/d1/ppermute | solution.py:294
  12.9 2.4 %collective-permute-start.1 = (bf16[3,64,1024]{2,1,0:T(8,128)(2,1)S(1)}, bf16[3,64,1024]{2,1,0:T(8,128)(2,1)S(1)}, u32[]{:S(2)}, u32[]{:S(2)}) collective-permute-start(bf16[3,64,1024]{2,1,0:T(8,128)(2,1)S(1)} %collective-permute-done.refs_2_), channel_id=1, source_target_pairs={{0,4},{4,12},{8,0},{12,20},{16,8},{20,28},{24,16},{28,24},{1,5},{5... | collective-permute-start | bytes 1179656 | tf_op jit(solution)/shard_map/d2/ppermute | solution.py:294
  15.2 0.0 collective-permute-done.3.refs_1_
  15.3 0.0 collective-permute-start.4
  15.3 8.4 %collective-permute-done.7.came = bf16[4,3,16,1024]{3,2,1,0:T(8,128)(2,1)S(1)} collective-permute-done((bf16[4,3,16,1024]{3,2,1,0:T(8,128)(2,1)S(1)}, bf16[4,3,16,1024]{3,2,1,0:T(8,128)(2,1)S(1)}, u32[]{:S(2)}, u32[]{:S(2)}) %collective-permute-start.7) | collective-permute-done | bytes 393248 | tf_op jit(solution)/shard_map/ay/ppermute | solution.py:294
  23.7 0.1 pair.1
  23.8 1.6 %collective-permute-start.8 = (bf16[2,3,16,1024]{3,2,1,0:T(8,128)(2,1)S(1)}, bf16[2,3,16,1024]{3,2,1,0:T(8,128)(2,1)S(1)}, u32[]{:S(2)}, u32[]{:S(2)}) collective-permute-start(bf16[2,3,16,1024]{3,2,1,0:T(8,128)(2,1)S(1)} %get-tuple-element.27.refs_0_), channel_id=1, source_target_pairs={{0,2},{1,3},{2,0},{3,1},{4,6},{5,7},{6,4},{7,5},{8,10},{9,11},{10,... | collective-permute-start | bytes 589832 | tf_op jit(solution)/shard_map/x02/ppermute | solution.py:294
  25.3 2.0 %collective-permute-start.11 = (bf16[2,3,16,1024]{3,2,1,0:T(8,128)(2,1)S(1)}, bf16[2,3,16,1024]{3,2,1,0:T(8,128)(2,1)S(1)}, u32[]{:S(2)}, u32[]{:S(2)}) collective-permute-start(bf16[2,3,16,1024]{3,2,1,0:T(8,128)(2,1)S(1)} %get-tuple-element.31), channel_id=1, source_target_pairs={{0,24},{4,28},{8,0},{12,4},{16,8},{20,12},{24,16},{28,20},{1,25},{... | collective-permute-start | bytes 589832 | tf_op jit(solution)/shard_map/az3/ppermute | solution.py:294
  27.4 0.0 collective-permute-start.10
  27.4 1.1 %collective-permute-done.1.refs_0_ = bf16[3,64,1024]{2,1,0:T(8,128)(2,1)S(1)} collective-permute-done((bf16[3,64,1024]{2,1,0:T(8,128)(2,1)S(1)}, bf16[3,64,1024]{2,1,0:T(8,128)(2,1)S(1)}, u32[]{:S(2)}, u32[]{:S(2)}) %collective-permute-start.1) | collective-permute-done | bytes 393248 | tf_op jit(solution)/shard_map/d2/ppermute | solution.py:294
  28.5 0.0 collective-permute-start.14
  28.5 0.0 copy-done.1
  28.5 0.0 copy-done
  28.5 1.8 %spread.1 = (bf16[4,256,256]{2,1,0:T(8,128)(2,1)S(1)}, bf16[4,256,256]{2,1,0:T(8,128)(2,1)S(1)}, bf16[4,256,256]{2,1,0:T(8,128)(2,1)S(1)}, bf16[4,256,256]{2,1,0:T(8,128)(2,1)S(1)}) custom-call(f32[64,128]{1,0:T(8,128)S(1)} %bitcast.9, f32[64,128]{1,0:T(8,128)S(1)} %bitcast.10), custom_call_target="tpu_custom_call" | custom-call | tf_op jit(solution)/shard_map/spread/pallas_call | solution.py:77
  30.3 0.0 collective-permute-done.8.refs_1_
  30.3 0.1 collective-permute-start.9
  30.4 4.8 %collective-permute-done.11.refs_1_ = bf16[2,3,16,1024]{3,2,1,0:T(8,128)(2,1)S(1)} collective-permute-done((bf16[2,3,16,1024]{3,2,1,0:T(8,128)(2,1)S(1)}, bf16[2,3,16,1024]{3,2,1,0:T(8,128)(2,1)S(1)}, u32[]{:S(2)}, u32[]{:S(2)}) %collective-permute-start.11) | collective-permute-done | bytes 196640 | tf_op jit(solution)/shard_map/az3/ppermute | solution.py:294
  35.2 2.0 %collective-permute-done.10.refs_0_ = bf16[2,3,16,1024]{3,2,1,0:T(8,128)(2,1)S(1)} collective-permute-done((bf16[2,3,16,1024]{3,2,1,0:T(8,128)(2,1)S(1)}, bf16[2,3,16,1024]{3,2,1,0:T(8,128)(2,1)S(1)}, u32[]{:S(2)}, u32[]{:S(2)}) %collective-permute-start.10) | collective-permute-done | bytes 196640 | tf_op jit(solution)/shard_map/az1/ppermute | solution.py:294
  37.2 0.1 collective-permute-start.12
  37.3 2.2 %collective-permute-start.2 = (bf16[3,64,1024]{2,1,0:T(8,128)(2,1)S(1)}, bf16[3,64,1024]{2,1,0:T(8,128)(2,1)S(1)}, u32[]{:S(2)}, u32[]{:S(2)}) collective-permute-start(bf16[3,64,1024]{2,1,0:T(8,128)(2,1)S(1)} %collective-permute-done.1.refs_0_), channel_id=1, source_target_pairs={{0,4},{4,12},{8,0},{12,20},{16,8},{20,28},{24,16},{28,24},{1,5},{5... | collective-permute-start | bytes 1179656 | tf_op jit(solution)/shard_map/d3/ppermute | solution.py:294
  39.5 0.0 collective-permute-done.4.refs_3_
  39.5 0.0 collective-permute-start.5
  39.5 4.1 %collective-permute-done.14.refs_0_ = bf16[2,3,16,1024]{3,2,1,0:T(8,128)(2,1)S(1)} collective-permute-done((bf16[2,3,16,1024]{3,2,1,0:T(8,128)(2,1)S(1)}, bf16[2,3,16,1024]{3,2,1,0:T(8,128)(2,1)S(1)}, u32[]{:S(2)}, u32[]{:S(2)}) %collective-permute-start.14) | collective-permute-done | bytes 196640 | tf_op jit(solution)/shard_map/az2/ppermute | solution.py:294
  43.7 0.7 %collective-permute-start.15 = (bf16[2,3,16,1024]{3,2,1,0:T(8,128)(2,1)S(1)}, bf16[2,3,16,1024]{3,2,1,0:T(8,128)(2,1)S(1)}, u32[]{:S(2)}, u32[]{:S(2)}) collective-permute-start(bf16[2,3,16,1024]{3,2,1,0:T(8,128)(2,1)S(1)} %collective-permute-done.14.refs_0_), channel_id=1, source_target_pairs={{0,2},{1,3},{2,0},{3,1},{4,6},{5,7},{6,4},{7,5},{8,10},{9,11},{10,... | collective-permute-start | bytes 589832 | tf_op jit(solution)/shard_map/x22/ppermute | solution.py:294
  44.4 1.8 %turn_grads.2.refs_0_ = bf16[3,1024,256]{2,1,0:T(8,128)(2,1)S(1)} custom-call(bf16[3,64,1024]{2,1,0:T(8,128)(2,1)S(1)} %copy-done.2, bf16[3,64,1024]{2,1,0:T(8,128)(2,1)S(1)} %collective-permute-done.3.refs_1_, bf16[3,64,1024]{2,1,0:T(8,128)(2,1)S(1)} %collective-permute-done.refs_2_, bf16[3,64,1024]{2,1,0:T(8,128)(2,1)S(1)} %collective-permute-done.4.refs_3_, ...), custom_call_target="tpu_custom_call" | custom-call | flops 10000000000 | tf_op jit(solution)/shard_map/turn_grads/pallas_call | solution.py:217
  46.2 0.0 collective-permute-done.12.refs_1_
  46.2 0.1 join.6.refs_3_
  46.2 0.1 collective-permute-start.13
  46.3 3.3 %collective-permute-done.2.first = bf16[3,64,1024]{2,1,0:T(8,128)(2,1)S(1)} collective-permute-done((bf16[3,64,1024]{2,1,0:T(8,128)(2,1)S(1)}, bf16[3,64,1024]{2,1,0:T(8,128)(2,1)S(1)}, u32[]{:S(2)}, u32[]{:S(2)}) %collective-permute-start.2) | collective-permute-done | bytes 393248 | tf_op jit(solution)/shard_map/d3/ppermute | solution.py:294
  49.6 0.1 collective-permute-start.17
  49.7 0.0 collective-permute-done.5.refs_1_
  49.7 2.1 %collective-permute-start.6 = (bf16[2,64,1024]{2,1,0:T(8,128)(2,1)S(1)}, bf16[2,64,1024]{2,1,0:T(8,128)(2,1)S(1)}, u32[]{:S(2)}, u32[]{:S(2)}) collective-permute-start(bf16[2,64,1024]{2,1,0:T(8,128)(2,1)S(1)} %slice.8), channel_id=1, source_target_pairs={{0,8},{4,0},{8,16},{12,4},{16,24},{20,12},{24,28},{28,20},{1,9},{5... | collective-permute-start | bytes 786440 | tf_op jit(solution)/shard_map/u/ppermute | solution.py:294
  51.8 0.0 collective-permute-done.15.refs_1_
  51.8 0.1 collective-permute-start.16
  51.9 1.0 %turn_grads.3.refs_1_ = bf16[3,1024,128]{2,1,0:T(8,128)(2,1)S(1)} custom-call(bf16[3,64,1024]{2,1,0:T(8,128)(2,1)S(1)} %collective-permute-done.1.refs_0_, bf16[3,64,1024]{2,1,0:T(8,128)(2,1)S(1)} %collective-permute-done.5.refs_1_, bf16[4,256,256]{2,1,0:T(8,128)(2,1)S(1)} %get-tuple-element.23.refs_4_.refs_2_.high, ...), custom_call_target="tpu_custom_call" | custom-call | flops 10000000000 | tf_op jit(solution)/shard_map/turn_grads/pallas_call | solution.py:217
  52.9 0.0 collective-permute-done.9.refs_0_
  52.9 0.7 %collective-permute-done.16.refs_4_ = bf16[4,3,16,1024]{3,2,1,0:T(8,128)(2,1)S(1)} collective-permute-done((bf16[4,3,16,1024]{3,2,1,0:T(8,128)(2,1)S(1)}, bf16[4,3,16,1024]{3,2,1,0:T(8,128)(2,1)S(1)}, u32[]{:S(2)}, u32[]{:S(2)}) %collective-permute-start.16) | collective-permute-done | bytes 393248 | tf_op jit(solution)/shard_map/x21/ppermute | solution.py:294
  53.6 0.0 collective-permute-done.13.refs_2_
  53.6 2.5 %turn_acts.1.acts = bf16[3,512,1024]{2,1,0:T(8,128)(2,1)S(1)} custom-call(s32[3]{0:T(128)S(1)} %pad_add_fusion.where_ref, bf16[4,3,16,1024]{3,2,1,0:T(8,128)(2,1)S(1)} %collective-permute-done.9.refs_0_, bf16[4,3,16,1024]{3,2,1,0:T(8,128)(2,1)S(1)} %join.4.refs_1_, bf16[8,3,16,1024]{3,2,1,0:T(8,128)(2,1)S(1)} %collective-permute-done.13.refs_2_, ...), custom_call_target="tpu_custom_call" | custom-call | flops 2000000000 | tf_op jit(solution)/shard_map/turn_acts/pallas_call | solution.py:185
  56.2 0.0 collective-permute-done.17.second
  56.2 2.1 %multiply.2.refs_2_ = f32[1024,1024]{1,0:T(8,128)S(1)} custom-call(bf16[3,64,1024]{2,1,0:T(8,128)(2,1)S(1)} %collective-permute-done.2.first, bf16[1,64,1024]{2,1,0:T(8,128)(2,1)S(1)} %collective-permute-done.17.second, bf16[4,256,256]{2,1,0:T(8,128)(2,1)S(1)} %get-tuple-element.23.refs_4_.refs_2_.high, ...), custom_call_target="tpu_custom_call" | custom-call | tf_op jit(solution)/shard_map/multiply/pallas_call | solution.py:258
  58.3 0.0 collective-permute-done.6.second
  58.3 4.6 %multiply.3 = f32[1024,1024]{1,0:T(8,128)} custom-call(bf16[3,64,1024]{2,1,0:T(8,128)(2,1)S(1)} %collective-permute-done.2.first, bf16[2,64,1024]{2,1,0:T(8,128)(2,1)S(1)} %collective-permute-done.6.second, bf16[4,256,256]{2,1,0:T(8,128)(2,1)S(1)} %get-tuple-element.23.refs_4_.refs_2_.high, bf16[4,256,256]{2,1,0:T(8,128)(2,1)S(1)} %get-tuple-element.24.refs_5_.refs_3_.low, ...), custom_call_target="tpu_custom_call" | custom-call | tf_op jit(solution)/shard_map/multiply/pallas_call | solution.py:258
  (9 shorter events, 0.1 us)
Async XLA Ops:
  0.0 44.4 %copy-start.2 = (bf16[3,64,1024]{2,1,0:T(8,128)(2,1)S(1)}, bf16[3,64,1024]{2,1,0:T(8,128)(2,1)}, u32[]{:S(2)}) copy-start(bf16[3,64,1024]{2,1,0:T(8,128)(2,1)} %refs_0_.1) | copy-start | bytes 1179652
  0.0 28.5 %copy-start.1 = (f32[128,8,8]{0,2,1:T(8,128)S(1)}, f32[128,8,8]{0,2,1:T(8,128)}, u32[]{:S(2)}) copy-start(f32[128,8,8]{0,2,1:T(8,128)} %param.7) | copy-start | bytes 98308
  0.0 28.5 %copy-start = (f32[128,8,8]{0,2,1:T(8,128)S(1)}, f32[128,8,8]{0,2,1:T(8,128)}, u32[]{:S(2)}) copy-start(f32[128,8,8]{0,2,1:T(8,128)} %param.6) | copy-start | bytes 98308
  0.0 12.9 %collective-permute-start = (bf16[3,64,1024]{2,1,0:T(8,128)(2,1)}, bf16[3,64,1024]{2,1,0:T(8,128)(2,1)S(1)}, u32[]{:S(2)}, u32[]{:S(2)}) collective-permute-start(bf16[3,64,1024]{2,1,0:T(8,128)(2,1)} %refs_0_.1), channel_id=1, source_target_pairs={{0,4},{4,12},{8,0},{12,20},{16,8},{20,28},{24,16},{28,24},{1,5},{5... | collective-permute-start | bytes 1179656 | tf_op jit(solution)/shard_map/d1/ppermute | solution.py:294
  3.0 12.2 %collective-permute-start.3 = (bf16[3,64,1024]{2,1,0:T(8,128)(2,1)}, bf16[3,64,1024]{2,1,0:T(8,128)(2,1)S(1)}, u32[]{:S(2)}, u32[]{:S(2)}) collective-permute-start(bf16[3,64,1024]{2,1,0:T(8,128)(2,1)} %refs_0_.1), channel_id=1, source_target_pairs={{0,8},{4,0},{8,16},{12,4},{16,24},{20,12},{24,28},{28,20},{1,9},{5... | collective-permute-start | bytes 1179656 | tf_op jit(solution)/shard_map/u1/ppermute | solution.py:294
  5.1 18.6 %collective-permute-start.7 = (bf16[4,3,16,1024]{3,2,1,0:T(8,128)(2,1)S(1)}, bf16[4,3,16,1024]{3,2,1,0:T(8,128)(2,1)S(1)}, u32[]{:S(2)}, u32[]{:S(2)}) collective-permute-start(bf16[4,3,16,1024]{3,2,1,0:T(8,128)(2,1)S(1)} %get-tuple-element.26), channel_id=1, source_target_pairs={{0,4},{4,0},{8,12},{12,8},{16,20},{20,16},{24,28},{28,24},{1,5},{5... | collective-permute-start | bytes 1179656 | tf_op jit(solution)/shard_map/ay/ppermute | solution.py:294
  12.9 15.6 %collective-permute-start.1 = (bf16[3,64,1024]{2,1,0:T(8,128)(2,1)S(1)}, bf16[3,64,1024]{2,1,0:T(8,128)(2,1)S(1)}, u32[]{:S(2)}, u32[]{:S(2)}) collective-permute-start(bf16[3,64,1024]{2,1,0:T(8,128)(2,1)S(1)} %collective-permute-done.refs_2_), channel_id=1, source_target_pairs={{0,4},{4,12},{8,0},{12,20},{16,8},{20,28},{24,16},{28,24},{1,5},{5... | collective-permute-start | bytes 1179656 | tf_op jit(solution)/shard_map/d2/ppermute | solution.py:294
  15.3 24.2 %collective-permute-start.4 = (bf16[3,64,1024]{2,1,0:T(8,128)(2,1)S(1)}, bf16[3,64,1024]{2,1,0:T(8,128)(2,1)S(1)}, u32[]{:S(2)}, u32[]{:S(2)}) collective-permute-start(bf16[3,64,1024]{2,1,0:T(8,128)(2,1)S(1)} %collective-permute-done.3.refs_1_), channel_id=1, source_target_pairs={{0,8},{4,0},{8,16},{12,4},{16,24},{20,12},{24,28},{28,20},{1,9},{5... | collective-permute-start | bytes 1179656 | tf_op jit(solution)/shard_map/u2/ppermute | solution.py:294
  23.8 6.5 %collective-permute-start.8 = (bf16[2,3,16,1024]{3,2,1,0:T(8,128)(2,1)S(1)}, bf16[2,3,16,1024]{3,2,1,0:T(8,128)(2,1)S(1)}, u32[]{:S(2)}, u32[]{:S(2)}) collective-permute-start(bf16[2,3,16,1024]{3,2,1,0:T(8,128)(2,1)S(1)} %get-tuple-element.27.refs_0_), channel_id=1, source_target_pairs={{0,2},{1,3},{2,0},{3,1},{4,6},{5,7},{6,4},{7,5},{8,10},{9,11},{10,... | collective-permute-start | bytes 589832 | tf_op jit(solution)/shard_map/x02/ppermute | solution.py:294
  25.3 9.9 %collective-permute-start.11 = (bf16[2,3,16,1024]{3,2,1,0:T(8,128)(2,1)S(1)}, bf16[2,3,16,1024]{3,2,1,0:T(8,128)(2,1)S(1)}, u32[]{:S(2)}, u32[]{:S(2)}) collective-permute-start(bf16[2,3,16,1024]{3,2,1,0:T(8,128)(2,1)S(1)} %get-tuple-element.31), channel_id=1, source_target_pairs={{0,24},{4,28},{8,0},{12,4},{16,8},{20,12},{24,16},{28,20},{1,25},{... | collective-permute-start | bytes 589832 | tf_op jit(solution)/shard_map/az3/ppermute | solution.py:294
  27.4 9.9 %collective-permute-start.10 = (bf16[2,3,16,1024]{3,2,1,0:T(8,128)(2,1)S(1)}, bf16[2,3,16,1024]{3,2,1,0:T(8,128)(2,1)S(1)}, u32[]{:S(2)}, u32[]{:S(2)}) collective-permute-start(bf16[2,3,16,1024]{3,2,1,0:T(8,128)(2,1)S(1)} %get-tuple-element.29), channel_id=1, source_target_pairs={{0,8},{4,12},{8,16},{12,20},{16,24},{20,28},{24,0},{28,4},{1,9},{5... | collective-permute-start | bytes 589832 | tf_op jit(solution)/shard_map/az1/ppermute | solution.py:294
  28.5 15.2 %collective-permute-start.14 = (bf16[2,3,16,1024]{3,2,1,0:T(8,128)(2,1)S(1)}, bf16[2,3,16,1024]{3,2,1,0:T(8,128)(2,1)S(1)}, u32[]{:S(2)}, u32[]{:S(2)}) collective-permute-start(bf16[2,3,16,1024]{3,2,1,0:T(8,128)(2,1)S(1)} %get-tuple-element.34), channel_id=1, source_target_pairs={{0,16},{4,20},{8,24},{12,28},{16,0},{20,4},{24,8},{28,12},{1,17},{... | collective-permute-start | bytes 589832 | tf_op jit(solution)/shard_map/az2/ppermute | solution.py:294
  30.3 22.6 %collective-permute-start.9 = (bf16[4,3,16,1024]{3,2,1,0:T(8,128)(2,1)S(1)}, bf16[4,3,16,1024]{3,2,1,0:T(8,128)(2,1)S(1)}, u32[]{:S(2)}, u32[]{:S(2)}) collective-permute-start(bf16[4,3,16,1024]{3,2,1,0:T(8,128)(2,1)S(1)} %join.4.refs_1_), channel_id=1, source_target_pairs={{0,1},{1,0},{2,3},{3,2},{4,5},{5,4},{6,7},{7,6},{8,9},{9,8},{10,11... | collective-permute-start | bytes 1179656 | tf_op jit(solution)/shard_map/x01/ppermute | solution.py:294
  37.2 8.9 %collective-permute-start.12 = (bf16[4,3,16,1024]{3,2,1,0:T(8,128)(2,1)S(1)}, bf16[4,3,16,1024]{3,2,1,0:T(8,128)(2,1)S(1)}, u32[]{:S(2)}, u32[]{:S(2)}) collective-permute-start(bf16[4,3,16,1024]{3,2,1,0:T(8,128)(2,1)S(1)} %join.5.refs_0_), channel_id=1, source_target_pairs={{0,2},{1,3},{2,0},{3,1},{4,6},{5,7},{6,4},{7,5},{8,10},{9,11},{10,... | collective-permute-start | bytes 1179656 | tf_op jit(solution)/shard_map/x12/ppermute | solution.py:294
  37.3 12.3 %collective-permute-start.2 = (bf16[3,64,1024]{2,1,0:T(8,128)(2,1)S(1)}, bf16[3,64,1024]{2,1,0:T(8,128)(2,1)S(1)}, u32[]{:S(2)}, u32[]{:S(2)}) collective-permute-start(bf16[3,64,1024]{2,1,0:T(8,128)(2,1)S(1)} %collective-permute-done.1.refs_0_), channel_id=1, source_target_pairs={{0,4},{4,12},{8,0},{12,20},{16,8},{20,28},{24,16},{28,24},{1,5},{5... | collective-permute-start | bytes 1179656 | tf_op jit(solution)/shard_map/d3/ppermute | solution.py:294
  39.5 10.1 %collective-permute-start.5 = (bf16[3,64,1024]{2,1,0:T(8,128)(2,1)S(1)}, bf16[3,64,1024]{2,1,0:T(8,128)(2,1)S(1)}, u32[]{:S(2)}, u32[]{:S(2)}) collective-permute-start(bf16[3,64,1024]{2,1,0:T(8,128)(2,1)S(1)} %collective-permute-done.4.refs_3_), channel_id=1, source_target_pairs={{0,8},{4,0},{8,16},{12,4},{16,24},{20,12},{24,28},{28,20},{1,9},{5... | collective-permute-start | bytes 1179656 | tf_op jit(solution)/shard_map/u3/ppermute | solution.py:294
  43.7 8.1 %collective-permute-start.15 = (bf16[2,3,16,1024]{3,2,1,0:T(8,128)(2,1)S(1)}, bf16[2,3,16,1024]{3,2,1,0:T(8,128)(2,1)S(1)}, u32[]{:S(2)}, u32[]{:S(2)}) collective-permute-start(bf16[2,3,16,1024]{3,2,1,0:T(8,128)(2,1)S(1)} %collective-permute-done.14.refs_0_), channel_id=1, source_target_pairs={{0,2},{1,3},{2,0},{3,1},{4,6},{5,7},{6,4},{7,5},{8,10},{9,11},{10,... | collective-permute-start | bytes 589832 | tf_op jit(solution)/shard_map/x22/ppermute | solution.py:294
  46.2 7.4 %collective-permute-start.13 = (bf16[8,3,16,1024]{3,2,1,0:T(8,128)(2,1)S(1)}, bf16[8,3,16,1024]{3,2,1,0:T(8,128)(2,1)S(1)}, u32[]{:S(2)}, u32[]{:S(2)}) collective-permute-start(bf16[8,3,16,1024]{3,2,1,0:T(8,128)(2,1)S(1)} %join.6.refs_3_), channel_id=1, source_target_pairs={{0,1},{1,0},{2,3},{3,2},{4,5},{5,4},{6,7},{7,6},{8,9},{9,8},{10,11... | collective-permute-start | bytes 2359304 | tf_op jit(solution)/shard_map/x11/ppermute | solution.py:294
  49.6 6.6 %collective-permute-start.17 = (bf16[1,64,1024]{2,1,0:T(8,128)(2,1)S(1)}, bf16[1,64,1024]{2,1,0:T(8,128)(2,1)S(1)}, u32[]{:S(2)}, u32[]{:S(2)}) collective-permute-start(bf16[1,64,1024]{2,1,0:T(8,128)(2,1)S(1)} %slice.9), channel_id=1, source_target_pairs={{0,4},{4,12},{8,0},{12,20},{16,8},{20,28},{24,16},{28,24},{1,5},{5... | collective-permute-start | bytes 393224 | tf_op jit(solution)/shard_map/d/ppermute | solution.py:294
  49.7 8.6 %collective-permute-start.6 = (bf16[2,64,1024]{2,1,0:T(8,128)(2,1)S(1)}, bf16[2,64,1024]{2,1,0:T(8,128)(2,1)S(1)}, u32[]{:S(2)}, u32[]{:S(2)}) collective-permute-start(bf16[2,64,1024]{2,1,0:T(8,128)(2,1)S(1)} %slice.8), channel_id=1, source_target_pairs={{0,8},{4,0},{8,16},{12,4},{16,24},{20,12},{24,28},{28,20},{1,9},{5... | collective-permute-start | bytes 786440 | tf_op jit(solution)/shard_map/u/ppermute | solution.py:294
  51.8 1.8 %collective-permute-start.16 = (bf16[4,3,16,1024]{3,2,1,0:T(8,128)(2,1)S(1)}, bf16[4,3,16,1024]{3,2,1,0:T(8,128)(2,1)S(1)}, u32[]{:S(2)}, u32[]{:S(2)}) collective-permute-start(bf16[4,3,16,1024]{3,2,1,0:T(8,128)(2,1)S(1)} %join.7.refs_5_), channel_id=1, source_target_pairs={{0,1},{1,0},{2,3},{3,2},{4,5},{5,4},{6,7},{7,6},{8,9},{9,8},{10,11... | collective-permute-start | bytes 1179656 | tf_op jit(solution)/shard_map/x21/ppermute | solution.py:294

commit v7 on v6

--- a/solution.py
+++ b/solution.py
@@ -8,7 +8,7 @@
 from jax.sharding import PartitionSpec as P
 
 BF, F32 = jnp.bfloat16, jnp.float32
-COSTS = {'tg1': 10000000000, 'tg2': 10000000000, 'turn_acts': 2000000000}
+COSTS = {'tg1': 10000000000, 'tg2': 10000000000, 'turn_acts': 2000000000, 'spread': 2000000000}
 
 
 def cost(name):
@@ -271,7 +271,7 @@
     return lax.optimization_barrier((value, *earlier))[0]
 
 
-TIES = {'az1': ('u1', 'd1'), 'az3': ('d1',), 'az2': ('d2',), 'x22': ('u2',), 'u': ('d1',), 'x11': ('u2',), 'x21': ('az1',)}
+TIES = {'az1': ('u1', 'd1'), 'az3': ('d1',), 'az2': ('d2',), 'u': ('d1',), 'x11': ('u2',), 'x21': ('az1',), 'u2': ('u1',), 'x01': ('x02',)}
 
 
 def shards(acts, grads, act_basis, grad_basis):

time: 63.1 us -> 63 us (level)
  no operation moved by 1% of the time
where the time goes in v7:
time: 63 us; the launch traced here: 62.9 us
  waiting for transfers between devices  30.3 us (48%)
  starting transfers between devices  16.4 us (26%)
  Pallas kernels  15.9 us (25%)
    ppermute x18, waiting for transfers between devices, run(): return lax.ppermute(value, axis, perm)  30.3 us
    ppermute x18, starting transfers between devices, run(): return lax.ppermute(value, axis, perm)  16.4 us
    pallas_call x2, Pallas kernels, multiply(): pl.pallas_call(functools.partial(multiply_kernel, 1.0 / length, begin, le...  6.73 us
    pallas_call x2, Pallas kernels, turn_grads(): pl.pallas_call(turn_grads_kernel, in_specs=[VECTORS] * (len(pieces) + 2),...  2.78 us
    pallas_call x1, Pallas kernels, turn_acts(): pl.pallas_call(functools.partial(turn_acts_kernel, place_of, half, m, con...  2.54 us
    pallas_call x1, Pallas kernels, cut(): pl.pallas_call(cut_kernel, in_specs=[SCALARS, pl.BlockSpec(memory_space=p...  1.84 us
    pallas_call x1, Pallas kernels, spread(): pl.pallas_call(spread_kernel, out_shape=tuple(shapes), compiler_params=pl...  1.8 us
  transfers between devices with their start and end apart: 18, of which 8 were waited for; matrix products, arithmetic and copies ran while one was open for 0% of the time, Pallas kernels for 18%

profile of v7, /device:TPU:0, one launch (start us, length us, event | category | flops | bytes accessed | tf_op | source)
XLA Modules:
  0.0 62.9 jit_solution(13854362059998368783)
XLA Ops:
  0.0 3.0 %collective-permute-start = (bf16[3,64,1024]{2,1,0:T(8,128)(2,1)}, bf16[3,64,1024]{2,1,0:T(8,128)(2,1)S(1)}, u32[]{:S(2)}, u32[]{:S(2)}) collective-permute-start(bf16[3,64,1024]{2,1,0:T(8,128)(2,1)} %refs_0_.1), channel_id=1, source_target_pairs={{0,4},{4,12},{8,0},{12,20},{16,8},{20,28},{24,16},{28,24},{1,5},{5... | collective-permute-start | bytes 1179656 | tf_op jit(solution)/shard_map/d1/ppermute | solution.py:294
  3.0 0.1 collective-permute-start.3
  3.1 0.1 pad_add_fusion.where_ref
  3.2 1.8 %cut.1 = (bf16[4,3,16,1024]{3,2,1,0:T(8,128)(2,1)S(1)}, bf16[4,3,16,1024]{3,2,1,0:T(8,128)(2,1)S(1)}) custom-call(s32[3]{0:T(128)S(1)} %pad_add_fusion.where_ref, bf16[3,64,8192]{2,1,0:T(8,128)(2,1)} %acts_ref.1), custom_call_target="tpu_custom_call" | custom-call | tf_op jit(solution)/shard_map/cut/pallas_call | solution.py:108
  5.0 2.0 %collective-permute-start.7 = (bf16[4,3,16,1024]{3,2,1,0:T(8,128)(2,1)S(1)}, bf16[4,3,16,1024]{3,2,1,0:T(8,128)(2,1)S(1)}, u32[]{:S(2)}, u32[]{:S(2)}) collective-permute-start(bf16[4,3,16,1024]{3,2,1,0:T(8,128)(2,1)S(1)} %get-tuple-element.28), channel_id=1, source_target_pairs={{0,4},{4,0},{8,12},{12,8},{16,20},{20,16},{24,28},{28,24},{1,5},{5... | collective-permute-start | bytes 1179656 | tf_op jit(solution)/shard_map/ay/ppermute | solution.py:294
  7.0 5.8 %collective-permute-done.refs_2_ = bf16[3,64,1024]{2,1,0:T(8,128)(2,1)S(1)} collective-permute-done((bf16[3,64,1024]{2,1,0:T(8,128)(2,1)}, bf16[3,64,1024]{2,1,0:T(8,128)(2,1)S(1)}, u32[]{:S(2)}, u32[]{:S(2)}) %collective-permute-start) | collective-permute-done | bytes 393248 | tf_op jit(solution)/shard_map/d1/ppermute | solution.py:294
  12.8 2.4 %collective-permute-start.1 = (bf16[3,64,1024]{2,1,0:T(8,128)(2,1)S(1)}, bf16[3,64,1024]{2,1,0:T(8,128)(2,1)S(1)}, u32[]{:S(2)}, u32[]{:S(2)}) collective-permute-start(bf16[3,64,1024]{2,1,0:T(8,128)(2,1)S(1)} %collective-permute-done.refs_2_), channel_id=1, source_target_pairs={{0,4},{4,12},{8,0},{12,20},{16,8},{20,28},{24,16},{28,24},{1,5},{5... | collective-permute-start | bytes 1179656 | tf_op jit(solution)/shard_map/d2/ppermute | solution.py:294
  15.2 0.0 collective-permute-done.3.refs_1_
  15.2 0.0 collective-permute-start.4
  15.2 8.4 %collective-permute-done.7.came = bf16[4,3,16,1024]{3,2,1,0:T(8,128)(2,1)S(1)} collective-permute-done((bf16[4,3,16,1024]{3,2,1,0:T(8,128)(2,1)S(1)}, bf16[4,3,16,1024]{3,2,1,0:T(8,128)(2,1)S(1)}, u32[]{:S(2)}, u32[]{:S(2)}) %collective-permute-start.7) | collective-permute-done | bytes 393248 | tf_op jit(solution)/shard_map/ay/ppermute | solution.py:294
  23.6 0.1 pair.1
  23.7 1.6 %collective-permute-start.8 = (bf16[2,3,16,1024]{3,2,1,0:T(8,128)(2,1)S(1)}, bf16[2,3,16,1024]{3,2,1,0:T(8,128)(2,1)S(1)}, u32[]{:S(2)}, u32[]{:S(2)}) collective-permute-start(bf16[2,3,16,1024]{3,2,1,0:T(8,128)(2,1)S(1)} %get-tuple-element.29.refs_0_), channel_id=1, source_target_pairs={{0,2},{1,3},{2,0},{3,1},{4,6},{5,7},{6,4},{7,5},{8,10},{9,11},{10,... | collective-permute-start | bytes 589832 | tf_op jit(solution)/shard_map/x02/ppermute | solution.py:294
  25.3 2.0 %collective-permute-start.11 = (bf16[2,3,16,1024]{3,2,1,0:T(8,128)(2,1)S(1)}, bf16[2,3,16,1024]{3,2,1,0:T(8,128)(2,1)S(1)}, u32[]{:S(2)}, u32[]{:S(2)}) collective-permute-start(bf16[2,3,16,1024]{3,2,1,0:T(8,128)(2,1)S(1)} %get-tuple-element.34), channel_id=1, source_target_pairs={{0,24},{4,28},{8,0},{12,4},{16,8},{20,12},{24,16},{28,20},{1,25},{... | collective-permute-start | bytes 589832 | tf_op jit(solution)/shard_map/az3/ppermute | solution.py:294
  27.3 0.0 collective-permute-start.10
  27.3 1.1 %collective-permute-done.1.refs_0_ = bf16[3,64,1024]{2,1,0:T(8,128)(2,1)S(1)} collective-permute-done((bf16[3,64,1024]{2,1,0:T(8,128)(2,1)S(1)}, bf16[3,64,1024]{2,1,0:T(8,128)(2,1)S(1)}, u32[]{:S(2)}, u32[]{:S(2)}) %collective-permute-start.1) | collective-permute-done | bytes 393248 | tf_op jit(solution)/shard_map/d2/ppermute | solution.py:294
  28.4 0.0 collective-permute-start.14
  28.4 0.0 copy-done.2
  28.4 0.0 copy-done.1
  28.4 1.8 %spread.1 = (bf16[4,256,256]{2,1,0:T(8,128)(2,1)S(1)}, bf16[4,256,256]{2,1,0:T(8,128)(2,1)S(1)}, bf16[4,256,256]{2,1,0:T(8,128)(2,1)S(1)}, bf16[4,256,256]{2,1,0:T(8,128)(2,1)S(1)}) custom-call(f32[64,128]{1,0:T(8,128)S(1)} %bitcast.9, f32[64,128]{1,0:T(8,128)S(1)} %bitcast.10), custom_call_target="tpu_custom_call" | custom-call | flops 2000000000 | tf_op jit(solution)/shard_map/spread/pallas_call | solution.py:77
  30.2 0.0 collective-permute-done.8.refs_1_
  30.3 0.1 collective-permute-start.9
  30.4 4.8 %collective-permute-done.11.refs_1_ = bf16[2,3,16,1024]{3,2,1,0:T(8,128)(2,1)S(1)} collective-permute-done((bf16[2,3,16,1024]{3,2,1,0:T(8,128)(2,1)S(1)}, bf16[2,3,16,1024]{3,2,1,0:T(8,128)(2,1)S(1)}, u32[]{:S(2)}, u32[]{:S(2)}) %collective-permute-start.11) | collective-permute-done | bytes 196640 | tf_op jit(solution)/shard_map/az3/ppermute | solution.py:294
  35.1 2.0 %collective-permute-done.10.refs_0_ = bf16[2,3,16,1024]{3,2,1,0:T(8,128)(2,1)S(1)} collective-permute-done((bf16[2,3,16,1024]{3,2,1,0:T(8,128)(2,1)S(1)}, bf16[2,3,16,1024]{3,2,1,0:T(8,128)(2,1)S(1)}, u32[]{:S(2)}, u32[]{:S(2)}) %collective-permute-start.10) | collective-permute-done | bytes 196640 | tf_op jit(solution)/shard_map/az1/ppermute | solution.py:294
  37.2 0.1 collective-permute-start.12
  37.3 2.2 %collective-permute-start.2 = (bf16[3,64,1024]{2,1,0:T(8,128)(2,1)S(1)}, bf16[3,64,1024]{2,1,0:T(8,128)(2,1)S(1)}, u32[]{:S(2)}, u32[]{:S(2)}) collective-permute-start(bf16[3,64,1024]{2,1,0:T(8,128)(2,1)S(1)} %collective-permute-done.1.refs_0_), channel_id=1, source_target_pairs={{0,4},{4,12},{8,0},{12,20},{16,8},{20,28},{24,16},{28,24},{1,5},{5... | collective-permute-start | bytes 1179656 | tf_op jit(solution)/shard_map/d3/ppermute | solution.py:294
  39.5 0.0 collective-permute-done.4.refs_3_
  39.5 0.0 collective-permute-start.5
  39.5 4.1 %collective-permute-done.14.refs_0_ = bf16[2,3,16,1024]{3,2,1,0:T(8,128)(2,1)S(1)} collective-permute-done((bf16[2,3,16,1024]{3,2,1,0:T(8,128)(2,1)S(1)}, bf16[2,3,16,1024]{3,2,1,0:T(8,128)(2,1)S(1)}, u32[]{:S(2)}, u32[]{:S(2)}) %collective-permute-start.14) | collective-permute-done | bytes 196640 | tf_op jit(solution)/shard_map/az2/ppermute | solution.py:294
  43.6 0.7 %collective-permute-start.15 = (bf16[2,3,16,1024]{3,2,1,0:T(8,128)(2,1)S(1)}, bf16[2,3,16,1024]{3,2,1,0:T(8,128)(2,1)S(1)}, u32[]{:S(2)}, u32[]{:S(2)}) collective-permute-start(bf16[2,3,16,1024]{3,2,1,0:T(8,128)(2,1)S(1)} %collective-permute-done.14.refs_0_), channel_id=1, source_target_pairs={{0,2},{1,3},{2,0},{3,1},{4,6},{5,7},{6,4},{7,5},{8,10},{9,11},{10,... | collective-permute-start | bytes 589832 | tf_op jit(solution)/shard_map/x22/ppermute | solution.py:294
  44.3 1.8 %turn_grads.2.refs_0_ = bf16[3,1024,256]{2,1,0:T(8,128)(2,1)S(1)} custom-call(bf16[3,64,1024]{2,1,0:T(8,128)(2,1)S(1)} %copy-done, bf16[3,64,1024]{2,1,0:T(8,128)(2,1)S(1)} %collective-permute-done.3.refs_1_, bf16[3,64,1024]{2,1,0:T(8,128)(2,1)S(1)} %collective-permute-done.refs_2_, bf16[3,64,1024]{2,1,0:T(8,128)(2,1)S(1)} %collective-permute-done.4.refs_3_, ...), custom_call_target="tpu_custom_call" | custom-call | flops 10000000000 | tf_op jit(solution)/shard_map/turn_grads/pallas_call | solution.py:217
  46.1 0.0 collective-permute-done.12.refs_1_
  46.1 0.1 join.6.refs_3_
  46.2 0.1 collective-permute-start.13
  46.2 3.3 %collective-permute-done.2.first = bf16[3,64,1024]{2,1,0:T(8,128)(2,1)S(1)} collective-permute-done((bf16[3,64,1024]{2,1,0:T(8,128)(2,1)S(1)}, bf16[3,64,1024]{2,1,0:T(8,128)(2,1)S(1)}, u32[]{:S(2)}, u32[]{:S(2)}) %collective-permute-start.2) | collective-permute-done | bytes 393248 | tf_op jit(solution)/shard_map/d3/ppermute | solution.py:294
  49.5 0.1 collective-permute-start.17
  49.6 0.0 collective-permute-done.5.refs_1_
  49.7 2.1 %collective-permute-start.6 = (bf16[2,64,1024]{2,1,0:T(8,128)(2,1)S(1)}, bf16[2,64,1024]{2,1,0:T(8,128)(2,1)S(1)}, u32[]{:S(2)}, u32[]{:S(2)}) collective-permute-start(bf16[2,64,1024]{2,1,0:T(8,128)(2,1)S(1)} %slice.8), channel_id=1, source_target_pairs={{0,8},{4,0},{8,16},{12,4},{16,24},{20,12},{24,28},{28,20},{1,9},{5... | collective-permute-start | bytes 786440 | tf_op jit(solution)/shard_map/u/ppermute | solution.py:294
  51.8 0.0 collective-permute-done.15.refs_1_
  51.8 0.1 collective-permute-start.16
  51.9 1.0 %turn_grads.3.refs_1_ = bf16[3,1024,128]{2,1,0:T(8,128)(2,1)S(1)} custom-call(bf16[3,64,1024]{2,1,0:T(8,128)(2,1)S(1)} %collective-permute-done.1.refs_0_, bf16[3,64,1024]{2,1,0:T(8,128)(2,1)S(1)} %collective-permute-done.5.refs_1_, bf16[4,256,256]{2,1,0:T(8,128)(2,1)S(1)} %get-tuple-element.25.refs_4_.refs_2_.high, ...), custom_call_target="tpu_custom_call" | custom-call | flops 10000000000 | tf_op jit(solution)/shard_map/turn_grads/pallas_call | solution.py:217
  52.9 0.0 collective-permute-done.9.refs_0_
  52.9 0.7 %collective-permute-done.16.refs_4_ = bf16[4,3,16,1024]{3,2,1,0:T(8,128)(2,1)S(1)} collective-permute-done((bf16[4,3,16,1024]{3,2,1,0:T(8,128)(2,1)S(1)}, bf16[4,3,16,1024]{3,2,1,0:T(8,128)(2,1)S(1)}, u32[]{:S(2)}, u32[]{:S(2)}) %collective-permute-start.16) | collective-permute-done | bytes 393248 | tf_op jit(solution)/shard_map/x21/ppermute | solution.py:294
  53.6 0.0 collective-permute-done.13.refs_2_
  53.6 2.5 %turn_acts.1.acts = bf16[3,512,1024]{2,1,0:T(8,128)(2,1)S(1)} custom-call(s32[3]{0:T(128)S(1)} %pad_add_fusion.where_ref, bf16[4,3,16,1024]{3,2,1,0:T(8,128)(2,1)S(1)} %collective-permute-done.9.refs_0_, bf16[4,3,16,1024]{3,2,1,0:T(8,128)(2,1)S(1)} %join.4.refs_1_, bf16[8,3,16,1024]{3,2,1,0:T(8,128)(2,1)S(1)} %collective-permute-done.13.refs_2_, ...), custom_call_target="tpu_custom_call" | custom-call | flops 2000000000 | tf_op jit(solution)/shard_map/turn_acts/pallas_call | solution.py:185
  56.1 0.0 collective-permute-done.17.second
  56.1 2.1 %multiply.2.refs_2_ = f32[1024,1024]{1,0:T(8,128)S(1)} custom-call(bf16[3,64,1024]{2,1,0:T(8,128)(2,1)S(1)} %collective-permute-done.2.first, bf16[1,64,1024]{2,1,0:T(8,128)(2,1)S(1)} %collective-permute-done.17.second, bf16[4,256,256]{2,1,0:T(8,128)(2,1)S(1)} %get-tuple-element.25.refs_4_.refs_2_.high, ...), custom_call_target="tpu_custom_call" | custom-call | tf_op jit(solution)/shard_map/multiply/pallas_call | solution.py:258
  58.2 0.0 collective-permute-done.6.second
  58.3 4.6 %multiply.3 = f32[1024,1024]{1,0:T(8,128)} custom-call(bf16[3,64,1024]{2,1,0:T(8,128)(2,1)S(1)} %collective-permute-done.2.first, bf16[2,64,1024]{2,1,0:T(8,128)(2,1)S(1)} %collective-permute-done.6.second, bf16[4,256,256]{2,1,0:T(8,128)(2,1)S(1)} %get-tuple-element.25.refs_4_.refs_2_.high, bf16[4,256,256]{2,1,0:T(8,128)(2,1)S(1)} %get-tuple-element.26.refs_5_.refs_3_.low, ...), custom_call_target="tpu_custom_call" | custom-call | tf_op jit(solution)/shard_map/multiply/pallas_call | solution.py:258
  (9 shorter events, 0.1 us)
Async XLA Ops:
  0.0 28.4 %copy-start.2 = (f32[128,8,8]{0,2,1:T(8,128)S(1)}, f32[128,8,8]{0,2,1:T(8,128)}, u32[]{:S(2)}) copy-start(f32[128,8,8]{0,2,1:T(8,128)} %param.7) | copy-start | bytes 98308
  0.0 28.4 %copy-start.1 = (f32[128,8,8]{0,2,1:T(8,128)S(1)}, f32[128,8,8]{0,2,1:T(8,128)}, u32[]{:S(2)}) copy-start(f32[128,8,8]{0,2,1:T(8,128)} %param.6) | copy-start | bytes 98308
  0.0 12.8 %collective-permute-start = (bf16[3,64,1024]{2,1,0:T(8,128)(2,1)}, bf16[3,64,1024]{2,1,0:T(8,128)(2,1)S(1)}, u32[]{:S(2)}, u32[]{:S(2)}) collective-permute-start(bf16[3,64,1024]{2,1,0:T(8,128)(2,1)} %refs_0_.1), channel_id=1, source_target_pairs={{0,4},{4,12},{8,0},{12,20},{16,8},{20,28},{24,16},{28,24},{1,5},{5... | collective-permute-start | bytes 1179656 | tf_op jit(solution)/shard_map/d1/ppermute | solution.py:294
  3.0 12.2 %collective-permute-start.3 = (bf16[3,64,1024]{2,1,0:T(8,128)(2,1)}, bf16[3,64,1024]{2,1,0:T(8,128)(2,1)S(1)}, u32[]{:S(2)}, u32[]{:S(2)}) collective-permute-start(bf16[3,64,1024]{2,1,0:T(8,128)(2,1)} %refs_0_.1), channel_id=1, source_target_pairs={{0,8},{4,0},{8,16},{12,4},{16,24},{20,12},{24,28},{28,20},{1,9},{5... | collective-permute-start | bytes 1179656 | tf_op jit(solution)/shard_map/u1/ppermute | solution.py:294
  5.0 18.6 %collective-permute-start.7 = (bf16[4,3,16,1024]{3,2,1,0:T(8,128)(2,1)S(1)}, bf16[4,3,16,1024]{3,2,1,0:T(8,128)(2,1)S(1)}, u32[]{:S(2)}, u32[]{:S(2)}) collective-permute-start(bf16[4,3,16,1024]{3,2,1,0:T(8,128)(2,1)S(1)} %get-tuple-element.28), channel_id=1, source_target_pairs={{0,4},{4,0},{8,12},{12,8},{16,20},{20,16},{24,28},{28,24},{1,5},{5... | collective-permute-start | bytes 1179656 | tf_op jit(solution)/shard_map/ay/ppermute | solution.py:294
  12.8 15.6 %collective-permute-start.1 = (bf16[3,64,1024]{2,1,0:T(8,128)(2,1)S(1)}, bf16[3,64,1024]{2,1,0:T(8,128)(2,1)S(1)}, u32[]{:S(2)}, u32[]{:S(2)}) collective-permute-start(bf16[3,64,1024]{2,1,0:T(8,128)(2,1)S(1)} %collective-permute-done.refs_2_), channel_id=1, source_target_pairs={{0,4},{4,12},{8,0},{12,20},{16,8},{20,28},{24,16},{28,24},{1,5},{5... | collective-permute-start | bytes 1179656 | tf_op jit(solution)/shard_map/d2/ppermute | solution.py:294
  15.2 24.2 %collective-permute-start.4 = (bf16[3,64,1024]{2,1,0:T(8,128)(2,1)S(1)}, bf16[3,64,1024]{2,1,0:T(8,128)(2,1)S(1)}, u32[]{:S(2)}, u32[]{:S(2)}) collective-permute-start(bf16[3,64,1024]{2,1,0:T(8,128)(2,1)S(1)} %collective-permute-done.3.refs_1_), channel_id=1, source_target_pairs={{0,8},{4,0},{8,16},{12,4},{16,24},{20,12},{24,28},{28,20},{1,9},{5... | collective-permute-start | bytes 1179656 | tf_op jit(solution)/shard_map/u2/ppermute | solution.py:294
  23.7 6.5 %collective-permute-start.8 = (bf16[2,3,16,1024]{3,2,1,0:T(8,128)(2,1)S(1)}, bf16[2,3,16,1024]{3,2,1,0:T(8,128)(2,1)S(1)}, u32[]{:S(2)}, u32[]{:S(2)}) collective-permute-start(bf16[2,3,16,1024]{3,2,1,0:T(8,128)(2,1)S(1)} %get-tuple-element.29.refs_0_), channel_id=1, source_target_pairs={{0,2},{1,3},{2,0},{3,1},{4,6},{5,7},{6,4},{7,5},{8,10},{9,11},{10,... | collective-permute-start | bytes 589832 | tf_op jit(solution)/shard_map/x02/ppermute | solution.py:294
  25.3 9.9 %collective-permute-start.11 = (bf16[2,3,16,1024]{3,2,1,0:T(8,128)(2,1)S(1)}, bf16[2,3,16,1024]{3,2,1,0:T(8,128)(2,1)S(1)}, u32[]{:S(2)}, u32[]{:S(2)}) collective-permute-start(bf16[2,3,16,1024]{3,2,1,0:T(8,128)(2,1)S(1)} %get-tuple-element.34), channel_id=1, source_target_pairs={{0,24},{4,28},{8,0},{12,4},{16,8},{20,12},{24,16},{28,20},{1,25},{... | collective-permute-start | bytes 589832 | tf_op jit(solution)/shard_map/az3/ppermute | solution.py:294
  27.3 9.9 %collective-permute-start.10 = (bf16[2,3,16,1024]{3,2,1,0:T(8,128)(2,1)S(1)}, bf16[2,3,16,1024]{3,2,1,0:T(8,128)(2,1)S(1)}, u32[]{:S(2)}, u32[]{:S(2)}) collective-permute-start(bf16[2,3,16,1024]{3,2,1,0:T(8,128)(2,1)S(1)} %get-tuple-element.32), channel_id=1, source_target_pairs={{0,8},{4,12},{8,16},{12,20},{16,24},{20,28},{24,0},{28,4},{1,9},{5... | collective-permute-start | bytes 589832 | tf_op jit(solution)/shard_map/az1/ppermute | solution.py:294
  28.4 15.2 %collective-permute-start.14 = (bf16[2,3,16,1024]{3,2,1,0:T(8,128)(2,1)S(1)}, bf16[2,3,16,1024]{3,2,1,0:T(8,128)(2,1)S(1)}, u32[]{:S(2)}, u32[]{:S(2)}) collective-permute-start(bf16[2,3,16,1024]{3,2,1,0:T(8,128)(2,1)S(1)} %get-tuple-element.37), channel_id=1, source_target_pairs={{0,16},{4,20},{8,24},{12,28},{16,0},{20,4},{24,8},{28,12},{1,17},{... | collective-permute-start | bytes 589832 | tf_op jit(solution)/shard_map/az2/ppermute | solution.py:294
  28.4 15.9 %copy-start = (bf16[3,64,1024]{2,1,0:T(8,128)(2,1)S(1)}, bf16[3,64,1024]{2,1,0:T(8,128)(2,1)}, u32[]{:S(2)}) copy-start(bf16[3,64,1024]{2,1,0:T(8,128)(2,1)} %refs_0_.1) | copy-start | bytes 1179652
  30.3 22.6 %collective-permute-start.9 = (bf16[4,3,16,1024]{3,2,1,0:T(8,128)(2,1)S(1)}, bf16[4,3,16,1024]{3,2,1,0:T(8,128)(2,1)S(1)}, u32[]{:S(2)}, u32[]{:S(2)}) collective-permute-start(bf16[4,3,16,1024]{3,2,1,0:T(8,128)(2,1)S(1)} %join.4.refs_1_), channel_id=1, source_target_pairs={{0,1},{1,0},{2,3},{3,2},{4,5},{5,4},{6,7},{7,6},{8,9},{9,8},{10,11... | collective-permute-start | bytes 1179656 | tf_op jit(solution)/shard_map/x01/ppermute | solution.py:294
  37.2 8.9 %collective-permute-start.12 = (bf16[4,3,16,1024]{3,2,1,0:T(8,128)(2,1)S(1)}, bf16[4,3,16,1024]{3,2,1,0:T(8,128)(2,1)S(1)}, u32[]{:S(2)}, u32[]{:S(2)}) collective-permute-start(bf16[4,3,16,1024]{3,2,1,0:T(8,128)(2,1)S(1)} %join.5.refs_0_), channel_id=1, source_target_pairs={{0,2},{1,3},{2,0},{3,1},{4,6},{5,7},{6,4},{7,5},{8,10},{9,11},{10,... | collective-permute-start | bytes 1179656 | tf_op jit(solution)/shard_map/x12/ppermute | solution.py:294
  37.3 12.3 %collective-permute-start.2 = (bf16[3,64,1024]{2,1,0:T(8,128)(2,1)S(1)}, bf16[3,64,1024]{2,1,0:T(8,128)(2,1)S(1)}, u32[]{:S(2)}, u32[]{:S(2)}) collective-permute-start(bf16[3,64,1024]{2,1,0:T(8,128)(2,1)S(1)} %collective-permute-done.1.refs_0_), channel_id=1, source_target_pairs={{0,4},{4,12},{8,0},{12,20},{16,8},{20,28},{24,16},{28,24},{1,5},{5... | collective-permute-start | bytes 1179656 | tf_op jit(solution)/shard_map/d3/ppermute | solution.py:294
  39.5 10.1 %collective-permute-start.5 = (bf16[3,64,1024]{2,1,0:T(8,128)(2,1)S(1)}, bf16[3,64,1024]{2,1,0:T(8,128)(2,1)S(1)}, u32[]{:S(2)}, u32[]{:S(2)}) collective-permute-start(bf16[3,64,1024]{2,1,0:T(8,128)(2,1)S(1)} %collective-permute-done.4.refs_3_), channel_id=1, source_target_pairs={{0,8},{4,0},{8,16},{12,4},{16,24},{20,12},{24,28},{28,20},{1,9},{5... | collective-permute-start | bytes 1179656 | tf_op jit(solution)/shard_map/u3/ppermute | solution.py:294
  43.6 8.1 %collective-permute-start.15 = (bf16[2,3,16,1024]{3,2,1,0:T(8,128)(2,1)S(1)}, bf16[2,3,16,1024]{3,2,1,0:T(8,128)(2,1)S(1)}, u32[]{:S(2)}, u32[]{:S(2)}) collective-permute-start(bf16[2,3,16,1024]{3,2,1,0:T(8,128)(2,1)S(1)} %collective-permute-done.14.refs_0_), channel_id=1, source_target_pairs={{0,2},{1,3},{2,0},{3,1},{4,6},{5,7},{6,4},{7,5},{8,10},{9,11},{10,... | collective-permute-start | bytes 589832 | tf_op jit(solution)/shard_map/x22/ppermute | solution.py:294
  46.2 7.4 %collective-permute-start.13 = (bf16[8,3,16,1024]{3,2,1,0:T(8,128)(2,1)S(1)}, bf16[8,3,16,1024]{3,2,1,0:T(8,128)(2,1)S(1)}, u32[]{:S(2)}, u32[]{:S(2)}) collective-permute-start(bf16[8,3,16,1024]{3,2,1,0:T(8,128)(2,1)S(1)} %join.6.refs_3_), channel_id=1, source_target_pairs={{0,1},{1,0},{2,3},{3,2},{4,5},{5,4},{6,7},{7,6},{8,9},{9,8},{10,11... | collective-permute-start | bytes 2359304 | tf_op jit(solution)/shard_map/x11/ppermute | solution.py:294
  49.5 6.6 %collective-permute-start.17 = (bf16[1,64,1024]{2,1,0:T(8,128)(2,1)S(1)}, bf16[1,64,1024]{2,1,0:T(8,128)(2,1)S(1)}, u32[]{:S(2)}, u32[]{:S(2)}) collective-permute-start(bf16[1,64,1024]{2,1,0:T(8,128)(2,1)S(1)} %slice.9), channel_id=1, source_target_pairs={{0,4},{4,12},{8,0},{12,20},{16,8},{20,28},{24,16},{28,24},{1,5},{5... | collective-permute-start | bytes 393224 | tf_op jit(solution)/shard_map/d/ppermute | solution.py:294
  49.7 8.6 %collective-permute-start.6 = (bf16[2,64,1024]{2,1,0:T(8,128)(2,1)S(1)}, bf16[2,64,1024]{2,1,0:T(8,128)(2,1)S(1)}, u32[]{:S(2)}, u32[]{:S(2)}) collective-permute-start(bf16[2,64,1024]{2,1,0:T(8,128)(2,1)S(1)} %slice.8), channel_id=1, source_target_pairs={{0,8},{4,0},{8,16},{12,4},{16,24},{20,12},{24,28},{28,20},{1,9},{5... | collective-permute-start | bytes 786440 | tf_op jit(solution)/shard_map/u/ppermute | solution.py:294
  51.8 1.8 %collective-permute-start.16 = (bf16[4,3,16,1024]{3,2,1,0:T(8,128)(2,1)S(1)}, bf16[4,3,16,1024]{3,2,1,0:T(8,128)(2,1)S(1)}, u32[]{:S(2)}, u32[]{:S(2)}) collective-permute-start(bf16[4,3,16,1024]{3,2,1,0:T(8,128)(2,1)S(1)} %join.7.refs_5_), channel_id=1, source_target_pairs={{0,1},{1,0},{2,3},{3,2},{4,5},{5,4},{6,7},{7,6},{8,9},{9,8},{10,11... | collective-permute-start | bytes 1179656 | tf_op jit(solution)/shard_map/x21/ppermute | solution.py:294
